TPU v7x, 128 devices: a whole 4x4x4 slice. The times are simulated.
128 devices in a mesh: lat: 16 (over z, x), lon: 8 (over y, core).
Axes of the slice: x: 4, y: 4, z: 4, core: 2. Of those that a mesh axis runs over, the one named last changes fastest.
Arguments:
- adjoint_grid: float32 [1280, 8, 3072], P('lat', None, 'lon'), may hold values from -6 to 6
- tile_owner: int32 [16, 8, 240, 1], P('lat', 'lon'), may hold values from 0 to 127, as said below
- tile_slot: int32 [16, 8, 240, 1], P('lat', 'lon'), may hold values from 0 to 239
- stencil: int32 [1280, 24, 4, 128], P('lat', 'lon'), may hold values from 0 to 127
- interp_weight: float32 [1280, 24, 4, 128], P('lat', 'lon'), may hold values from 0 to 0.5
- vertical_offset: float32 [1280, 4, 2, 2], P('lat'), may hold values from -0.6 to 0.6
- diffusion_rate: float32 [8], replicated, may hold values from 1 to 1000
Outputs:
- adjoint_out: float32 [1280, 8, 3072], P('lat', None, 'lon')
Inputs may be any that keep to these rules, and one draw needn't show every extreme that they name: `tile_owner`: A device is named as its latitude band times the number of longitude bands plus its longitude band. A tile of band pair (a, b) names a band pair (a + da, (b + db) mod the number of longitude bands) with da and db in -1, 0, 1 and a + da a valid latitude band: its own pair or one of its neighbours, longitude wrapping around. Among the 240 tiles of one band pair, no band pair is named more than 80 times, and every band pair names some band pair exactly 80 times.
All inputs are finite; a program needn't handle non-finite values.
Results may differ from a plain program's by a relative error of at most 0.00055.
Values sent between devices are 32-bit elements; how exact they have to be, the bound alone decides.
No kernel may reach another device: no remote copies, remote signals or barrier semaphores. Data moves between devices by JAX's collectives and lax.ppermute only.
A program may use at most 256 MiB of HBM per device.

v0:
```python
import math

import jax
import jax.numpy as jnp
from jax import lax
from jax.sharding import PartitionSpec as P

NM = 640


highest = lax.Precision.HIGHEST
gamma_shift = 0.5 * math.log(math.pi)
log_floor = -60.0


def extended(cells, sides, width):
    for axis, dim in sides:
        count = lax.axis_size(axis)
        head = lax.slice_in_dim(cells, 0, width, axis=dim)
        tail = lax.slice_in_dim(cells, cells.shape[dim] - width, cells.shape[dim], axis=dim)
        cells = jnp.concatenate(
            [
                lax.ppermute(tail, axis, [(i, (i + 1) % count) for i in range(count)]),
                cells,
                lax.ppermute(head, axis, [((i + 1) % count, i) for i in range(count)]),
            ],
            axis=dim,
        )
    return cells


def fourier_table(point_count, wave_total, block_count):
    per_block = wave_total // block_count
    column = jnp.arange(2 * wave_total, dtype=jnp.int32)
    wave_ids = column // (2 * per_block) * per_block + column % per_block
    part_ids = column // per_block % 2
    points = jnp.arange(point_count, dtype=jnp.int32)
    phase_ids = points[:, None] * wave_ids[None, :] % point_count
    angles = phase_ids.astype(jnp.float32) * (2.0 * math.pi / point_count)
    return jnp.where(part_ids[None, :] == 0, jnp.cos(angles), -jnp.sin(angles))


def latitude_rows(lat_total, row_count):
    rows_f = jnp.arange(row_count, dtype=jnp.int32).astype(jnp.float32)
    latitude = 0.5 * math.pi - math.pi * (rows_f + 0.5) / lat_total
    return (jnp.sin(latitude), jnp.cos(latitude))


def legendre_diagonal(order_f, cos_lat):
    log_norm = 0.5 * (lax.lgamma(order_f + 1.5) - lax.lgamma(order_f + 1.0) - gamma_shift)
    exponent = log_norm + order_f * jnp.log(cos_lat)[None, :]
    kept = exponent >= log_floor
    return jnp.where(kept, jnp.exp(jnp.where(kept, exponent, 0.0)), 0.0)


def legendre_scan(recurrence, first_degree, degree_count, wave_ids, order_f, sine_lat, diagonal):

    def advance(carried, degree):
        previous, earlier, scale_prev = carried
        degree_f = degree.astype(jnp.float32)
        scale_now = jnp.sqrt(
            jnp.maximum(4.0 * degree_f * degree_f - 1.0, 1.0)
            / jnp.maximum(degree_f * degree_f - order_f * order_f, 1.0)
        )
        stepped = scale_now * (sine_lat[None, :] * previous - earlier / scale_prev)
        current = jnp.where(
            degree < wave_ids[:, None],
            0.0,
            jnp.where(degree == wave_ids[:, None], diagonal, stepped),
        )
        return ((current, previous, scale_now), current)

    degrees = first_degree + jnp.arange(degree_count, dtype=jnp.int32)
    return lax.scan(advance, recurrence, degrees, unroll=8)


def damping(local_rates, degrees):
    degree_f = degrees.astype(jnp.float32)
    ratio = local_rates[:, None] * (degree_f * (degree_f + 1.0) / float(NM * (NM + 1)))[None, :]
    return -ratio / (1.0 + ratio)


def spread_tiles(field, stencil, interp_weight):
    row_count, fields_levels, lon_width = field.shape
    tiles_row, stencil_count, tile_width = (stencil.shape[1], stencil.shape[2], stencil.shape[3])
    tiled = field.reshape(row_count, fields_levels, tiles_row, tile_width)
    targets = jnp.arange(tile_width, dtype=jnp.int32)
    spread_map = jnp.zeros((row_count, tiles_row, tile_width, tile_width), jnp.float32)
    for stencil_id in range(stencil_count):
        spread_map = spread_map + jnp.where(
            stencil[:, :, stencil_id, :, None] == targets,
            interp_weight[:, :, stencil_id, :, None],
            0.0,
        )
    return jnp.einsum("rfkp,rkpq->rkfq", tiled, spread_map, precision=highest)


def vertical_mix(field, offset):
    row_count, fields_levels, lon_width = field.shape
    layered = field.reshape(row_count, offset.shape[1], offset.shape[2], lon_width)
    mixed = layered + jnp.einsum("rilk,rilx->rikx", offset, layered, precision=highest)
    return mixed.reshape(row_count, fields_levels, lon_width)


def spectral_local(spectral_side, wave_ids, local_rates, lat_total):
    half_rows = lat_total // 2
    sine_lat, cos_lat = latitude_rows(lat_total, half_rows)
    lat_weight = math.pi / lat_total * cos_lat
    northern = spectral_side[:half_rows]
    southern = jnp.flip(spectral_side[half_rows:], 0)
    row_scale = lat_weight[:, None, None, None]
    folded = jnp.stack(
        [(northern + southern) * row_scale, (northern - southern) * row_scale], axis=1
    )
    order_f = wave_ids.astype(jnp.float32)[:, None]
    diagonal = legendre_diagonal(order_f, cos_lat)
    wave_count = wave_ids.shape[0]
    recurrence = (
        jnp.zeros((wave_count, half_rows), jnp.float32),
        jnp.zeros((wave_count, half_rows), jnp.float32),
        jnp.ones((wave_count, 1), jnp.float32),
    )
    block_size = math.gcd(NM, 128)
    summed = jnp.zeros((half_rows, 2) + spectral_side.shape[1:], jnp.float32)
    for first_degree in range(0, NM, block_size):
        recurrence, legendre = legendre_scan(
            recurrence, first_degree, block_size, wave_ids, order_f, sine_lat, diagonal
        )
        degrees = first_degree + jnp.arange(block_size, dtype=jnp.int32)
        paired = jnp.einsum("nml,lsfcm->sfcmn", legendre, folded, precision=highest)
        parity = (degrees[None, :] - wave_ids[:, None]) % 2 == 0
        spectrum = jnp.where(parity, paired[0], paired[1])
        damped = spectrum * damping(local_rates, degrees)[:, None, None, :]
        signed = jnp.stack([damped, jnp.where(parity, damped, -damped)], axis=0)
        summed = summed + jnp.einsum("nml,sfcmn->lsfcm", legendre, signed, precision=highest)
    return jnp.concatenate([summed[:, 0], jnp.flip(summed[:, 1], 0)], axis=0)


def local(
    adjoint_grid, tile_owner, tile_slot, stencil, interp_weight, vertical_offset, diffusion_rate
):
    row_count, fields_levels, lon_width = adjoint_grid.shape
    tiles_row, tile_width = (stencil.shape[1], stencil.shape[3])
    tile_count = row_count * tiles_row
    lat_count = lax.axis_size("lat")
    lon_count = lax.axis_size("lon")
    capacity = max(2, (tile_count + 2) // 3)
    lat_here = lax.axis_index("lat")
    lon_here = lax.axis_index("lon")
    spread = spread_tiles(adjoint_grid, stencil, interp_weight).reshape(
        tile_count, fields_levels, tile_width
    )
    owners = tile_owner.reshape(tile_count)
    slot_ids = tile_slot.reshape(tile_count)
    lat_step = owners // lon_count - lat_here
    lon_step = (owners % lon_count - lon_here + 1 + lon_count) % lon_count - 1
    classes = (lat_step + 1) * 3 + (lon_step + 1)
    marked = (classes[:, None] == jnp.arange(9, dtype=jnp.int32)[None, :]).astype(jnp.int32)
    order_in = jnp.sum(jnp.cumsum(marked, axis=0) * marked, axis=1) - 1
    position = classes * capacity + order_in
    source = (
        jnp.full((9 * capacity,), tile_count, jnp.int32)
        .at[position]
        .set(jnp.arange(tile_count, dtype=jnp.int32))
    )
    slot_rows = jnp.broadcast_to(
        slot_ids.astype(jnp.float32)[:, None, None], (tile_count, 1, tile_width)
    )
    labelled = jnp.concatenate([spread, slot_rows], axis=1)
    empty_row = jnp.concatenate(
        [
            jnp.zeros((1, fields_levels, tile_width), jnp.float32),
            jnp.full((1, 1, tile_width), float(tile_count), jnp.float32),
        ],
        axis=1,
    )
    padded = jnp.concatenate([labelled, empty_row], axis=0)
    outgoing = padded[source].reshape(3, 3, capacity, fields_levels + 1, tile_width)
    widened = extended(outgoing, (("lat", 0), ("lon", 1)), 1)
    arrived = widened[::-2, ::-2]
    arrived = arrived.reshape(9 * capacity, fields_levels + 1, tile_width)
    targets = arrived[:, fields_levels, 0].astype(jnp.int32)
    departed = jax.ops.segment_sum(
        arrived[:, :fields_levels], targets, num_segments=tile_count + 1
    )[:tile_count]
    departed = (
        departed.reshape(row_count, tiles_row, fields_levels, tile_width)
        .transpose(0, 2, 1, 3)
        .reshape(row_count, fields_levels, lon_width)
    )
    diffused = vertical_mix(departed, vertical_offset)
    full_width = lon_width * lon_count
    field_share = fields_levels // lon_count
    wave_share = NM // lat_count
    fourier = fourier_table(full_width, NM, lat_count)
    coefficients = (
        jnp.einsum(
            "rfx,xc->rfc",
            lax.all_to_all(diffused, "lon", split_axis=1, concat_axis=2, tiled=True),
            fourier,
            precision=highest,
        )
        / full_width
    )
    spectral_side = lax.all_to_all(coefficients, "lat", split_axis=2, concat_axis=0, tiled=True)
    lat_total = spectral_side.shape[0]
    spectral_side = spectral_side.reshape(lat_total, field_share, 2, wave_share)
    wave_ids = lat_here * wave_share + jnp.arange(wave_share, dtype=jnp.int32)
    local_rates = lax.dynamic_slice_in_dim(diffusion_rate, lon_here * field_share, field_share)
    synthesis = spectral_local(spectral_side, wave_ids, local_rates, lat_total)
    factor = jnp.where(wave_ids == 0, 1.0, 2.0)
    synthesis = (synthesis * factor[None, None, None, :]).reshape(
        lat_total, field_share, 2 * wave_share
    )
    returned = lax.all_to_all(synthesis, "lat", split_axis=0, concat_axis=2, tiled=True)
    grid_part = jnp.einsum("rfc,xc->rfx", returned, fourier, precision=highest)
    regridded = lax.all_to_all(grid_part, "lon", split_axis=2, concat_axis=1, tiled=True)
    return diffused + regridded


def solution(mesh):
    in_specs = (
        P("lat", None, "lon"),
        P("lat", "lon", None, None),
        P("lat", "lon", None, None),
        P("lat", "lon", None, None),
        P("lat", "lon", None, None),
        P("lat", None, None, None),
        P(),
    )
    out_specs = P("lat", None, "lon")
    return jax.shard_map(local, mesh=mesh, in_specs=in_specs, out_specs=out_specs, check_vma=False)
```

profile of v0, /device:TPU:1, one launch (start us, length us, event | category | flops | bytes accessed | tf_op | source)
XLA Modules:
  0.0 1651.1 jit_solution(12239158918443588646)
XLA Ops:
  10.0 86.2 %fusion.212 = f32[80,3,128,8]{2,3,1,0:T(8,128)S(1)} fusion(f32[80,3,128]{2,1,0:T(4,128)S(1)} %copy.177, s32[80,3,128]{2,1,0:T(4,128)S(1)} %copy.175, f32[80,3,128]{2,1,0:T(4,128)S(1)} %copy.173, s32[80,3,128]{2,1,0:T(4,128)S(1)} %copy.171, f32[80,3,128]{2,1,0:T(4,128)S(1)} %copy.169, s32[80,3,128]{2,1,0:T(4,128)S(1)} %copy.167, ...), kind=kOutput, calls=%fused_computation.315 | convolution fusion | flops 420741120 | bytes 2949120 | tf_op jit(solution)/shard_map/rfkp,rkpq->rkfq/dot_general | solution.py:95
  119.5 209.8 %while.115 = (s32[]{:T(128)}, f32[40,640]{1,0:T(8,128)S(1)}, f32[40,640]{1,0:T(8,128)S(1)}, f32[40,1]{0,1:T(1,128)S(1)}, f32[16,8,40,640]{3,2,1,0:T(8,128)}, /*i...) while((s32[]{:T(128)}, f32[40,640]{1,0:T(8,128)S(1)}, ...), condition=%wide.region_6.7_spmd.clone.clone.clone.clone, body=%wide.region_5.6_spmd.clone.clone.clone.clone.sunk | while | flops 2335010 | bytes 5006349 | solution.py:74
  335.5 208.6 %while.111 = (s32[]{:T(128)}, f32[40,640]{1,0:T(8,128)S(1)}, f32[40,640]{1,0:T(8,128)S(1)}, f32[40,1]{0,1:T(1,128)S(1)}, f32[16,8,40,640]{3,2,1,0:T(8,128)}, /*i...) while((s32[]{:T(128)}, f32[40,640]{1,0:T(8,128)S(1)}, ...), condition=%wide.region_8.9_spmd.clone.clone.clone, body=%wide.region_7.8_spmd.clone.clone.clone.sunk | while | flops 2258169 | bytes 5006009 | solution.py:74
  550.1 203.2 %while.112 = (s32[]{:T(128)}, f32[40,640]{1,0:T(8,128)S(1)}, f32[40,640]{1,0:T(8,128)S(1)}, f32[40,1]{0,1:T(1,128)S(1)}, f32[16,8,40,640]{3,2,1,0:T(8,128)}, /*i...) while((s32[]{:T(128)}, f32[40,640]{1,0:T(8,128)S(1)}, ...), condition=%wide.region_10.11_spmd.clone.clone.clone, body=%wide.region_9.10_spmd.clone.clone.clone.sunk | while | flops 2258169 | bytes 5006009 | solution.py:74
  771.8 211.7 %while.113 = (s32[]{:T(128)}, f32[40,640]{1,0:T(8,128)S(1)}, f32[40,640]{1,0:T(8,128)S(1)}, f32[40,1]{0,1:T(1,128)S(1)}, f32[16,8,40,640]{3,2,1,0:T(8,128)}, /*i...) while((s32[]{:T(128)}, f32[40,640]{1,0:T(8,128)S(1)}, ...), condition=%wide.region_12.13_spmd.clone.clone.clone, body=%wide.region_11.12_spmd.clone.clone.clone.sunk | while | flops 2258169 | bytes 5006009 | solution.py:74
  1000.0 53.4 %scatter_fusion = f32[241,8,128]{2,1,0:T(8,128)S(1)} fusion(f32[241,8,128]{2,1,0:T(8,128)S(1)} %broadcast_in_dim.1444, s32[720]{0:T(1024)S(1)} %convert_reduce_fusion, f32[720,8,128]{2,1,0:T(8,128)} %copy.266), kind=kCustom, calls=%fused_computation.2 | custom fusion | flops 737280 | bytes 8850240 | tf_op jit(solution)/shard_map/scatter-add | solution.py:183
  1054.7 6.5 fusion.264
  1064.2 6.2 all-to-all-start
  1076.4 209.3 %while.114 = (s32[]{:T(128)}, f32[40,640]{1,0:T(8,128)S(1)}, f32[40,640]{1,0:T(8,128)S(1)}, f32[40,1]{0,1:T(1,128)S(1)}, f32[16,8,40,640]{3,2,1,0:T(8,128)}, /*i...) while((s32[]{:T(128)}, f32[40,640]{1,0:T(8,128)S(1)}, ...), condition=%wide.region_14.15_spmd.clone.clone.clone, body=%wide.region_13.14_spmd.clone.clone.clone.sunk | while | flops 2258169 | bytes 5006009 | solution.py:74
  1288.2 76.9 %fusion.263 = f32[80,1,1280]{2,0,1:T(8,128)S(1)} fusion(f32[80,3072]{1,0:T(8,128)S(1)} %bitcast.647, s32[1280]{0:T(1024)S(1)} %fusion.332, pred[1280]{0:T(1024)(128)(4,1)S(1)} %fusion.334), kind=kOutput, calls=%fused_computation.371 | convolution fusion | flops 3818229760 | bytes 1399040 | tf_op jit(solution)/shard_map/rfx,xc->rfc/dot_general | solution.py:197
  1370.3 12.3 all-to-all-done.1
  1384.4 21.7 %fusion.265 = f32[2,1,2,40,128]{4,2,0,3,1:T(2,128)S(1)} fusion(f32[128,40,640,1]{2,1,0,3:T(8,128)} %bitcast.611, f32[640,1,1,2,40]{0,3,1,4,2:T(2,128)S(1)} %get-tuple-element.1834, f32[640,1,1,2,40]{0,3,1,4,2:T(2,128)S(1)} %get-tuple-element.1833), kind=kOutput, calls=%fused_computation.378 | convolution fusion | flops 157388800 | bytes 13598720 | tf_op jit(solution)/shard_map/nml,lsfcm->sfcmn/dot_general | solution.py:130
  1406.1 22.1 %fusion.268 = f32[2,1,2,40,128]{4,2,0,3,1:T(2,128)S(1)} fusion(f32[128,40,640,1]{2,1,0,3:T(8,128)} %bitcast.619, f32[640,1,1,2,40]{0,3,1,4,2:T(2,128)S(1)} %get-tuple-element.1834, f32[640,1,1,2,40]{0,3,1,4,2:T(2,128)S(1)} %get-tuple-element.1833), kind=kOutput, calls=%fused_computation.379 | convolution fusion | flops 157388800 | bytes 13598720 | tf_op jit(solution)/shard_map/nml,lsfcm->sfcmn/dot_general | solution.py:130
  1428.4 14.0 fusion.271
  1442.5 14.2 fusion.274
  1456.8 14.4 fusion.277
  1471.3 9.1 fusion.233
  1480.5 17.7 %fusion.229 = f32[40,2,2,640]{3,2,1,0:T(2,128)S(1)} fusion(f32[128,40,640,1]{2,1,0,3:T(8,128)} %bitcast.623, f32[1,1,2,40,128]{4,2,0,3,1:T(2,128)S(1)} %get-tuple-element.1661, f32[1,1,2,40,128]{4,2,0,3,1:T(2,128)S(1)} %get-tuple-element.1662), kind=kOutput, calls=%fused_computation.336 | convolution fusion | flops 157306880 | bytes 13598720 | tf_op jit(solution)/shard_map/nml,sfcmn->lsfcm/dot_general | solution.py:135
  1498.4 9.0 fusion.225
  1507.4 9.1 fusion.221
  1516.7 9.1 fusion.292
  1527.3 15.0 all_to_all.51
  1542.8 76.1 %fusion.241 = f32[80,3072]{0,1:T(8,128)S(1)} fusion(f32[80,1280]{1,0:T(8,128)S(1)} %reshape.2232, s32[1280]{0:T(1024)S(1)} %fusion.332, pred[1280]{0:T(1024)(128)(4,1)S(1)} %fusion.334), kind=kOutput, calls=%fused_computation.349 | convolution fusion | flops 3818127360 | bytes 1399040 | tf_op jit(solution)/shard_map/rfc,xc->rfx/dot_general | solution.py:216
  1618.9 26.9 %all_to_all.52 = f32[80,1,3072]{0,1,2:T(1,128)} all-to-all(f32[80,1,3072]{0,1,2:T(1,128)S(1)} %bitcast.645), channel_id=1, replica_groups=mesh['lat'=16,'lon'=8] {'lon'}, dimensions={2} | all-to-all | bytes 1966080 | tf_op jit(solution)/shard_map/all_to_all | solution.py:217
  (2267 shorter events, 734.9 us)
Async XLA Ops:
  10.0 86.2 %copy-start.2 = (f32[1,9,128]{2,1,0:T(8,128)S(1)}, f32[1,9,128]{2,1,0:T(8,128)}, u32[]{:S(2)}) copy-start(f32[1,9,128]{2,1,0:T(8,128)} %constant.437.clone.1) | copy-start | bytes 13828
  105.1 653.7 %collective-permute-start = (f32[1,3,80,9,128]{4,2,3,1,0:T(8,128)}, f32[1,3,80,9,128]{4,2,3,1,0:T(8,128)S(1)}, u32[]{:S(2)}, u32[]{:S(2)}) collective-permute-start(f32[1,3,80,9,128]{4,2,3,1,0:T(8,128)} %copy.181), channel_id=1, source_target_pairs={{0,8},{8,16},{16,24},{24,32},{32,40},{40,48},{48,56},{56,64},{64,7... | collective-permute-start | bytes 3317768 | tf_op jit(solution)/shard_map/ppermute | solution.py:23
  108.5 650.3 %collective-permute-start.1 = (f32[1,3,80,9,128]{4,2,3,1,0:T(8,128)}, f32[1,3,80,9,128]{4,2,3,1,0:T(8,128)}, u32[]{:S(2)}, u32[]{:S(2)}) collective-permute-start(f32[1,3,80,9,128]{4,2,3,1,0:T(8,128)} %copy.184), channel_id=1, source_target_pairs={{8,0},{16,8},{24,16},{32,24},{40,32},{48,40},{56,48},{64,56},{72,6... | collective-permute-start | bytes 3317768 | tf_op jit(solution)/shard_map/ppermute | solution.py:25
  762.3 222.1 %collective-permute-start.2 = (f32[5,1,80,9,128]{4,2,3,1,0:T(8,128)}, f32[5,1,80,9,128]{4,2,3,1,0:T(8,128)}, u32[]{:S(2)}, u32[]{:S(2)}) collective-permute-start(f32[5,1,80,9,128]{4,2,3,1,0:T(8,128)} %copy.187), channel_id=1, source_target_pairs={{0,1},{1,2},{2,3},{3,4},{4,5},{5,6},{6,7},{7,0},{8,9},{9,10},{10,1... | collective-permute-start | bytes 5529608 | tf_op jit(solution)/shard_map/ppermute | solution.py:23
  765.8 218.6 %collective-permute-start.3 = (f32[5,1,80,9,128]{4,2,3,1,0:T(8,128)}, f32[5,1,80,9,128]{4,2,3,1,0:T(8,128)}, u32[]{:S(2)}, u32[]{:S(2)}) collective-permute-start(f32[5,1,80,9,128]{4,2,3,1,0:T(8,128)} %copy.188), channel_id=1, source_target_pairs={{1,0},{2,1},{3,2},{4,3},{5,4},{6,5},{7,6},{0,7},{9,8},{10,9},{11,1... | collective-permute-start | bytes 5529608 | tf_op jit(solution)/shard_map/ppermute | solution.py:25
  771.8 211.7 %copy-start.3 = (f32[80,4,2,2]{0,3,2,1:T(2,128)S(1)}, f32[80,4,2,2]{0,3,2,1:T(2,128)}, u32[]{:S(2)}) copy-start(f32[80,4,2,2]{0,3,2,1:T(2,128)} %param.22) | copy-start | bytes 15364
  1064.2 222.7 %all-to-all-start = ((f32[80,8,384]{2,0,1:T(8,128)}), f32[80,8,384]{2,0,1:T(8,128)}, u32[]{:S(2)}, u32[]{:S(2)}) async-start(f32[80,8,384]{2,0,1:T(8,128)} %copy.197), calls=%async_computation | async-start | bytes 1966080 | tf_op jit(solution)/shard_map/all_to_all | solution.py:199
  1076.4 209.3 %copy-start.4 = (f32[8]{0:T(128)S(1)}, f32[8]{0:T(128)}, u32[]{:S(2)}) copy-start(f32[8]{0:T(128)} %param.23) | copy-start | bytes 100
  1366.2 16.3 all-to-all-start.1
  1384.3 44.0 %slice-start.12 = ((s8[13107200]{0:T(1024)(128)(4,1)}), s8[4194304]{0:T(1024)(128)(4,1)S(1)}, s32[]{:S(2)}) async-start(s8[13107200]{0:T(1024)(128)(4,1)} %bitcast.624), calls=%async_computation.16 | async-start | bytes 8388608
  1384.3 44.0 %slice-start.13 = ((s8[13107200]{0:T(1024)(128)(4,1)}), s8[4194304]{0:T(1024)(128)(4,1)S(1)}, s32[]{:S(2)}) async-start(s8[13107200]{0:T(1024)(128)(4,1)} %bitcast.624), calls=%async_computation.17 | async-start | bytes 8388608
  1384.3 58.1 %slice-start.16 = ((s8[13107200]{0:T(1024)(128)(4,1)}), s8[4194304]{0:T(1024)(128)(4,1)S(1)}, s32[]{:S(2)}) async-start(s8[13107200]{0:T(1024)(128)(4,1)} %bitcast.627), calls=%async_computation.20 | async-start | bytes 8388608
  1384.3 58.1 %slice-start.17 = ((s8[13107200]{0:T(1024)(128)(4,1)}), s8[4194304]{0:T(1024)(128)(4,1)S(1)}, s32[]{:S(2)}) async-start(s8[13107200]{0:T(1024)(128)(4,1)} %bitcast.627), calls=%async_computation.21 | async-start | bytes 8388608
  1406.1 22.2 %slice-start.14 = ((s8[13107200]{0:T(1024)(128)(4,1)}), s8[4194304]{0:T(1024)(128)(4,1)S(1)}, s32[]{:S(2)}) async-start(s8[13107200]{0:T(1024)(128)(4,1)} %bitcast.624), calls=%async_computation.18 | async-start | bytes 8388608
  1406.1 22.2 %slice-start.15 = ((s8[13107200]{0:T(1024)(128)(4,1)}), s8[524288]{0:T(1024)(128)(4,1)S(1)}, s32[]{:S(2)}) async-start(s8[13107200]{0:T(1024)(128)(4,1)} %bitcast.624), calls=%async_computation.19 | async-start | bytes 1048576
  1406.1 36.3 %slice-start.18 = ((s8[13107200]{0:T(1024)(128)(4,1)}), s8[4194304]{0:T(1024)(128)(4,1)S(1)}, s32[]{:S(2)}) async-start(s8[13107200]{0:T(1024)(128)(4,1)} %bitcast.627), calls=%async_computation.22 | async-start | bytes 8388608
  1428.3 28.4 %slice-start.4 = ((s8[13107200]{0:T(1024)(128)(4,1)}), s8[4194304]{0:T(1024)(128)(4,1)S(1)}, s32[]{:S(2)}) async-start(s8[13107200]{0:T(1024)(128)(4,1)} %bitcast.615), calls=%async_computation.8 | async-start | bytes 8388608
  1428.4 28.4 %slice-start.5 = ((s8[13107200]{0:T(1024)(128)(4,1)}), s8[4194304]{0:T(1024)(128)(4,1)S(1)}, s32[]{:S(2)}) async-start(s8[13107200]{0:T(1024)(128)(4,1)} %bitcast.615), calls=%async_computation.9 | async-start | bytes 8388608
  1442.5 28.8 %slice-start.8 = ((s8[13107200]{0:T(1024)(128)(4,1)}), s8[4194304]{0:T(1024)(128)(4,1)S(1)}, s32[]{:S(2)}) async-start(s8[13107200]{0:T(1024)(128)(4,1)} %bitcast.620), calls=%async_computation.12 | async-start | bytes 8388608
  1442.5 28.8 %slice-start.9 = ((s8[13107200]{0:T(1024)(128)(4,1)}), s8[4194304]{0:T(1024)(128)(4,1)S(1)}, s32[]{:S(2)}) async-start(s8[13107200]{0:T(1024)(128)(4,1)} %bitcast.620), calls=%async_computation.13 | async-start | bytes 8388608
  1471.3 27.0 %slice-start.20 = ((s8[13107200]{0:T(1024)(128)(4,1)}), s8[524288]{0:T(1024)(128)(4,1)S(1)}, s32[]{:S(2)}) async-start(s8[13107200]{0:T(1024)(128)(4,1)} %bitcast.630), calls=%async_computation.24 | async-start | bytes 1048576
  1471.3 27.0 %slice-start.21 = ((s8[13107200]{0:T(1024)(128)(4,1)}), s8[4194304]{0:T(1024)(128)(4,1)S(1)}, s32[]{:S(2)}) async-start(s8[13107200]{0:T(1024)(128)(4,1)} %bitcast.630), calls=%async_computation.25 | async-start | bytes 8388608
  1498.4 18.3 %slice-start = ((s8[13107200]{0:T(1024)(128)(4,1)}), s8[4194304]{0:T(1024)(128)(4,1)S(1)}, s32[]{:S(2)}) async-start(s8[13107200]{0:T(1024)(128)(4,1)} %bitcast.612), calls=%async_computation.4 | async-start | bytes 8388608
  1542.8 108.1 %copy-start.1 = (f32[80,8,384]{2,1,0:T(8,128)S(1)}, f32[80,8,384]{2,1,0:T(8,128)}, u32[]{:S(2)}) copy-start(f32[80,8,384]{2,1,0:T(8,128)} %param.17) | copy-start | bytes 2949124
  (11 other events, 154.1 us)
where the time goes:
time: 1670 us; the launch traced here: 1650 us
  other arithmetic  562 us (34%)
  loops' own time  414 us (25%)
  matrix products  386 us (23%)
  local copies, waits for them, and re-layouts  213 us (13%)
  blocking collectives  41.9 us (3%)
  starting transfers between devices  18.9 us (1%)
    another operation x5, loops' own time, legendre_scan(): return lax.scan(advance, recurrence, degrees, unroll=8)  414 us
    eq x640, other arithmetic, advance(): degree == wave_ids[:, None]  403 us
    dot_general x5, matrix products, spectral_local(): paired = jnp.einsum('nml,lsfcm->sfcmn', legendre, folded, precision=highest)  86.5 us
    dot_general x1, matrix products, spread_tiles(): return jnp.einsum('rfkp,rkpq->rkfq', tiled, spread_map, precision=highest)  86.2 us
    dynamic_update_slice x80, local copies, waits for them, and re-layouts, legendre_scan(): return lax.scan(advance, recurrence, degrees, unroll=8)  77.5 us
    dot_general x1, matrix products, local(): jnp.einsum('rfx,xc->rfc', lax.all_to_all(diffused, 'lon', split_axis=1, c...  76.9 us
    dot_general x1, matrix products, local(): grid_part = jnp.einsum('rfc,xc->rfx', returned, fourier, precision=highest)  76.1 us
    while x560, other arithmetic  71.6 us
  transfers between devices with their start and end apart: 6, of which 1 were waited for; matrix products, arithmetic and copies ran while one was open for 40% of the time, Pallas kernels for 0%

commit v1 on v0

v1 whole, which is shorter than its diff:
```python
import math

import jax
import jax.numpy as jnp
import ml_dtypes
import numpy as np
from jax import lax
from jax.experimental import pallas as pl
from jax.experimental.pallas import tpu as pltpu
from jax.sharding import PartitionSpec as P

NLAT = 1280
NLON = 3072
NM = 640
FL = 8
STEN = 4
TILE = 128
ROWS = 80
TPR = 3
TILES = 240
N_LAT = 16
N_LON = 8
HALF = NLAT // 2
BAND = NLON // N_LON
GROUPS = 5
WAVE_DEV = 2 * GROUPS
DENSE = N_LON * TPR * ROWS
CHAINS = 4
DEG_PAD = (384, 256, 256, 128, 128)
DEG_USED = (320, 256, 192, 128, 64)
DEG_BASE = (0, 768, 1280, 1792, 2048)
DEG_TOTAL = 2304
VMEM = 60 * 1024 * 1024

f32 = jnp.float32
bf16 = jnp.bfloat16
NT = (((1,), (1,)), ((), ()))
NN = (((1,), (0,)), ((), ()))


def two_parts(values):
    high = values.astype(ml_dtypes.bfloat16)
    low = (values - high.astype(np.float64)).astype(ml_dtypes.bfloat16)
    return high, low


def wave_tables():
    h = np.arange(N_LAT)[:, None]
    g = np.arange(GROUPS)[None, :]
    points = np.arange(BAND)

    def angle(m1):
        waves = (m1 + 8 * h + 128 * g).reshape(-1)
        return (waves[:, None] * points[None, :] % NLON) * (2.0 * math.pi / NLON)

    def rows(first, second):
        return np.stack([first, second], axis=1).reshape(-1, first.shape[-1])

    real = np.stack([rows(np.cos(angle(m1)), -np.sin(angle(m1))) for m1 in (0, 4)])
    mixed = []
    for q in (1, 2, 3):
        a, b = angle(q), angle(8 - q)
        upper = rows(
            np.concatenate([np.cos(a), np.sin(a)], 1), np.concatenate([-np.sin(a), np.cos(a)], 1)
        )
        lower = rows(
            np.concatenate([np.cos(b), -np.sin(b)], 1),
            np.concatenate([-np.sin(b), -np.cos(b)], 1),
        )
        mixed.append(np.concatenate([upper, lower], 0))
    return real, np.stack(mixed)


def log_norms():
    return np.array(
        [
            0.5 * (math.lgamma(m + 1.5) - math.lgamma(m + 1.0) - 0.5 * math.log(math.pi))
            for m in range(NM)
        ]
    )


def split(values):
    high = values.astype(bf16)
    low = (values - high.astype(f32)).astype(bf16)
    return high, low


def dot(a, b, dims):
    return lax.dot_general(a, b, dims, preferred_element_type=f32)


def spread_kernel(grid_ref, stencil_ref, weight_ref, out_ref):
    block = grid_ref.shape[0]
    step = pl.program_id(0)
    target = lax.broadcasted_iota(jnp.int32, (TILE, STEN * TILE), 0).astype(jnp.int16)
    one = jnp.ones((TILE, STEN * TILE), bf16)
    zero = jnp.zeros((TILE, STEN * TILE), bf16)
    for r in range(block):
        for k in range(TPR):
            field = grid_ref[r, :, k * TILE : (k + 1) * TILE]
            scaled = jnp.concatenate(
                [field * weight_ref[r, k, s : s + 1, :] for s in range(STEN)], axis=1
            )
            high = scaled.astype(bf16).astype(f32)
            sides = jnp.concatenate([high, scaled - high], axis=0).astype(bf16)
            points = jnp.concatenate(
                [
                    jnp.broadcast_to(stencil_ref[r, k, s : s + 1, :], (16, TILE))
                    for s in range(STEN)
                ],
                axis=1,
            ).astype(jnp.int16)
            points = jnp.concatenate([points] * (TILE // 16), axis=0)
            hot = jnp.where(points == target, one, zero)
            both = dot(sides, hot, NT)
            tile = step * (block * TPR) + r * TPR + k
            out_ref[pl.ds(tile, FL, stride=TILES), :] = both[:FL] + both[FL:]


def spread_call(grid, stencil, weight):
    block = 8
    return pl.pallas_call(
        spread_kernel,
        grid=(ROWS // block,),
        in_specs=[
            pl.BlockSpec((block, FL, BAND), lambda i: (i, 0, 0)),
            pl.BlockSpec((block, TPR, STEN, TILE), lambda i: (i, 0, 0, 0)),
            pl.BlockSpec((block, TPR, STEN, TILE), lambda i: (i, 0, 0, 0)),
        ],
        out_specs=pl.BlockSpec((FL * TILES, TILE), lambda i: (0, 0)),
        out_shape=jax.ShapeDtypeStruct((FL * TILES, TILE), f32),
        compiler_params=pltpu.CompilerParams(vmem_limit_bytes=VMEM),
        name="spread",
    )(grid, stencil, weight)


def table_kernel(order_ref, norm_ref, sine_ref, logcos_ref, high_ref, low_ref, ring):
    order = order_ref[...]
    order_wide = jnp.concatenate([order] * GROUPS, axis=1)
    norm_wide = jnp.concatenate([norm_ref[...]] * GROUPS, axis=1)
    sine = jnp.broadcast_to(sine_ref[...], (8, HALF))
    exponent = norm_wide + order_wide * logcos_ref[...]
    kept = exponent >= -60.0
    diagonal = jnp.where(kept, jnp.exp(jnp.where(kept, exponent, 0.0)), 0.0)
    order_sq = order * order

    def scale_of(degree):
        return jnp.sqrt(
            jnp.maximum(4.0 * degree * degree - 1.0, 1.0)
            / jnp.maximum(degree * degree - order_sq, 1.0)
        )

    def advance(block, carried):
        previous, earlier, scale_prev = carried
        for local in range(32):
            degree = order + (block * 32 + local).astype(f32)
            scale = scale_of(degree)
            ratio = scale / scale_prev
            wide = jnp.concatenate([scale] * GROUPS, axis=1)
            wide_ratio = jnp.concatenate([ratio] * GROUPS, axis=1)
            stepped = (wide * sine) * previous - wide_ratio * earlier
            if local == 0:
                stepped = jnp.where(block == 0, diagonal, stepped)
            slot = (local % 2) * 16 + local // 2
            for v in range(GROUPS):
                at = v * 256 + slot * 8
                ring[at : at + 8, :] = stepped[:, v * TILE : (v + 1) * TILE]
            earlier = previous
            previous = stepped
            scale_prev = scale
        for g in range(GROUPS):

            @pl.when(block * 16 < DEG_USED[g])
            def _():
                for parity in range(2):
                    rows = jnp.concatenate(
                        [
                            ring[pl.ds(v * 256 + parity * 128 + g, 16, stride=8), :]
                            for v in range(GROUPS)
                        ],
                        axis=1,
                    )
                    high, low = split(rows)
                    start = pl.multiple_of(
                        DEG_BASE[g] + parity * DEG_PAD[g] + block * 16, 16
                    )
                    high_ref[pl.ds(start, 16), :] = high
                    low_ref[pl.ds(start, 16), :] = low

        return previous, earlier, scale_prev

    for g in range(GROUPS):
        extra = DEG_PAD[g] - DEG_USED[g]
        if extra:
            for parity in range(2):
                start = DEG_BASE[g] + parity * DEG_PAD[g] + DEG_USED[g]
                high_ref[start : start + extra, :] = jnp.zeros((extra, HALF), bf16)
                low_ref[start : start + extra, :] = jnp.zeros((extra, HALF), bf16)
    blank = jnp.zeros((8, HALF), f32)
    lax.fori_loop(0, NM // 32, advance, (blank, blank, jnp.ones((8, TILE), f32)))


def table_call(order, norm, sine, logcos):
    shape = jax.ShapeDtypeStruct((DEG_TOTAL, HALF), bf16)
    return pl.pallas_call(
        table_kernel,
        out_shape=(shape, shape),
        scratch_shapes=[pltpu.VMEM((GROUPS * 256, TILE), f32)],
        compiler_params=pltpu.CompilerParams(vmem_limit_bytes=VMEM),
        cost_estimate=pl.CostEstimate(
            flops=640 * 5120 * 20, bytes_accessed=6_000_000, transcendentals=640 * 2048
        ),
        name="legendre_table",
    )(order, norm, sine, logcos)


def fourier_kernel(
    key_ref,
    south_ref,
    tiles_ref,
    real_high,
    real_low,
    mixed_high,
    mixed_low,
    dense_ref,
    out_ref,
    *scratch,
):
    sums = scratch[:CHAINS]
    c_high, c_low = scratch[CHAINS:]
    per_chain = N_LON * TILES // CHAINS
    for chain in sums:
        chain[...] = jnp.zeros(chain.shape, f32)

    def scatter(t, _):
        for c, chain in enumerate(sums):
            at = c * per_chain + t
            slot = key_ref[at]
            chain[pl.ds(slot, 1), :] = chain[pl.ds(slot, 1), :] + tiles_ref[pl.ds(at, 1), :]
        return 0

    lax.fori_loop(0, per_chain, scatter, 0, unroll=4)
    south = south_ref[0]
    root = math.sqrt(0.5)
    blank = jnp.zeros((16, NLON), bf16)
    c_high[240:256, :] = blank
    c_low[240:256, :] = blank

    def butterfly(item, _):
        place = item // 5
        chunk = item % 5
        band = jnp.where(south == 1, 2 - place, place)
        row = pl.multiple_of(place * ROWS + chunk * 16, 16)

        def put(column, values):
            high, low = split(values)
            c_high[pl.ds(row, 16), column : column + TILE] = high
            c_low[pl.ds(row, 16), column : column + TILE] = low

        for k in range(TPR):
            d = []
            for b in range(N_LON):
                start = pl.multiple_of(
                    band * DENSE + (b * TPR + k) * ROWS + chunk * 16, 16
                )
                total = sums[0][pl.ds(start, 16), :]
                for chain in sums[1:]:
                    total = total + chain[pl.ds(start, 16), :]
                dense_ref[pl.ds(start, 16), :] = total
                d.append(total)
            s = [d[i] + d[i + 4] for i in range(4)]
            t = [d[i] - d[i + 4] for i in range(4)]
            even, odd = s[0] + s[2], s[1] + s[3]
            minus = (t[1] - t[3]) * root
            plus = (t[1] + t[3]) * root
            at = k * TILE
            put(at, even + odd)
            put(BAND + at, even - odd)
            put(2 * BAND + at, t[0] + minus)
            put(3 * BAND + at, -t[2] - plus)
            put(4 * BAND + at, s[0] - s[2])
            put(5 * BAND + at, s[3] - s[1])
            put(6 * BAND + at, t[0] - minus)
            put(7 * BAND + at, t[2] - plus)
        return 0

    lax.fori_loop(0, 15, butterfly, 0)

    def emit(m1, block):
        for h in range(N_LAT):
            for g in range(GROUPS):
                start = h * WAVE_DEV + 2 * g
                out_ref[h * 8 + m1, g, :, :] = block[start : start + 2, :]

    for i, m1 in enumerate((0, 4)):
        ch = c_high[:, i * BAND : (i + 1) * BAND]
        cl = c_low[:, i * BAND : (i + 1) * BAND]
        wh, wl = real_high[i], real_low[i]
        emit(m1, dot(wh, ch, NT) + (dot(wh, cl, NT) + dot(wl, ch, NT)))
    for q in (1, 2, 3):
        ch = c_high[:, 2 * q * BAND : (2 * q + 2) * BAND]
        cl = c_low[:, 2 * q * BAND : (2 * q + 2) * BAND]
        for half, m1 in enumerate((q, 8 - q)):
            wh = mixed_high[q - 1, half * 160 : half * 160 + 160, :]
            wl = mixed_low[q - 1, half * 160 : half * 160 + 160, :]
            emit(m1, dot(wh, ch, NT) + (dot(wh, cl, NT) + dot(wl, ch, NT)))


def fourier_call(keys, south, tiles, tables):
    vmem = pl.BlockSpec(memory_space=pltpu.VMEM)
    smem = pl.BlockSpec(memory_space=pltpu.SMEM)
    return pl.pallas_call(
        fourier_kernel,
        in_specs=[smem, smem] + [vmem] * 5,
        out_specs=(vmem, vmem),
        out_shape=(
            jax.ShapeDtypeStruct((3 * DENSE, TILE), f32),
            jax.ShapeDtypeStruct((N_LAT * N_LON, GROUPS, 2, 256), f32),
        ),
        scratch_shapes=[pltpu.VMEM((3 * DENSE, TILE), f32)] * CHAINS
        + [pltpu.VMEM((256, NLON), bf16)] * 2,
        compiler_params=pltpu.CompilerParams(vmem_limit_bytes=VMEM),
        name="scatter_fourier",
    )(keys, south, tiles, *tables)


def legendre_kernel(
    wave_ref, coeff_ref, high_ref, low_ref, mix_ref, weight_ref, rate_ref, out_ref, north, south
):
    weight = weight_ref[...]
    row16 = lax.broadcasted_iota(jnp.int32, (16, HALF), 0)
    first_level = (row16 // 2) % 2 == 0
    dn, xn, ds, xs = (mix_ref[i] for i in range(4))

    def mixed(values, own, cross):
        ahead = pltpu.roll(values, 14, 0)
        behind = pltpu.roll(values, 2, 0)
        other = jnp.where(first_level, ahead, behind)
        return values + own * values + cross * other

    pad = jnp.zeros((16, TILE), f32)
    for g in range(GROUPS):
        north[...] = jnp.zeros(north.shape, f32)
        south[...] = jnp.zeros(south.shape, f32)
        for a in range(N_LAT):
            total, place = (north, a) if a < 8 else (south, 15 - a)
            piece = jnp.concatenate([coeff_ref[a * 8 + f, g, :, :] for f in range(FL)], axis=0)
            piece = jnp.concatenate([piece, pad], axis=1)
            offset = ROWS * place + 48
            base = offset // TILE * TILE
            total[:, base : base + 384] += pltpu.roll(piece, offset % TILE, 1)
        extra_n = north[:, 768:896]
        extra_s = south[:, 768:896]
        north[:, 640:768] += pltpu.roll(extra_s, 48, 1)
        south[:, 640:768] += pltpu.roll(extra_n, 48, 1)
        full_n = mixed(north[:, 128:768], dn, xn)
        full_s = mixed(south[:, 128:768], ds, xs)
        pad_len = DEG_PAD[g]
        wave = wave_ref[0] + 128 * g
        factor = jnp.where(wave == 0, 1.0, 2.0).astype(f32)
        lane = lax.broadcasted_iota(jnp.int32, (16, pad_len), 1)
        rate = jnp.concatenate([rate_ref[...]] * (pad_len // TILE), axis=1)
        results = []
        for parity, folded in enumerate((full_n + full_s, full_n - full_s)):
            folded = folded * weight
            fh, fl = split(folded)
            start = DEG_BASE[g] + parity * pad_len
            ph = high_ref[start : start + pad_len, :]
            pw = low_ref[start : start + pad_len, :]
            spectrum = dot(fh, ph, NT) + (dot(fl, ph, NT) + dot(fh, pw, NT))
            degree = wave + parity + 2 * lane
            degree_f = degree.astype(f32)
            ratio = rate * (degree_f * (degree_f + 1.0) / float(NM * (NM + 1)))
            damped = spectrum * (-ratio / (1.0 + ratio)) * factor
            damped = jnp.where(degree < NM, damped, 0.0)
            dh, dl = split(damped)
            results.append(dot(dh, ph, NN) + (dot(dl, ph, NN) + dot(dh, pw, NN)))
        for a in range(N_LAT):
            place = a if a < 8 else 15 - a
            offset = ROWS * place
            base = offset // TILE * TILE
            shift = offset % TILE
            width = TILE if shift <= 48 else 256
            even = results[0][:, base : base + width]
            odd = results[1][:, base : base + width]
            piece = even + odd if a < 8 else even - odd
            if shift:
                piece = pltpu.roll(piece, width - shift, 1)
            for f in range(FL):
                out_ref[a * 8 + f, g, :, :] = piece[2 * f : 2 * f + 2, :TILE]


def legendre_call(wave, coeff, high, low, mix, weight, rate):
    vmem = pl.BlockSpec(memory_space=pltpu.VMEM)
    smem = pl.BlockSpec(memory_space=pltpu.SMEM)
    return pl.pallas_call(
        legendre_kernel,
        in_specs=[smem] + [vmem] * 6,
        out_specs=vmem,
        out_shape=jax.ShapeDtypeStruct((N_LAT * N_LON, GROUPS, 2, TILE), f32),
        scratch_shapes=[pltpu.VMEM((16, 896), f32)] * 2,
        compiler_params=pltpu.CompilerParams(vmem_limit_bytes=VMEM),
        name="legendre",
    )(wave, coeff, high, low, mix, weight, rate)


def inverse_kernel(
    back_ref,
    real_high,
    real_low,
    mixed_high,
    mixed_low,
    own_ref,
    other_ref,
    mix_ref,
    out_ref,
    waves,
    synth,
):
    for m1 in range(8):
        for h in range(N_LAT):
            for g in range(GROUPS):
                start = m1 * 160 + h * WAVE_DEV + 2 * g
                waves[start : start + 2, :] = back_ref[h * 8 + m1, g, :, :]

    def transform(parts, wh, wl):
        stacked = jnp.concatenate([waves[m1 * 160 : m1 * 160 + 160, :] for m1 in parts], axis=0)
        ah, al = split(stacked.T[:ROWS, :])
        return dot(ah, wh, NN) + (dot(al, wh, NN) + dot(ah, wl, NN))

    for i, m1 in enumerate((0, 4)):
        synth[:, i * BAND : (i + 1) * BAND] = transform((m1,), real_high[i], real_low[i])
    for q in (1, 2, 3):
        synth[:, 2 * q * BAND : (2 * q + 2) * BAND] = transform(
            (q, 8 - q), mixed_high[q - 1], mixed_low[q - 1]
        )
    root = math.sqrt(0.5)

    def combine(chunk, _):
        row = pl.multiple_of(chunk * 16, 16)
        diag = mix_ref[0, pl.ds(row, 16), :]
        cross = mix_ref[1, pl.ds(row, 16), :]
        for k in range(TPR):
            y = [
                synth[pl.ds(row, 16), i * BAND + k * TILE : i * BAND + (k + 1) * TILE]
                for i in range(8)
            ]
            e0, e1 = y[0] + y[1], y[0] - y[1]
            r1, i1, r2, i2, r3, i3 = y[2:]
            even = (e0 + r2, e1 - i2, e0 - r2, e1 + i2)
            odd = (
                r1 + r3,
                ((r1 - i1) - (r3 + i3)) * root,
                i3 - i1,
                ((r3 - i3) - (r1 + i1)) * root,
            )
            for b in range(N_LON):
                at = pl.multiple_of((b * TPR + k) * ROWS + chunk * 16, 16)
                own = own_ref[pl.ds(at, 16), :]
                diffused = own + diag * own + cross * other_ref[pl.ds(at, 16), :]
                wave = even[b % 4] + odd[b % 4] if b < 4 else even[b % 4] - odd[b % 4]
                out_ref[pl.ds(at, 16), :] = diffused + wave
        return 0

    lax.fori_loop(0, ROWS // 16, combine, 0)


def inverse_call(back, tables, own, other, mix):
    vmem = pl.BlockSpec(memory_space=pltpu.VMEM)
    return pl.pallas_call(
        inverse_kernel,
        in_specs=[vmem] * 8,
        out_specs=vmem,
        out_shape=jax.ShapeDtypeStruct((DENSE, TILE), f32),
        scratch_shapes=[pltpu.VMEM((8 * 160, TILE), f32), pltpu.VMEM((ROWS, NLON), f32)],
        compiler_params=pltpu.CompilerParams(vmem_limit_bytes=VMEM),
        name="inverse_fourier",
    )(back, *tables, own, other, mix)


def place_kernel(south_ref, rows_ref, out_ref):
    south = south_ref[0]

    def place(i, _):
        target = jnp.where(south == 1, ROWS - 1 - i, i)
        for k in range(TPR):
            out_ref[target, :, k * TILE : (k + 1) * TILE] = rows_ref[
                pl.ds(k * ROWS + i, FL, stride=TILES), :
            ]
        return 0

    lax.fori_loop(0, ROWS, place, 0, unroll=8)


def place_call(south, rows):
    vmem = pl.BlockSpec(memory_space=pltpu.VMEM)
    smem = pl.BlockSpec(memory_space=pltpu.SMEM)
    return pl.pallas_call(
        place_kernel,
        in_specs=[smem, vmem],
        out_specs=vmem,
        out_shape=jax.ShapeDtypeStruct((ROWS, FL, BAND), f32),
        compiler_params=pltpu.CompilerParams(vmem_limit_bytes=VMEM),
        name="place_rows",
    )(south, rows)


def local(
    adjoint_grid, tile_owner, tile_slot, stencil, interp_weight, vertical_offset, diffusion_rate
):
    lat_here = lax.axis_index("lat")
    lon_here = lax.axis_index("lon")
    is_south = lat_here >= N_LAT // 2
    south = is_south.astype(jnp.int32).reshape(1)
    wave = (lon_here + 8 * lat_here).astype(jnp.int32)

    owners = tile_owner.reshape(TILES)
    slots = tile_slot.reshape(TILES)
    dest_lat = owners // N_LON
    rows = slots // TPR
    rows = jnp.where(dest_lat >= N_LAT // 2, ROWS - 1 - rows, rows)
    columns = (owners % N_LON) * TPR + slots % TPR
    keys = ((dest_lat - lat_here + 1) * (N_LON * TPR) + columns) * ROWS + rows
    keys = lax.all_gather(keys, "lon", tiled=True)

    mix = vertical_offset.reshape(ROWS, 16)
    mix = jnp.where(is_south, jnp.flip(mix, 0), mix).T
    mix_all = lax.all_gather(mix, "lat")
    half = N_LAT // 2
    mix_north = mix_all[:half].transpose(1, 0, 2).reshape(16, HALF)
    mix_south = jnp.flip(mix_all[half:], 0).transpose(1, 0, 2).reshape(16, HALF)
    own_ids = [(f // 2) * 4 + (f % 2) * 2 + f % 2 for f in range(FL)]
    cross_ids = [(f // 2) * 4 + (1 - f % 2) * 2 + f % 2 for f in range(FL)]

    def picked(table, ids):
        return jnp.stack([table[i] for i in ids for _ in range(2)], axis=0)

    mix_waves = jnp.stack(
        [
            picked(mix_north, own_ids),
            picked(mix_north, cross_ids),
            picked(mix_south, own_ids),
            picked(mix_south, cross_ids),
        ]
    )
    level = lon_here % 2
    field = lon_here // 2
    own_row = lax.dynamic_index_in_dim(mix, field * 4 + level * 3, 0, False)
    cross_row = lax.dynamic_index_in_dim(mix, field * 4 + (1 - level) * 2 + level, 0, False)
    mix_grid = jnp.broadcast_to(
        jnp.stack([own_row, cross_row])[:, :, None], (2, ROWS, TILE)
    )

    latitude = 0.5 * math.pi - math.pi * (np.arange(HALF) + 0.5) / NLAT
    sine = jnp.asarray(np.sin(latitude)[None, :], f32)
    logcos = jnp.asarray(np.log(np.cos(latitude))[None, :], f32)
    weight = jnp.asarray((math.pi / NLAT * np.cos(latitude) / NLON)[None, :], f32)
    groups = np.zeros((TILE, 8))
    groups[:, :GROUPS] = log_norms().reshape(GROUPS, TILE).T
    norm = lax.dynamic_index_in_dim(jnp.asarray(groups, f32), wave, 0, False)
    norm = jnp.broadcast_to(norm[:, None], (8, TILE))
    group_start = jnp.minimum(jnp.arange(8, dtype=jnp.int32), GROUPS - 1) * TILE
    order = jnp.broadcast_to((wave + group_start).astype(f32)[:, None], (8, TILE))
    rate = jnp.broadcast_to(
        jnp.repeat(diffusion_rate, 2, total_repeat_length=16)[:, None], (16, TILE)
    )
    real, mixed = wave_tables()
    tables = tuple(jnp.asarray(part) for part in two_parts(real) + two_parts(mixed))

    spread = spread_call(adjoint_grid, stencil, interp_weight)
    tiles = lax.all_to_all(spread, "lon", 0, 0, tiled=True)
    high, low = table_call(order, norm, sine, logcos)
    dense, coeff = fourier_call(keys, south, tiles, tables)
    dense = dense.reshape(3, DENSE, TILE)
    below = lax.ppermute(dense[0], "lat", [(i + 1, i) for i in range(N_LAT - 1)])
    above = lax.ppermute(dense[2], "lat", [(i, i + 1) for i in range(N_LAT - 1)])
    coeff = lax.all_to_all(coeff, ("lat", "lon"), 0, 0, tiled=True)
    back = legendre_call(wave.reshape(1), coeff, high, low, mix_waves, weight, rate)
    departed = dense[1] + below + above
    other = lax.ppermute(departed, "lon", [(i, i ^ 1) for i in range(N_LON)])
    back = lax.all_to_all(back, ("lat", "lon"), 0, 0, tiled=True)
    result = inverse_call(back, tables, departed, other, mix_grid)
    result = lax.all_to_all(result, "lon", 0, 0, tiled=True)
    return place_call(south, result)


def solution(mesh):
    in_specs = (
        P("lat", None, "lon"),
        P("lat", "lon", None, None),
        P("lat", "lon", None, None),
        P("lat", "lon", None, None),
        P("lat", "lon", None, None),
        P("lat", None, None, None),
        P(),
    )
    out_specs = P("lat", None, "lon")
    return jax.shard_map(local, mesh=mesh, in_specs=in_specs, out_specs=out_specs, check_vma=False)
```

time: 1670 us -> 188 us (0.11); the launches traced: 1650 us -> 188 us
  other arithmetic: 562 us -> 2.64 us
  loops' own time: 414 us -> 0 us
  matrix products: 386 us -> 0 us
  local copies, waits for them, and re-layouts: 213 us -> 12.3 us
  Pallas kernels: 0 us -> 50.5 us
  blocking collectives: 41.9 us -> 70.6 us
    another operation x5 -> x0, loops' own time: 414 us -> none  [legendre_scan(): return lax.scan(advance, recurrence, degrees, unroll=8)]
    eq x643 -> x0, other arithmetic: 403 us -> none  [the longest x640 403 us: advance(): degree == wave_ids[:, None]]
    dot_general x14 -> x0, matrix products: 386 us -> none  [the longest x5 86.5 us: spectral_local(): paired = jnp.einsum('nml,lsfcm->sfcmn', legendre, folded, precision=highest)]
    dynamic_update_slice x80 -> x0, local copies, waits for them, and re-layouts: 77.5 us -> none  [legendre_scan(): return lax.scan(advance, recurrence, degrees, unroll=8)]
    while x560 -> x0, other arithmetic: 71.6 us -> none
    slice x98 -> x38, local copies, waits for them, and re-layouts: 67.3 us -> 5.22 us  [the longest x34 2.6 us: picked(): return jnp.stack([table[i] for i in ids for _ in range(2)], axis=0)]
    scatter-add x1 -> x0, other arithmetic: 53.4 us -> none  [local(): jax.ops.segment_sum(arrived[:, :fields_levels], targets, num_segments=til...]
    pallas_call x0 -> x6, Pallas kernels: none -> 50.5 us  [the longest x1 11.4 us: fourier_call(): pl.pallas_call(fourier_kernel, in_specs=[smem, smem] + [vmem] * 5, out_sp...]
  transfers between devices with their start and end apart: 6 -> 6, of which waited for: 1 -> 2; matrix products, arithmetic and copies ran while one was open for 40% -> 5% of each run, Pallas kernels for 0% -> 11%
where the time goes in v1:
time: 188 us
  blocking collectives  70.6 us (38%)
  Pallas kernels  50.5 us (27%)
  starting transfers between devices  32.4 us (17%)
  waiting for transfers between devices  18.2 us (10%)
  local copies, waits for them, and re-layouts  12.3 us (7%)
  other arithmetic  2.64 us (1%)
    all_gather x1, blocking collectives, local(): mix_all = lax.all_gather(mix, 'lat')  35.5 us
    all_to_all x1, blocking collectives, local(): result = lax.all_to_all(result, 'lon', 0, 0, tiled=True)  19.9 us
    unnamed x1, blocking collectives  15.3 us
    all_to_all x1, waiting for transfers between devices, local(): back = lax.all_to_all(back, ('lat', 'lon'), 0, 0, tiled=True)  14.7 us
    all_to_all x1, starting transfers between devices, local(): coeff = lax.all_to_all(coeff, ('lat', 'lon'), 0, 0, tiled=True)  13.4 us
    pallas_call x1, Pallas kernels, fourier_call(): pl.pallas_call(fourier_kernel, in_specs=[smem, smem] + [vmem] * 5, out_sp...  11.4 us
    pallas_call x1, Pallas kernels, spread_call(): pl.pallas_call(spread_kernel, grid=(ROWS // block,), in_specs=[pl.BlockSp...  11.3 us
    pallas_call x1, Pallas kernels, legendre_call(): pl.pallas_call(legendre_kernel, in_specs=[smem] + [vmem] * 6, out_specs=v...  11.3 us
  transfers between devices with their start and end apart: 6, of which 2 were waited for; matrix products, arithmetic and copies ran while one was open for 5% of the time, Pallas kernels for 11%

profile of v1, /device:TPU:1, one launch (start us, length us, event | category | flops | bytes accessed | tf_op | source)
XLA Modules:
  0.0 187.6 jit_solution(17060566964624268134)
XLA Ops:
  0.0 11.3 %spread.1 = f32[1920,128]{1,0:T(8,128)} custom-call(f32[80,8,384]{2,1,0:T(8,128)} %grid_ref.1, s32[80,3,4,128]{3,2,1,0:T(4,128)} %stencil_ref.1, f32[80,3,4,128]{3,2,1,0:T(4,128)} %weight_ref.2), custom_call_target="tpu_custom_call" | custom-call | tf_op jit(solution)/shard_map/spread/pallas_call | solution.py:123
  11.4 6.0 %all-to-all-start = ((f32[8,240,128]{2,1,0:T(8,128)}), f32[8,240,128]{2,1,0:T(8,128)S(1)}, u32[]{:S(2)}, u32[]{:S(2)}) async-start(f32[8,240,128]{2,1,0:T(8,128)} %bitcast.30), calls=%async_computation | async-start | bytes 1966080 | tf_op jit(solution)/shard_map/all_to_all | solution.py:572
  18.9 15.3 %all-reduce.key_ref = s32[1920]{0:T(1024)} all-reduce(s32[1920]{0:T(1024)S(1)} %fusion.4), channel_id=1, replica_groups=mesh['lat'=16,'lon'=8] {'lon'}, use_global_device_ids=true, to_apply=%add | all-reduce | flops 1920 | bytes 15360
  34.1 0.9 copy-done.3
  35.1 11.4 %scatter_fourier.1 = (f32[5760,128]{1,0:T(8,128)}, f32[128,5,2,256]{3,2,1,0:T(2,128)}) custom-call(s32[1920]{0:T(1024)} %all-reduce.key_ref, s32[1]{0:T(128)} %bitcast.south_ref, f32[1920,128]{1,0:T(8,128)} %bitcast.29, bf16[2,160,384]{2,1,0:T(8,128)(2,1)} %constant.192.clone.real_high, bf16[2,160,384]{2,1,0:T(8,128)(2,1)} %constant.193.clone.real_low, ...), custom_call_target="tpu_custom_call" | custom-call | tf_op jit(solution)/shard_map/scatter_fourier/pallas_call | solution.py:313
  46.5 2.6 %fusion.8 = (f32[1920,128]{1,0:T(8,128)}, f32[1920,128]{1,0:T(8,128)S(1)}) fusion(f32[5760,128]{1,0:T(8,128)} %get-tuple-element.24), kind=kLoop, calls=%fused_computation.30 | loop fusion | bytes 3932160 | tf_op jit(solution)/shard_map/slice | solution.py:576
  49.1 1.4 collective-permute-start
  50.5 5.0 %collective-permute-start.1 = (f32[1920,128]{1,0:T(8,128)S(1)}, f32[1920,128]{1,0:T(8,128)}, u32[]{:S(2)}, u32[]{:S(2)}) collective-permute-start(f32[1920,128]{1,0:T(8,128)S(1)} %get-tuple-element.26), channel_id=1, source_target_pairs={{0,8},{8,16},{16,24},{24,32},{32,40},{40,48},{48,56},{56,64},{64,7... | collective-permute-start | bytes 2949128 | tf_op jit(solution)/shard_map/ppermute | solution.py:577
  55.5 35.5 %all-gather = f32[256,80]{1,0:T(8,128)S(1)} all-gather(f32[16,80]{1,0:T(8,128)S(1)} %bitcast.40), channel_id=2, replica_groups=mesh['lat'=16,'lon'=8] {'lat'}, dimensions={0}, use_global_device_ids=true | all-gather | bytes 87040 | tf_op jit(solution)/shard_map/all_gather | solution.py:529
  91.0 13.4 %all-to-all-start.1 = ((f32[128,5,2,256]{3,2,1,0:T(2,128)}), f32[128,5,2,256]{3,2,1,0:T(2,128)S(1)}, u32[]{:S(2)}, u32[]{:S(2)}) async-start(f32[128,5,2,256]{3,2,1,0:T(2,128)} %get-tuple-element.21), calls=%async_computation.1 | async-start | bytes 2621440 | tf_op jit(solution)/shard_map/all_to_all | solution.py:578
  108.3 1.7 add_add_fusion.own_ref
  110.0 1.1 collective-permute-start.2
  111.2 0.7 fusion.5
  113.2 8.8 %legendre_table.1 = (bf16[2304,640]{1,0:T(8,128)(2,1)}, bf16[2304,640]{1,0:T(8,128)(2,1)}) custom-call(f32[8,128]{1,0:T(8,128)} %broadcast_in_dim.11.order_ref, f32[8,128]{1,0:T(8,128)} %broadcast_in_dim.13.norm_ref, f32[1,640]{1,0:T(1,128)} %constant.188.clone.sine_ref, f32[1,640]{1,0:T(1,128)} %constant.189.clone.logcos_ref), custom_call_target="tpu_custom_call" | custom-call | flops 65536000 | bytes 6000000 | tf_op jit(solution)/shard_map/legendre_table/pallas_call | solution.py:206
  122.0 0.7 pad_maximum_fusion.mix_ref
  122.7 3.4 %all-to-all-done.1.coeff_ref = f32[128,5,2,256]{3,2,1,0:T(2,128)S(1)} async-done(((f32[128,5,2,256]{3,2,1,0:T(2,128)}), f32[128,5,2,256]{3,2,1,0:T(2,128)S(1)}, u32[]{:S(2)}, u32[]{:S(2)}) %all-to-all-start.1) | async-done | bytes 1310752 | tf_op jit(solution)/shard_map/all_to_all | solution.py:578
  126.1 0.7 broadcast_in_dim.15.rate_ref
  127.2 11.3 %legendre.1 = f32[128,5,2,128]{3,2,1,0:T(2,128)} custom-call(s32[1]{0:T(128)} %bitcast.1.wave_ref, f32[128,5,2,256]{3,2,1,0:T(2,128)} %copy-done.1, bf16[2304,640]{1,0:T(8,128)(2,1)} %get-tuple-element.22.high_ref, bf16[2304,640]{1,0:T(8,128)(2,1)} %get-tuple-element.23.low_ref, f32[4,16,640]{2,1,0:T(8,128)} %pad_maximum_fusion.mix_ref, ...), custom_call_target="tpu_custom_call" | custom-call | tf_op jit(solution)/shard_map/legendre/pallas_call | solution.py:397
  138.5 5.5 %all-to-all-start.2 = ((f32[128,5,2,128]{3,2,1,0:T(2,128)}), f32[128,5,2,128]{3,2,1,0:T(2,128)S(1)}, u32[]{:S(2)}, u32[]{:S(2)}) async-start(f32[128,5,2,128]{3,2,1,0:T(2,128)} %legendre.1), calls=%async_computation.2 | async-start | bytes 1310720 | tf_op jit(solution)/shard_map/all_to_all | solution.py:582
  144.1 14.7 %all-to-all-done.2.back_ref = f32[128,5,2,128]{3,2,1,0:T(2,128)S(1)} async-done(((f32[128,5,2,128]{3,2,1,0:T(2,128)}), f32[128,5,2,128]{3,2,1,0:T(2,128)S(1)}, u32[]{:S(2)}, u32[]{:S(2)}) %all-to-all-start.2) | async-done | bytes 655392 | tf_op jit(solution)/shard_map/all_to_all | solution.py:582
  158.8 0.9 broadcast_in_dim.16.mix_ref
  160.0 5.2 %inverse_fourier.1 = f32[1920,128]{1,0:T(8,128)} custom-call(f32[128,5,2,128]{3,2,1,0:T(2,128)} %copy-done.4, bf16[2,160,384]{2,1,0:T(8,128)(2,1)} %constant.192.clone.real_high, bf16[2,160,384]{2,1,0:T(8,128)(2,1)} %constant.193.clone.real_low, bf16[3,320,768]{2,1,0:T(8,128)(2,1)} %constant.194.clone.mixed_high, ...), custom_call_target="tpu_custom_call" | custom-call | tf_op jit(solution)/shard_map/inverse_fourier/pallas_call | solution.py:471
  165.2 19.9 %all_to_all.32 = f32[8,240,128]{2,1,0:T(8,128)} all-to-all(f32[8,240,128]{2,1,0:T(8,128)} %bitcast.28), channel_id=1, replica_groups=mesh['lat'=16,'lon'=8] {'lon'}, dimensions={0} | all-to-all | bytes 1966080 | tf_op jit(solution)/shard_map/all_to_all | solution.py:584
  185.1 2.5 %place_rows.1 = f32[80,8,384]{2,1,0:T(8,128)} custom-call(s32[1]{0:T(128)} %bitcast.south_ref, f32[1920,128]{1,0:T(8,128)} %bitcast.31), custom_call_target="tpu_custom_call" | custom-call | tf_op jit(solution)/shard_map/place_rows/pallas_call | solution.py:499
  (81 shorter events, 6.7 us)
Async XLA Ops:
  0.0 107.2 %copy-start = (f32[8]{0:T(128)S(1)}, f32[8]{0:T(128)}, u32[]{:S(2)}) copy-start(f32[8]{0:T(128)} %param.23) | copy-start | bytes 100
  0.0 17.4 %copy-start.10 = (u32[128]{0:T(128)S(1)}, u32[128]{0:T(128)}, u32[]{:S(2)}) copy-start(u32[128]{0:T(128)} %constant.203) | copy-start | bytes 1540
  0.0 17.3 %copy-start.6 = (f32[80,4,2,2]{0,3,2,1:T(2,128)S(1)}, f32[80,4,2,2]{0,3,2,1:T(2,128)}, u32[]{:S(2)}) copy-start(f32[80,4,2,2]{0,3,2,1:T(2,128)} %param.22) | copy-start | bytes 15364
  0.0 18.6 %copy-start.7 = (s32[1,1,240,1]{2,3,1,0:T(1,128)S(1)}, s32[1,1,240,1]{2,3,1,0:T(1,128)}, u32[]{:S(2)}) copy-start(s32[1,1,240,1]{2,3,1,0:T(1,128)} %param.19) | copy-start | bytes 2884
  0.0 18.7 %copy-start.8 = (s32[1,1,240,1]{2,3,1,0:T(1,128)S(1)}, s32[1,1,240,1]{2,3,1,0:T(1,128)}, u32[]{:S(2)}) copy-start(s32[1,1,240,1]{2,3,1,0:T(1,128)} %param.18) | copy-start | bytes 2884
  11.4 22.8 %all-to-all-start = ((f32[8,240,128]{2,1,0:T(8,128)}), f32[8,240,128]{2,1,0:T(8,128)S(1)}, u32[]{:S(2)}, u32[]{:S(2)}) async-start(f32[8,240,128]{2,1,0:T(8,128)} %bitcast.30), calls=%async_computation | async-start | bytes 1966080 | tf_op jit(solution)/shard_map/all_to_all | solution.py:572
  34.1 0.9 copy-start.3
  49.1 58.1 %copy-start.9 = (s32[16]{0:T(128)S(1)}, s32[16]{0:T(128)}, u32[]{:S(2)}) copy-start(s32[16]{0:T(128)} %constant.200) | copy-start | bytes 196
  49.1 59.2 %collective-permute-start = (f32[1920,128]{1,0:T(8,128)}, f32[1920,128]{1,0:T(8,128)S(1)}, u32[]{:S(2)}, u32[]{:S(2)}) collective-permute-start(f32[1920,128]{1,0:T(8,128)} %get-tuple-element.25), channel_id=1, source_target_pairs={{8,0},{16,8},{24,16},{32,24},{40,32},{48,40},{56,48},{64,56},{72,6... | collective-permute-start | bytes 2949128 | tf_op jit(solution)/shard_map/ppermute | solution.py:576
  50.5 57.8 %collective-permute-start.1 = (f32[1920,128]{1,0:T(8,128)S(1)}, f32[1920,128]{1,0:T(8,128)}, u32[]{:S(2)}, u32[]{:S(2)}) collective-permute-start(f32[1920,128]{1,0:T(8,128)S(1)} %get-tuple-element.26), channel_id=1, source_target_pairs={{0,8},{8,16},{16,24},{24,32},{32,40},{40,48},{48,56},{56,64},{64,7... | collective-permute-start | bytes 2949128 | tf_op jit(solution)/shard_map/ppermute | solution.py:577
  91.0 35.1 %all-to-all-start.1 = ((f32[128,5,2,256]{3,2,1,0:T(2,128)}), f32[128,5,2,256]{3,2,1,0:T(2,128)S(1)}, u32[]{:S(2)}, u32[]{:S(2)}) async-start(f32[128,5,2,256]{3,2,1,0:T(2,128)} %get-tuple-element.21), calls=%async_computation.1 | async-start | bytes 2621440 | tf_op jit(solution)/shard_map/all_to_all | solution.py:578
  110.0 28.5 %copy-start.2 = (f32[1920,128]{1,0:T(8,128)}, f32[1920,128]{1,0:T(8,128)S(1)}, u32[]{:S(2)}) copy-start(f32[1920,128]{1,0:T(8,128)S(1)} %add_add_fusion.own_ref) | copy-start | bytes 2949124
  110.0 48.8 %collective-permute-start.2 = (f32[1920,128]{1,0:T(8,128)S(1)}, f32[1920,128]{1,0:T(8,128)S(1)}, u32[]{:S(2)}, u32[]{:S(2)}) collective-permute-start(f32[1920,128]{1,0:T(8,128)S(1)} %add_add_fusion.own_ref), channel_id=1, source_target_pairs={{0,1},{1,0},{2,3},{3,2},{4,5},{5,4},{6,7},{7,6},{8,9},{9,8},{10,11... | collective-permute-start | bytes 2949128 | tf_op jit(solution)/shard_map/ppermute | solution.py:581
  126.1 1.1 copy-start.1
  138.5 20.3 %all-to-all-start.2 = ((f32[128,5,2,128]{3,2,1,0:T(2,128)}), f32[128,5,2,128]{3,2,1,0:T(2,128)S(1)}, u32[]{:S(2)}, u32[]{:S(2)}) async-start(f32[128,5,2,128]{3,2,1,0:T(2,128)} %legendre.1), calls=%async_computation.2 | async-start | bytes 1310720 | tf_op jit(solution)/shard_map/all_to_all | solution.py:582
  158.8 0.9 copy-start.4
  158.8 1.2 copy-start.5

commit v2 on v1

--- a/solution.py
+++ b/solution.py
@@ -25,6 +25,7 @@
 GROUPS = 5
 WAVE_DEV = 2 * GROUPS
 DENSE = N_LON * TPR * ROWS
+CHUNK = TILES + 8
 CHAINS = 4
 DEG_PAD = (384, 256, 256, 128, 128)
 DEG_USED = (320, 256, 192, 128, 64)
@@ -86,11 +87,17 @@
     return high, low
 
 
+def stacked_parts(values):
+    high = values.astype(bf16).astype(f32)
+    return jnp.concatenate([high, values - high], axis=0).astype(bf16)
+
+
 def dot(a, b, dims):
     return lax.dot_general(a, b, dims, preferred_element_type=f32)
 
 
-def spread_kernel(grid_ref, stencil_ref, weight_ref, out_ref):
+def spread_kernel(lon_ref, grid_ref, stencil_ref, weight_ref, owner_ref, slot_ref, *rest):
+    outs, (out_ref, sems) = rest[:N_LON], rest[N_LON:]
     block = grid_ref.shape[0]
     step = pl.program_id(0)
     target = lax.broadcasted_iota(jnp.int32, (TILE, STEN * TILE), 0).astype(jnp.int16)
@@ -115,24 +122,58 @@
             hot = jnp.where(points == target, one, zero)
             both = dot(sides, hot, NT)
             tile = step * (block * TPR) + r * TPR + k
-            out_ref[pl.ds(tile, FL, stride=TILES), :] = both[:FL] + both[FL:]
-
-
-def spread_call(grid, stencil, weight):
+            out_ref[pl.ds(tile, FL, stride=CHUNK), :] = both[:FL] + both[FL:]
+
+    @pl.when(step == pl.num_programs(0) - 1)
+    def _():
+        owner, slot = owner_ref[...], slot_ref[...]
+        dest_lat = owner // N_LON
+        line = (slot * 171) // 512
+        column = (owner - dest_lat * N_LON) * TPR + slot - line * TPR
+        line = jnp.where(dest_lat >= N_LAT // 2, ROWS - 1 - line, line)
+        keys = ((dest_lat - lon_ref[1] + 1) * (N_LON * TPR) + column) * ROWS + line
+        keys = keys.astype(f32)
+        for f in range(FL):
+            at = f * CHUNK + TILES
+            out_ref[at : at + 8, :] = jnp.zeros((8, TILE), f32)
+            out_ref[at : at + 1, :] = keys[:, :TILE]
+            out_ref[at + 1 : at + 2, : TILES - TILE] = keys[:, TILE:]
+        exchange = [
+            pltpu.make_async_copy(
+                out_ref.at[pl.ds(pl.multiple_of((lon_ref[0] ^ k) * CHUNK, 8), CHUNK), :],
+                outs[k],
+                sems.at[k],
+            )
+            for k in range(N_LON)
+        ]
+        for copy in exchange:
+            copy.start()
+        for copy in exchange:
+            copy.wait()
+
+
+def spread_call(lon, grid, stencil, weight, owner, slot):
     block = 8
     return pl.pallas_call(
         spread_kernel,
         grid=(ROWS // block,),
         in_specs=[
+            pl.BlockSpec(memory_space=pltpu.SMEM),
             pl.BlockSpec((block, FL, BAND), lambda i: (i, 0, 0)),
             pl.BlockSpec((block, TPR, STEN, TILE), lambda i: (i, 0, 0, 0)),
             pl.BlockSpec((block, TPR, STEN, TILE), lambda i: (i, 0, 0, 0)),
+            pl.BlockSpec((1, TILES), lambda i: (0, 0)),
+            pl.BlockSpec((1, TILES), lambda i: (0, 0)),
         ],
-        out_specs=pl.BlockSpec((FL * TILES, TILE), lambda i: (0, 0)),
-        out_shape=jax.ShapeDtypeStruct((FL * TILES, TILE), f32),
+        out_specs=[pl.BlockSpec(memory_space=pl.ANY)] * N_LON,
+        out_shape=[jax.ShapeDtypeStruct((CHUNK, TILE), f32)] * N_LON,
+        scratch_shapes=[
+            pltpu.VMEM((FL * CHUNK, TILE), f32),
+            pltpu.SemaphoreType.DMA((N_LON,)),
+        ],
         compiler_params=pltpu.CompilerParams(vmem_limit_bytes=VMEM),
         name="spread",
-    )(grid, stencil, weight)
+    )(lon, grid, stencil, weight, owner, slot)
 
 
 def table_kernel(order_ref, norm_ref, sine_ref, logcos_ref, high_ref, low_ref, ring):
@@ -215,32 +256,41 @@
     )(order, norm, sine, logcos)
 
 
-def fourier_kernel(
-    key_ref,
-    south_ref,
-    tiles_ref,
-    real_high,
-    real_low,
-    mixed_high,
-    mixed_low,
-    dense_ref,
-    out_ref,
-    *scratch,
-):
+def fourier_kernel(south_ref, *refs):
+    chunks = refs[:N_LON]
+    real_high, real_low, mixed_high, mixed_low, extra_ref = refs[N_LON : N_LON + 5]
+    bands = refs[N_LON + 5 : N_LON + 8]
+    out_ref = refs[N_LON + 8]
+    scratch = refs[N_LON + 9 :]
     sums = scratch[:CHAINS]
-    c_high, c_low = scratch[CHAINS:]
-    per_chain = N_LON * TILES // CHAINS
+    c_high, c_low, tiles, keys, dense_ref, sems = scratch[CHAINS:]
+    loads = []
+    for k in range(N_LON):
+        loads.append(pltpu.make_async_copy(chunks[k], tiles.at[k], sems.at[k]))
+        loads.append(
+            pltpu.make_async_copy(
+                chunks[k].at[pl.ds(TILES, 8), :], keys.at[k], sems.at[N_LON + k]
+            )
+        )
+    for copy in loads:
+        copy.start()
     for chain in sums:
         chain[...] = jnp.zeros(chain.shape, f32)
-
-    def scatter(t, _):
-        for c, chain in enumerate(sums):
-            at = c * per_chain + t
-            slot = key_ref[at]
-            chain[pl.ds(slot, 1), :] = chain[pl.ds(slot, 1), :] + tiles_ref[pl.ds(at, 1), :]
-        return 0
-
-    lax.fori_loop(0, per_chain, scatter, 0, unroll=4)
+    for copy in loads:
+        copy.wait()
+    share = N_LON // CHAINS
+    for part in range(share):
+        for line, count in ((0, TILE), (1, TILES - TILE)):
+
+            def scatter(t, _):
+                for c, chain in enumerate(sums):
+                    k = c * share + part
+                    slot = keys[k, line, t].astype(jnp.int32)
+                    tile = tiles[k, pl.ds(line * TILE + t, 1), :]
+                    chain[pl.ds(slot, 1), :] = chain[pl.ds(slot, 1), :] + tile
+                return 0
+
+            lax.fori_loop(0, count, scatter, 0, unroll=4)
     south = south_ref[0]
     root = math.sqrt(0.5)
     blank = jnp.zeros((16, NLON), bf16)
@@ -286,52 +336,71 @@
         return 0
 
     lax.fori_loop(0, 15, butterfly, 0)
+    stores = [
+        pltpu.make_async_copy(
+            dense_ref.at[pl.ds(i * DENSE, DENSE), :], bands[i], sems.at[2 * N_LON + i]
+        )
+        for i in range(3)
+    ]
+    for copy in stores:
+        copy.start()
+    extra = extra_ref[...]
 
     def emit(m1, block):
+        block = jnp.concatenate([block[:, :TILE], block[:, TILE:] + extra], axis=1)
         for h in range(N_LAT):
             for g in range(GROUPS):
                 start = h * WAVE_DEV + 2 * g
                 out_ref[h * 8 + m1, g, :, :] = block[start : start + 2, :]
 
+    def transform(ch, cl, wh, wl):
+        rows = wh.shape[0]
+        both = dot(jnp.concatenate([wh, wl], axis=0), ch, NT)
+        return both[:rows] + (both[rows:] + dot(wh, cl, NT))
+
     for i, m1 in enumerate((0, 4)):
-        ch = c_high[:, i * BAND : (i + 1) * BAND]
-        cl = c_low[:, i * BAND : (i + 1) * BAND]
-        wh, wl = real_high[i], real_low[i]
-        emit(m1, dot(wh, ch, NT) + (dot(wh, cl, NT) + dot(wl, ch, NT)))
+        at = slice(i * BAND, (i + 1) * BAND)
+        emit(m1, transform(c_high[:, at], c_low[:, at], real_high[i], real_low[i]))
     for q in (1, 2, 3):
-        ch = c_high[:, 2 * q * BAND : (2 * q + 2) * BAND]
-        cl = c_low[:, 2 * q * BAND : (2 * q + 2) * BAND]
-        for half, m1 in enumerate((q, 8 - q)):
-            wh = mixed_high[q - 1, half * 160 : half * 160 + 160, :]
-            wl = mixed_low[q - 1, half * 160 : half * 160 + 160, :]
-            emit(m1, dot(wh, ch, NT) + (dot(wh, cl, NT) + dot(wl, ch, NT)))
-
-
-def fourier_call(keys, south, tiles, tables):
+        at = slice(2 * q * BAND, (2 * q + 2) * BAND)
+        pair = transform(c_high[:, at], c_low[:, at], mixed_high[q - 1], mixed_low[q - 1])
+        emit(q, pair[:160])
+        emit(8 - q, pair[160:])
+    for copy in stores:
+        copy.wait()
+
+
+def fourier_call(south, chunks, tables, extra):
     vmem = pl.BlockSpec(memory_space=pltpu.VMEM)
     smem = pl.BlockSpec(memory_space=pltpu.SMEM)
     return pl.pallas_call(
         fourier_kernel,
-        in_specs=[smem, smem] + [vmem] * 5,
-        out_specs=(vmem, vmem),
-        out_shape=(
-            jax.ShapeDtypeStruct((3 * DENSE, TILE), f32),
-            jax.ShapeDtypeStruct((N_LAT * N_LON, GROUPS, 2, 256), f32),
-        ),
+        in_specs=[smem] + [pl.BlockSpec(memory_space=pl.ANY)] * N_LON + [vmem] * 5,
+        out_specs=[pl.BlockSpec(memory_space=pl.ANY)] * 3 + [vmem],
+        out_shape=[jax.ShapeDtypeStruct((DENSE, TILE), f32)] * 3
+        + [jax.ShapeDtypeStruct((N_LAT * N_LON, GROUPS, 2, 256), f32)],
         scratch_shapes=[pltpu.VMEM((3 * DENSE, TILE), f32)] * CHAINS
-        + [pltpu.VMEM((256, NLON), bf16)] * 2,
+        + [pltpu.VMEM((256, NLON), bf16)] * 2
+        + [
+            pltpu.VMEM((N_LON, CHUNK, TILE), f32),
+            pltpu.SMEM((N_LON, 8, TILE), f32),
+            pltpu.VMEM((3 * DENSE, TILE), f32),
+            pltpu.SemaphoreType.DMA((2 * N_LON + 3,)),
+        ],
         compiler_params=pltpu.CompilerParams(vmem_limit_bytes=VMEM),
         name="scatter_fourier",
-    )(keys, south, tiles, *tables)
+    )(south, *chunks, *tables, extra)
 
 
 def legendre_kernel(
-    wave_ref, coeff_ref, high_ref, low_ref, mix_ref, weight_ref, rate_ref, out_ref, north, south
+    wave_ref, coeff_ref, high_ref, low_ref, weight_ref, rate_ref, out_ref, north, south, blend
 ):
     weight = weight_ref[...]
     row16 = lax.broadcasted_iota(jnp.int32, (16, HALF), 0)
     first_level = (row16 // 2) % 2 == 0
-    dn, xn, ds, xs = (mix_ref[i] for i in range(4))
+    is_first = row16 % 2 == 0
+    lane128 = lax.broadcasted_iota(jnp.int32, (16, TILE), 1)
+    is_blend = lane128 >= TILE - 16
 
     def mixed(values, own, cross):
         ahead = pltpu.roll(values, 14, 0)
@@ -340,22 +409,35 @@
         return values + own * values + cross * other
 
     pad = jnp.zeros((16, TILE), f32)
+    north[...] = jnp.zeros(north.shape, f32)
+    south[...] = jnp.zeros(south.shape, f32)
+    blend[...] = jnp.zeros(blend.shape, f32)
     for g in range(GROUPS):
-        north[...] = jnp.zeros(north.shape, f32)
-        south[...] = jnp.zeros(south.shape, f32)
         for a in range(N_LAT):
             total, place = (north, a) if a < 8 else (south, 15 - a)
             piece = jnp.concatenate([coeff_ref[a * 8 + f, g, :, :] for f in range(FL)], axis=0)
-            piece = jnp.concatenate([piece, pad], axis=1)
+            last = piece[:, TILE:]
+            piece = jnp.concatenate([piece[:, :TILE], jnp.where(is_blend, 0.0, last), pad], axis=1)
             offset = ROWS * place + 48
             base = offset // TILE * TILE
-            total[:, base : base + 384] += pltpu.roll(piece, offset % TILE, 1)
-        extra_n = north[:, 768:896]
-        extra_s = south[:, 768:896]
-        north[:, 640:768] += pltpu.roll(extra_s, 48, 1)
-        south[:, 640:768] += pltpu.roll(extra_n, 48, 1)
-        full_n = mixed(north[:, 128:768], dn, xn)
-        full_s = mixed(south[:, 128:768], ds, xs)
+            total[g, :, base : base + 384] += pltpu.roll(piece, offset % TILE, 1)
+            offset = ROWS * place + 16 * g
+            base = offset // TILE * TILE
+            last = pltpu.roll(jnp.where(is_blend, last, 0.0), (offset % TILE + 16) % TILE, 1)
+            blend[a // 8, :, base : base + TILE] += last
+    blends = []
+    for side in range(2):
+        both = blend[side]
+        blends.append(jnp.where(is_first, both, pltpu.roll(both, 1, 0)))
+        blends.append(jnp.where(is_first, pltpu.roll(both, 15, 0), both))
+    dn, xn, ds, xs = blends
+    for g in range(GROUPS):
+        extra_n = north[g, :, 768:896]
+        extra_s = south[g, :, 768:896]
+        north[g, :, 640:768] += pltpu.roll(extra_s, 48, 1)
+        south[g, :, 640:768] += pltpu.roll(extra_n, 48, 1)
+        full_n = mixed(north[g, :, 128:768], dn, xn)
+        full_s = mixed(south[g, :, 128:768], ds, xs)
         pad_len = DEG_PAD[g]
         wave = wave_ref[0] + 128 * g
         factor = jnp.where(wave == 0, 1.0, 2.0).astype(f32)
@@ -364,18 +446,20 @@
         results = []
         for parity, folded in enumerate((full_n + full_s, full_n - full_s)):
             folded = folded * weight
-            fh, fl = split(folded)
+            both = stacked_parts(folded)
             start = DEG_BASE[g] + parity * pad_len
             ph = high_ref[start : start + pad_len, :]
             pw = low_ref[start : start + pad_len, :]
-            spectrum = dot(fh, ph, NT) + (dot(fl, ph, NT) + dot(fh, pw, NT))
+            main = dot(both, ph, NT)
+            spectrum = main[:16] + (main[16:] + dot(both[:16], pw, NT))
             degree = wave + parity + 2 * lane
             degree_f = degree.astype(f32)
             ratio = rate * (degree_f * (degree_f + 1.0) / float(NM * (NM + 1)))
             damped = spectrum * (-ratio / (1.0 + ratio)) * factor
             damped = jnp.where(degree < NM, damped, 0.0)
-            dh, dl = split(damped)
-            results.append(dot(dh, ph, NN) + (dot(dl, ph, NN) + dot(dh, pw, NN)))
+            both = stacked_parts(damped)
+            main = dot(both, ph, NN)
+            results.append(main[:16] + (main[16:] + dot(both[:16], pw, NN)))
         for a in range(N_LAT):
             place = a if a < 8 else 15 - a
             offset = ROWS * place
@@ -391,33 +475,22 @@
                 out_ref[a * 8 + f, g, :, :] = piece[2 * f : 2 * f + 2, :TILE]
 
 
-def legendre_call(wave, coeff, high, low, mix, weight, rate):
+def legendre_call(wave, coeff, high, low, weight, rate):
     vmem = pl.BlockSpec(memory_space=pltpu.VMEM)
     smem = pl.BlockSpec(memory_space=pltpu.SMEM)
     return pl.pallas_call(
         legendre_kernel,
-        in_specs=[smem] + [vmem] * 6,
+        in_specs=[smem] + [vmem] * 5,
         out_specs=vmem,
         out_shape=jax.ShapeDtypeStruct((N_LAT * N_LON, GROUPS, 2, TILE), f32),
-        scratch_shapes=[pltpu.VMEM((16, 896), f32)] * 2,
+        scratch_shapes=[pltpu.VMEM((GROUPS, 16, 896), f32)] * 2
+        + [pltpu.VMEM((2, 16, HALF), f32)],
         compiler_params=pltpu.CompilerParams(vmem_limit_bytes=VMEM),
         name="legendre",
-    )(wave, coeff, high, low, mix, weight, rate)
-
-
-def inverse_kernel(
-    back_ref,
-    real_high,
-    real_low,
-    mixed_high,
-    mixed_low,
-    own_ref,
-    other_ref,
-    mix_ref,
-    out_ref,
-    waves,
-    synth,
-):
+    )(wave, coeff, high, low, weight, rate)
+
+
+def synthesis_kernel(back_ref, real_high, real_low, mixed_high, mixed_low, synth, waves):
     for m1 in range(8):
         for h in range(N_LAT):
             for g in range(GROUPS):
@@ -426,8 +499,9 @@
 
     def transform(parts, wh, wl):
         stacked = jnp.concatenate([waves[m1 * 160 : m1 * 160 + 160, :] for m1 in parts], axis=0)
-        ah, al = split(stacked.T[:ROWS, :])
-        return dot(ah, wh, NN) + (dot(al, wh, NN) + dot(ah, wl, NN))
+        both = stacked_parts(stacked.T[:ROWS, :])
+        main = dot(both, wh, NN)
+        return main[:ROWS] + (main[ROWS:] + dot(both[:ROWS], wl, NN))
 
     for i, m1 in enumerate((0, 4)):
         synth[:, i * BAND : (i + 1) * BAND] = transform((m1,), real_high[i], real_low[i])
@@ -435,6 +509,26 @@
         synth[:, 2 * q * BAND : (2 * q + 2) * BAND] = transform(
             (q, 8 - q), mixed_high[q - 1], mixed_low[q - 1]
         )
+
+
+def synthesis_call(back, tables):
+    vmem = pl.BlockSpec(memory_space=pltpu.VMEM)
+    return pl.pallas_call(
+        synthesis_kernel,
+        in_specs=[vmem] * 5,
+        out_specs=vmem,
+        out_shape=jax.ShapeDtypeStruct((ROWS, NLON), f32),
+        scratch_shapes=[pltpu.VMEM((8 * 160, TILE), f32)],
+        compiler_params=pltpu.CompilerParams(vmem_limit_bytes=VMEM),
+        cost_estimate=pl.CostEstimate(
+            flops=6 * 80 * 860_160, bytes_accessed=8_000_000, transcendentals=0
+        ),
+        name="wave_synthesis",
+    )(back, *tables)
+
+
+def combine_kernel(lon_ref, synth, own_ref, other_ref, mix_ref, *rest):
+    outs, (out_ref, sems) = rest[:N_LON], rest[N_LON:]
     root = math.sqrt(0.5)
 
     def combine(chunk, _):
@@ -464,23 +558,52 @@
         return 0
 
     lax.fori_loop(0, ROWS // 16, combine, 0)
-
-
-def inverse_call(back, tables, own, other, mix):
+    exchange = [
+        pltpu.make_async_copy(
+            out_ref.at[pl.ds(pl.multiple_of((lon_ref[0] ^ k) * TILES, 8), TILES), :],
+            outs[k],
+            sems.at[k],
+        )
+        for k in range(N_LON)
+    ]
+    for copy in exchange:
+        copy.start()
+    for copy in exchange:
+        copy.wait()
+
+
+def combine_call(lon, synth, own, other, mix):
     vmem = pl.BlockSpec(memory_space=pltpu.VMEM)
+    smem = pl.BlockSpec(memory_space=pltpu.SMEM)
     return pl.pallas_call(
-        inverse_kernel,
-        in_specs=[vmem] * 8,
-        out_specs=vmem,
-        out_shape=jax.ShapeDtypeStruct((DENSE, TILE), f32),
-        scratch_shapes=[pltpu.VMEM((8 * 160, TILE), f32), pltpu.VMEM((ROWS, NLON), f32)],
+        combine_kernel,
+        in_specs=[smem] + [vmem] * 4,
+        out_specs=[pl.BlockSpec(memory_space=pl.ANY)] * N_LON,
+        out_shape=[jax.ShapeDtypeStruct((TILES, TILE), f32)] * N_LON,
+        scratch_shapes=[
+            pltpu.VMEM((DENSE, TILE), f32),
+            pltpu.SemaphoreType.DMA((N_LON,)),
+        ],
         compiler_params=pltpu.CompilerParams(vmem_limit_bytes=VMEM),
-        name="inverse_fourier",
-    )(back, *tables, own, other, mix)
-
-
-def place_kernel(south_ref, rows_ref, out_ref):
+        name="combine",
+    )(lon, synth, own, other, mix)
+
+
+def place_kernel(south_ref, lon_ref, *rest):
+    chunks, (out_ref, rows_ref, sems) = rest[:N_LON], rest[N_LON:]
     south = south_ref[0]
+    loads = [
+        pltpu.make_async_copy(
+            chunks[k],
+            rows_ref.at[pl.ds(pl.multiple_of((lon_ref[0] ^ k) * TILES, 8), TILES), :],
+            sems.at[k],
+        )
+        for k in range(N_LON)
+    ]
+    for copy in loads:
+        copy.start()
+    for copy in loads:
+        copy.wait()
 
     def place(i, _):
         target = jnp.where(south == 1, ROWS - 1 - i, i)
@@ -493,17 +616,21 @@
     lax.fori_loop(0, ROWS, place, 0, unroll=8)
 
 
-def place_call(south, rows):
+def place_call(south, lon, chunks):
     vmem = pl.BlockSpec(memory_space=pltpu.VMEM)
     smem = pl.BlockSpec(memory_space=pltpu.SMEM)
     return pl.pallas_call(
         place_kernel,
-        in_specs=[smem, vmem],
+        in_specs=[smem, smem] + [pl.BlockSpec(memory_space=pl.ANY)] * N_LON,
         out_specs=vmem,
         out_shape=jax.ShapeDtypeStruct((ROWS, FL, BAND), f32),
+        scratch_shapes=[
+            pltpu.VMEM((FL * TILES, TILE), f32),
+            pltpu.SemaphoreType.DMA((N_LON,)),
+        ],
         compiler_params=pltpu.CompilerParams(vmem_limit_bytes=VMEM),
         name="place_rows",
-    )(south, rows)
+    )(south, lon, *chunks)
 
 
 def local(
@@ -515,42 +642,16 @@
     south = is_south.astype(jnp.int32).reshape(1)
     wave = (lon_here + 8 * lat_here).astype(jnp.int32)
 
-    owners = tile_owner.reshape(TILES)
-    slots = tile_slot.reshape(TILES)
-    dest_lat = owners // N_LON
-    rows = slots // TPR
-    rows = jnp.where(dest_lat >= N_LAT // 2, ROWS - 1 - rows, rows)
-    columns = (owners % N_LON) * TPR + slots % TPR
-    keys = ((dest_lat - lat_here + 1) * (N_LON * TPR) + columns) * ROWS + rows
-    keys = lax.all_gather(keys, "lon", tiled=True)
-
     mix = vertical_offset.reshape(ROWS, 16)
     mix = jnp.where(is_south, jnp.flip(mix, 0), mix).T
-    mix_all = lax.all_gather(mix, "lat")
-    half = N_LAT // 2
-    mix_north = mix_all[:half].transpose(1, 0, 2).reshape(16, HALF)
-    mix_south = jnp.flip(mix_all[half:], 0).transpose(1, 0, 2).reshape(16, HALF)
-    own_ids = [(f // 2) * 4 + (f % 2) * 2 + f % 2 for f in range(FL)]
-    cross_ids = [(f // 2) * 4 + (1 - f % 2) * 2 + f % 2 for f in range(FL)]
-
-    def picked(table, ids):
-        return jnp.stack([table[i] for i in ids for _ in range(2)], axis=0)
-
-    mix_waves = jnp.stack(
-        [
-            picked(mix_north, own_ids),
-            picked(mix_north, cross_ids),
-            picked(mix_south, own_ids),
-            picked(mix_south, cross_ids),
-        ]
-    )
     level = lon_here % 2
     field = lon_here // 2
     own_row = lax.dynamic_index_in_dim(mix, field * 4 + level * 3, 0, False)
     cross_row = lax.dynamic_index_in_dim(mix, field * 4 + (1 - level) * 2 + level, 0, False)
-    mix_grid = jnp.broadcast_to(
-        jnp.stack([own_row, cross_row])[:, :, None], (2, ROWS, TILE)
-    )
+    blend = jnp.stack([own_row, cross_row])
+    mix_grid = jnp.broadcast_to(blend[:, :, None], (2, ROWS, TILE))
+    extra = blend.reshape(2, GROUPS, 16).transpose(1, 0, 2).reshape(WAVE_DEV, 16)
+    extra = jnp.pad(jnp.tile(extra, (N_LAT, 1)), ((0, 0), (TILE - 16, 0)))
 
     latitude = 0.5 * math.pi - math.pi * (np.arange(HALF) + 0.5) / NLAT
     sine = jnp.asarray(np.sin(latitude)[None, :], f32)
@@ -568,21 +669,39 @@
     real, mixed = wave_tables()
     tables = tuple(jnp.asarray(part) for part in two_parts(real) + two_parts(mixed))
 
-    spread = spread_call(adjoint_grid, stencil, interp_weight)
-    tiles = lax.all_to_all(spread, "lon", 0, 0, tiled=True)
+    lon = lon_here.astype(jnp.int32).reshape(1)
+
+    def exchanged(chunks):
+        return [chunks[0]] + [
+            lax.ppermute(chunks[k], "lon", [(i, i ^ k) for i in range(N_LON)])
+            for k in range(1, N_LON)
+        ]
+
+    chunks = exchanged(spread_call(
+        jnp.stack([lon_here, lat_here]).astype(jnp.int32),
+        adjoint_grid,
+        stencil,
+        interp_weight,
+        tile_owner.reshape(1, TILES),
+        tile_slot.reshape(1, TILES),
+    ))
     high, low = table_call(order, norm, sine, logcos)
-    dense, coeff = fourier_call(keys, south, tiles, tables)
-    dense = dense.reshape(3, DENSE, TILE)
-    below = lax.ppermute(dense[0], "lat", [(i + 1, i) for i in range(N_LAT - 1)])
-    above = lax.ppermute(dense[2], "lat", [(i, i + 1) for i in range(N_LAT - 1)])
+    tables, high, low, extra, rate, mix_grid = lax.optimization_barrier(
+        (tables, high, low, extra, rate, mix_grid)
+    )
+    dense_below, dense_here, dense_above, coeff = fourier_call(south, chunks, tables, extra)
     coeff = lax.all_to_all(coeff, ("lat", "lon"), 0, 0, tiled=True)
-    back = legendre_call(wave.reshape(1), coeff, high, low, mix_waves, weight, rate)
-    departed = dense[1] + below + above
+    dense_below, dense_above, coeff = lax.optimization_barrier((dense_below, dense_above, coeff))
+    below = lax.ppermute(dense_below, "lat", [(i + 1, i) for i in range(N_LAT - 1)])
+    above = lax.ppermute(dense_above, "lat", [(i, i + 1) for i in range(N_LAT - 1)])
+    back = legendre_call(wave.reshape(1), coeff, high, low, weight, rate)
+    back = lax.all_to_all(back, ("lat", "lon"), 0, 0, tiled=True)
+    dense_here, back = lax.optimization_barrier((dense_here, back))
+    departed = dense_here + below + above
     other = lax.ppermute(departed, "lon", [(i, i ^ 1) for i in range(N_LON)])
-    back = lax.all_to_all(back, ("lat", "lon"), 0, 0, tiled=True)
-    result = inverse_call(back, tables, departed, other, mix_grid)
-    result = lax.all_to_all(result, "lon", 0, 0, tiled=True)
-    return place_call(south, result)
+    synth = synthesis_call(back, tables)
+    result = exchanged(combine_call(lon, synth, departed, other, mix_grid))
+    return place_call(south, lon, result)
 
 
 def solution(mesh):

time: 188 us -> 153 us (0.81)
  blocking collectives: 70.6 us -> 55.6 us
  starting transfers between devices: 32.4 us -> 24.8 us
  waiting for transfers between devices: 18.2 us -> 10.9 us
  local copies, waits for them, and re-layouts: 12.3 us -> 7.83 us
    all_to_all x1 -> x2, blocking collectives: 19.9 us -> 55.6 us  [the longest x1 31 us: local(): coeff = lax.all_to_all(coeff, ('lat', 'lon'), 0, 0, tiled=True)]
    all_gather x1 -> x0, blocking collectives: 35.5 us -> none  [local(): mix_all = lax.all_gather(mix, 'lat')]
    all_to_all x3 -> x0, starting transfers between devices: 24.9 us -> none  [the longest x1 13.4 us: local(): coeff = lax.all_to_all(coeff, ('lat', 'lon'), 0, 0, tiled=True)]
    all_to_all x3 -> x0, waiting for transfers between devices: 18.2 us -> none  [the longest x1 14.7 us: local(): back = lax.all_to_all(back, ('lat', 'lon'), 0, 0, tiled=True)]
    ppermute x2 -> x16, starting transfers between devices: 6.38 us -> 24.2 us  [the longest x14 18.9 us: exchanged(): lax.ppermute(chunks[k], 'lon', [(i, i ^ k) for i in range(N_LON)])]
    unnamed x1 -> x0, blocking collectives: 15.3 us -> none
    ppermute x2 -> x16, waiting for transfers between devices: 0.01 us -> 10.9 us  [the longest x14 10.9 us: exchanged(): lax.ppermute(chunks[k], 'lon', [(i, i ^ k) for i in range(N_LON)])]
    slice x38 -> x0, local copies, waits for them, and re-layouts: 5.22 us -> none  [the longest x34 2.6 us: picked(): return jnp.stack([table[i] for i in ids for _ in range(2)], axis=0)]
  transfers between devices with their start and end apart: 6 -> 17, of which waited for: 2 -> 5; matrix products, arithmetic and copies ran while one was open for 5% -> 4% of each run, Pallas kernels for 11% -> 14%
where the time goes in v2:
time: 153 us
  blocking collectives  55.6 us (36%)
  Pallas kernels  52.2 us (34%)
  starting transfers between devices  24.8 us (16%)
  waiting for transfers between devices  10.9 us (7%)
  local copies, waits for them, and re-layouts  7.83 us (5%)
    all_to_all x1, blocking collectives, local(): coeff = lax.all_to_all(coeff, ('lat', 'lon'), 0, 0, tiled=True)  31 us
    all_to_all x1, blocking collectives, local(): back = lax.all_to_all(back, ('lat', 'lon'), 0, 0, tiled=True)  24.6 us
    ppermute x14, starting transfers between devices, exchanged(): lax.ppermute(chunks[k], 'lon', [(i, i ^ k) for i in range(N_LON)])  18.9 us
    pallas_call x1, Pallas kernels, fourier_call(): pl.pallas_call(fourier_kernel, in_specs=[smem] + [pl.BlockSpec(memory_spa...  13.1 us
    pallas_call x1, Pallas kernels, spread_call(): pl.pallas_call(spread_kernel, grid=(ROWS // block,), in_specs=[pl.BlockSp...  11.4 us
    ppermute x14, waiting for transfers between devices, exchanged(): lax.ppermute(chunks[k], 'lon', [(i, i ^ k) for i in range(N_LON)])  10.9 us
    pallas_call x1, Pallas kernels, legendre_call(): pl.pallas_call(legendre_kernel, in_specs=[smem] + [vmem] * 5, out_specs=v...  8.92 us
    pallas_call x1, Pallas kernels, table_call(): pl.pallas_call(table_kernel, out_shape=(shape, shape), scratch_shapes=[pl...  8.82 us
  transfers between devices with their start and end apart: 17, of which 5 were waited for; matrix products, arithmetic and copies ran while one was open for 4% of the time, Pallas kernels for 14%

profile of v2, /device:TPU:1, one launch (start us, length us, event | category | flops | bytes accessed | tf_op | source)
XLA Modules:
  0.0 152.6 jit_solution(4869493444808290340)
XLA Ops:
  0.7 11.4 %spread.1 = (f32[248,128]{1,0:T(8,128)}, f32[248,128]{1,0:T(8,128)}, f32[248,128]{1,0:T(8,128)}, f32[248,128]{1,0:T(8,128)}, f32[248,128]{1,0:T(8,128)}, /*index...) custom-call(s32[2]{0:T(128)} %pad_add_fusion.lon_ref, f32[80,8,384]{2,1,0:T(8,128)} %grid_ref.1, ...), custom_call_target="tpu_custom_call" | custom-call | tf_op jit(solution)/shard_map/spread/pallas_call | solution.py:157
  12.1 1.5 collective-permute-start
  13.6 1.4 collective-permute-start.1
  15.3 3.0 %collective-permute-start.3 = (f32[248,128]{1,0:T(8,128)}, f32[248,128]{1,0:T(8,128)S(1)}, u32[]{:S(2)}, u32[]{:S(2)}) collective-permute-start(f32[248,128]{1,0:T(8,128)} %get-tuple-element.57), channel_id=1, source_target_pairs={{0,4},{1,5},{2,6},{3,7},{4,0},{5,1},{6,2},{7,3},{8,12},{9,13},{10,... | collective-permute-start | bytes 380936 | tf_op jit(solution)/shard_map/ppermute | solution.py:676
  18.9 2.9 %collective-permute-start.5 = (f32[248,128]{1,0:T(8,128)}, f32[248,128]{1,0:T(8,128)S(1)}, u32[]{:S(2)}, u32[]{:S(2)}) collective-permute-start(f32[248,128]{1,0:T(8,128)} %get-tuple-element.59), channel_id=1, source_target_pairs={{0,6},{1,7},{2,4},{3,5},{4,2},{5,3},{6,0},{7,1},{8,14},{9,15},{10,... | collective-permute-start | bytes 380936 | tf_op jit(solution)/shard_map/ppermute | solution.py:676
  26.6 8.8 %legendre_table.1 = (bf16[2304,640]{1,0:T(8,128)(2,1)}, bf16[2304,640]{1,0:T(8,128)(2,1)}) custom-call(f32[8,128]{1,0:T(8,128)} %broadcast_in_dim.11.order_ref, f32[8,128]{1,0:T(8,128)} %broadcast_in_dim.13.norm_ref, f32[1,640]{1,0:T(1,128)} %constant.149.clone.sine_ref, f32[1,640]{1,0:T(1,128)} %constant.150.clone.logcos_ref), custom_call_target="tpu_custom_call" | custom-call | flops 65536000 | bytes 6000000 | tf_op jit(solution)/shard_map/legendre_table/pallas_call | solution.py:247
  37.7 13.1 %scatter_fourier.1 = (f32[1920,128]{1,0:T(8,128)}, f32[1920,128]{1,0:T(8,128)}, f32[1920,128]{1,0:T(8,128)}, f32[128,5,2,256]{3,2,1,0:T(2,128)}) custom-call(s32[1]{0:T(128)} %bitcast.south_ref, f32[248,128]{1,0:T(8,128)} %get-tuple-element.53.refs_0_, f32[248,128]{1,0:T(8,128)} %copy-done.4, f32[248,128]{1,0:T(8,128)} %copy-done.5, f32[248,128]{1,0:T(8,128)} %copy-done.6, ...), custom_call_target="tpu_custom_call" | custom-call | tf_op jit(solution)/shard_map/scatter_fourier/pallas_call | solution.py:376
  50.9 31.0 %all_to_all.10.coeff_ref = f32[128,5,2,256]{3,2,1,0:T(2,128)} all-to-all(f32[128,5,2,256]{3,2,1,0:T(2,128)} %get-tuple-element.71), channel_id=1, replica_groups=mesh['lat'=16,'lon'=8] {'lat','lon'}, dimensions={0} | all-to-all | bytes 2621440 | tf_op jit(solution)/shard_map/all_to_all | solution.py:693
  81.9 1.3 collective-permute-start.7
  83.2 4.0 %collective-permute-start.8 = (f32[1920,128]{1,0:T(8,128)S(1)}, f32[1920,128]{1,0:T(8,128)S(1)}, u32[]{:S(2)}, u32[]{:S(2)}) collective-permute-start(f32[1920,128]{1,0:T(8,128)S(1)} %copy-done.20), channel_id=1, source_target_pairs={{0,8},{8,16},{16,24},{24,32},{32,40},{40,48},{48,56},{56,64},{64,7... | collective-permute-start | bytes 2949128 | tf_op jit(solution)/shard_map/ppermute | solution.py:696
  87.2 8.9 %legendre.1 = f32[128,5,2,128]{3,2,1,0:T(2,128)} custom-call(s32[1]{0:T(128)} %bitcast.10.wave_ref, f32[128,5,2,256]{3,2,1,0:T(2,128)} %all_to_all.10.coeff_ref, bf16[2304,640]{1,0:T(8,128)(2,1)} %get-tuple-element.73.high_ref, bf16[2304,640]{1,0:T(8,128)(2,1)} %get-tuple-element.74.low_ref, f32[1,640]{1,0:T(1,128)} %constant.151.clone.weight_ref, ...), custom_call_target="tpu_custom_call" | custom-call | tf_op jit(solution)/shard_map/legendre/pallas_call | solution.py:481
  96.1 24.6 %all_to_all.11.back_ref = f32[128,5,2,128]{3,2,1,0:T(2,128)} all-to-all(f32[128,5,2,128]{3,2,1,0:T(2,128)} %legendre.1), channel_id=1, replica_groups=mesh['lat'=16,'lon'=8] {'lat','lon'}, dimensions={0} | all-to-all | bytes 1310720 | tf_op jit(solution)/shard_map/all_to_all | solution.py:698
  121.6 4.2 %wave_synthesis.1.synth = f32[80,3072]{1,0:T(8,128)} custom-call(f32[128,5,2,128]{3,2,1,0:T(2,128)} %all_to_all.11.back_ref, bf16[2,160,384]{2,1,0:T(8,128)(2,1)} %constant.153.clone.refs_8_.real_high, bf16[2,160,384]{2,1,0:T(8,128)(2,1)} %constant.154.clone.refs_9_.real_low, bf16[3,320,768]{2,1,0:T(8,128)(2,1)} %constant.155.clone.refs_10_.mixed_high, ...), custom_call_target="tpu_custom_call" | custom-call | flops 412876800 | bytes 8000000 | tf_op jit(solution)/shard_map/wave_synthesis/pallas_call | solution.py:516
  126.8 3.1 %combine.1 = (f32[240,128]{1,0:T(8,128)}, f32[240,128]{1,0:T(8,128)}, f32[240,128]{1,0:T(8,128)}, f32[240,128]{1,0:T(8,128)}, f32[240,128]{1,0:T(8,128)}, /*inde...) custom-call(s32[1]{0:T(128)} %bitcast.1.lon_ref, f32[80,3072]{1,0:T(8,128)} %wave_synthesis.1.synth, ...), custom_call_target="tpu_custom_call" | custom-call | tf_op jit(solution)/shard_map/combine/pallas_call | solution.py:578
  130.1 1.1 collective-permute-start.11
  132.1 1.6 %collective-permute-start.13 = (f32[240,128]{1,0:T(8,128)}, f32[240,128]{1,0:T(8,128)S(1)}, u32[]{:S(2)}, u32[]{:S(2)}) collective-permute-start(f32[240,128]{1,0:T(8,128)} %get-tuple-element.85), channel_id=1, source_target_pairs={{0,4},{1,5},{2,6},{3,7},{4,0},{5,1},{6,2},{7,3},{8,12},{9,13},{10,... | collective-permute-start | bytes 368648 | tf_op jit(solution)/shard_map/ppermute | solution.py:676
  133.7 1.3 collective-permute-start.14
  135.1 1.6 %collective-permute-start.15 = (f32[240,128]{1,0:T(8,128)}, f32[240,128]{1,0:T(8,128)S(1)}, u32[]{:S(2)}, u32[]{:S(2)}) collective-permute-start(f32[240,128]{1,0:T(8,128)} %get-tuple-element.87), channel_id=1, source_target_pairs={{0,6},{1,7},{2,4},{3,5},{4,2},{5,3},{6,0},{7,1},{8,14},{9,15},{10,... | collective-permute-start | bytes 368648 | tf_op jit(solution)/shard_map/ppermute | solution.py:676
  136.7 1.7 %collective-permute-start.16 = (f32[240,128]{1,0:T(8,128)}, f32[240,128]{1,0:T(8,128)S(1)}, u32[]{:S(2)}, u32[]{:S(2)}) collective-permute-start(f32[240,128]{1,0:T(8,128)} %get-tuple-element.88), channel_id=1, source_target_pairs={{0,7},{1,6},{2,5},{3,4},{4,3},{5,2},{6,1},{7,0},{8,15},{9,14},{10,... | collective-permute-start | bytes 368648 | tf_op jit(solution)/shard_map/ppermute | solution.py:676
  138.8 2.5 %collective-permute-done.13.rest_4_ = f32[240,128]{1,0:T(8,128)S(1)} collective-permute-done((f32[240,128]{1,0:T(8,128)}, f32[240,128]{1,0:T(8,128)S(1)}, u32[]{:S(2)}, u32[]{:S(2)}) %collective-permute-start.13) | collective-permute-done | bytes 122912 | tf_op jit(solution)/shard_map/ppermute | solution.py:676
  141.3 3.3 %collective-permute-done.14.rest_5_ = f32[240,128]{1,0:T(8,128)S(1)} collective-permute-done((f32[240,128]{1,0:T(8,128)}, f32[240,128]{1,0:T(8,128)S(1)}, u32[]{:S(2)}, u32[]{:S(2)}) %collective-permute-start.14) | collective-permute-done | bytes 122912 | tf_op jit(solution)/shard_map/ppermute | solution.py:676
  144.6 1.8 %collective-permute-done.15.rest_6_ = f32[240,128]{1,0:T(8,128)S(1)} collective-permute-done((f32[240,128]{1,0:T(8,128)}, f32[240,128]{1,0:T(8,128)S(1)}, u32[]{:S(2)}, u32[]{:S(2)}) %collective-permute-start.15) | collective-permute-done | bytes 122912 | tf_op jit(solution)/shard_map/ppermute | solution.py:676
  146.4 2.8 %collective-permute-done.16.rest_7_ = f32[240,128]{1,0:T(8,128)S(1)} collective-permute-done((f32[240,128]{1,0:T(8,128)}, f32[240,128]{1,0:T(8,128)S(1)}, u32[]{:S(2)}, u32[]{:S(2)}) %collective-permute-start.16) | collective-permute-done | bytes 122912 | tf_op jit(solution)/shard_map/ppermute | solution.py:676
  149.8 2.6 %place_rows.1 = f32[80,8,384]{2,1,0:T(8,128)} custom-call(s32[1]{0:T(128)} %bitcast.south_ref, s32[1]{0:T(128)} %bitcast.1.lon_ref, f32[240,128]{1,0:T(8,128)} %get-tuple-element.81.rest_0_, f32[240,128]{1,0:T(8,128)} %copy-done.11, f32[240,128]{1,0:T(8,128)} %copy-done.12, f32[240,128]{1,0:T(8,128)} %copy-done.13, f32[240,128]{1,0:T(8,128)} %copy-done.14, ...), custom_call_target="tpu_custom_call" | custom-call | tf_op jit(solution)/shard_map/place_rows/pallas_call | solution.py:622
  (87 shorter events, 12.6 us)
Async XLA Ops:
  0.0 23.9 %copy-start = (f32[8]{0:T(128)S(1)}, f32[8]{0:T(128)}, u32[]{:S(2)}) copy-start(f32[8]{0:T(128)} %param.23) | copy-start | bytes 100
  0.0 18.6 %copy-start.19 = (s32[16]{0:T(128)S(1)}, s32[16]{0:T(128)}, u32[]{:S(2)}) copy-start(s32[16]{0:T(128)} %constant.163) | copy-start | bytes 196
  0.0 18.6 %copy-start.18 = (f32[80,4,2,2]{0,3,2,1:T(2,128)S(1)}, f32[80,4,2,2]{0,3,2,1:T(2,128)}, u32[]{:S(2)}) copy-start(f32[80,4,2,2]{0,3,2,1:T(2,128)} %param.22) | copy-start | bytes 15364
  12.1 6.8 %collective-permute-start = (f32[248,128]{1,0:T(8,128)}, f32[248,128]{1,0:T(8,128)S(1)}, u32[]{:S(2)}, u32[]{:S(2)}) collective-permute-start(f32[248,128]{1,0:T(8,128)} %get-tuple-element.54), channel_id=1, source_target_pairs={{0,1},{1,0},{2,3},{3,2},{4,5},{5,4},{6,7},{7,6},{8,9},{9,8},{10,11... | collective-permute-start | bytes 380936 | tf_op jit(solution)/shard_map/ppermute | solution.py:676
  13.6 8.3 %collective-permute-start.1 = (f32[248,128]{1,0:T(8,128)}, f32[248,128]{1,0:T(8,128)S(1)}, u32[]{:S(2)}, u32[]{:S(2)}) collective-permute-start(f32[248,128]{1,0:T(8,128)} %get-tuple-element.55), channel_id=1, source_target_pairs={{0,2},{1,3},{2,0},{3,1},{4,6},{5,7},{6,4},{7,5},{8,10},{9,11},{10,... | collective-permute-start | bytes 380936 | tf_op jit(solution)/shard_map/ppermute | solution.py:676
  15.0 21.8 %collective-permute-start.2 = (f32[248,128]{1,0:T(8,128)}, f32[248,128]{1,0:T(8,128)S(1)}, u32[]{:S(2)}, u32[]{:S(2)}) collective-permute-start(f32[248,128]{1,0:T(8,128)} %get-tuple-element.56), channel_id=1, source_target_pairs={{0,3},{1,2},{2,1},{3,0},{4,7},{5,6},{6,5},{7,4},{8,11},{9,10},{10,... | collective-permute-start | bytes 380936 | tf_op jit(solution)/shard_map/ppermute | solution.py:676
  15.3 21.5 %collective-permute-start.3 = (f32[248,128]{1,0:T(8,128)}, f32[248,128]{1,0:T(8,128)S(1)}, u32[]{:S(2)}, u32[]{:S(2)}) collective-permute-start(f32[248,128]{1,0:T(8,128)} %get-tuple-element.57), channel_id=1, source_target_pairs={{0,4},{1,5},{2,6},{3,7},{4,0},{5,1},{6,2},{7,3},{8,12},{9,13},{10,... | collective-permute-start | bytes 380936 | tf_op jit(solution)/shard_map/ppermute | solution.py:676
  18.3 18.5 %collective-permute-start.4 = (f32[248,128]{1,0:T(8,128)}, f32[248,128]{1,0:T(8,128)S(1)}, u32[]{:S(2)}, u32[]{:S(2)}) collective-permute-start(f32[248,128]{1,0:T(8,128)} %get-tuple-element.58), channel_id=1, source_target_pairs={{0,5},{1,4},{2,7},{3,6},{4,1},{5,0},{6,3},{7,2},{8,13},{9,12},{10,... | collective-permute-start | bytes 380936 | tf_op jit(solution)/shard_map/ppermute | solution.py:676
  18.9 16.5 %copy-start.4 = (f32[248,128]{1,0:T(8,128)}, f32[248,128]{1,0:T(8,128)S(1)}, u32[]{:S(2)}) copy-start(f32[248,128]{1,0:T(8,128)S(1)} %collective-permute-done.refs_1_) | copy-start | bytes 380932
  18.9 17.9 %collective-permute-start.5 = (f32[248,128]{1,0:T(8,128)}, f32[248,128]{1,0:T(8,128)S(1)}, u32[]{:S(2)}, u32[]{:S(2)}) collective-permute-start(f32[248,128]{1,0:T(8,128)} %get-tuple-element.59), channel_id=1, source_target_pairs={{0,6},{1,7},{2,4},{3,5},{4,2},{5,3},{6,0},{7,1},{8,14},{9,15},{10,... | collective-permute-start | bytes 380936 | tf_op jit(solution)/shard_map/ppermute | solution.py:676
  21.9 15.0 %collective-permute-start.6 = (f32[248,128]{1,0:T(8,128)}, f32[248,128]{1,0:T(8,128)S(1)}, u32[]{:S(2)}, u32[]{:S(2)}) collective-permute-start(f32[248,128]{1,0:T(8,128)} %get-tuple-element.60), channel_id=1, source_target_pairs={{0,7},{1,6},{2,5},{3,4},{4,3},{5,2},{6,1},{7,0},{8,15},{9,14},{10,... | collective-permute-start | bytes 380936 | tf_op jit(solution)/shard_map/ppermute | solution.py:676
  50.9 31.0 %copy-start.21 = (f32[1920,128]{1,0:T(8,128)S(1)}, f32[1920,128]{1,0:T(8,128)}, u32[]{:S(2)}) copy-start(f32[1920,128]{1,0:T(8,128)} %get-tuple-element.78) | copy-start | bytes 2949124
  50.9 32.3 %copy-start.20 = (f32[1920,128]{1,0:T(8,128)S(1)}, f32[1920,128]{1,0:T(8,128)}, u32[]{:S(2)}) copy-start(f32[1920,128]{1,0:T(8,128)} %get-tuple-element.79) | copy-start | bytes 2949124
  81.9 38.9 %collective-permute-start.7 = (f32[1920,128]{1,0:T(8,128)S(1)}, f32[1920,128]{1,0:T(8,128)S(1)}, u32[]{:S(2)}, u32[]{:S(2)}) collective-permute-start(f32[1920,128]{1,0:T(8,128)S(1)} %copy-done.21), channel_id=1, source_target_pairs={{8,0},{16,8},{24,16},{32,24},{40,32},{48,40},{56,48},{64,56},{72,6... | collective-permute-start | bytes 2949128 | tf_op jit(solution)/shard_map/ppermute | solution.py:695
  83.2 37.6 %collective-permute-start.8 = (f32[1920,128]{1,0:T(8,128)S(1)}, f32[1920,128]{1,0:T(8,128)S(1)}, u32[]{:S(2)}, u32[]{:S(2)}) collective-permute-start(f32[1920,128]{1,0:T(8,128)S(1)} %copy-done.20), channel_id=1, source_target_pairs={{0,8},{8,16},{16,24},{24,32},{32,40},{40,48},{48,56},{56,64},{64,7... | collective-permute-start | bytes 2949128 | tf_op jit(solution)/shard_map/ppermute | solution.py:696
  96.1 24.6 %copy-start.3 = (f32[1920,128]{1,0:T(8,128)S(1)}, f32[1920,128]{1,0:T(8,128)}, u32[]{:S(2)}) copy-start(f32[1920,128]{1,0:T(8,128)} %get-tuple-element.77) | copy-start | bytes 2949124
  121.0 4.9 %collective-permute-start.9 = (f32[1920,128]{1,0:T(8,128)S(1)}, f32[1920,128]{1,0:T(8,128)S(1)}, u32[]{:S(2)}, u32[]{:S(2)}) collective-permute-start(f32[1920,128]{1,0:T(8,128)S(1)} %add_add_fusion.own_ref), channel_id=1, source_target_pairs={{0,1},{1,0},{2,3},{3,2},{4,5},{5,4},{6,7},{7,6},{8,9},{9,8},{10,11... | collective-permute-start | bytes 2949128 | tf_op jit(solution)/shard_map/ppermute | solution.py:701
  129.9 5.2 %collective-permute-start.10 = (f32[240,128]{1,0:T(8,128)}, f32[240,128]{1,0:T(8,128)S(1)}, u32[]{:S(2)}, u32[]{:S(2)}) collective-permute-start(f32[240,128]{1,0:T(8,128)} %get-tuple-element.82), channel_id=1, source_target_pairs={{0,1},{1,0},{2,3},{3,2},{4,5},{5,4},{6,7},{7,6},{8,9},{9,8},{10,11... | collective-permute-start | bytes 368648 | tf_op jit(solution)/shard_map/ppermute | solution.py:676
  130.1 6.6 %collective-permute-start.11 = (f32[240,128]{1,0:T(8,128)}, f32[240,128]{1,0:T(8,128)S(1)}, u32[]{:S(2)}, u32[]{:S(2)}) collective-permute-start(f32[240,128]{1,0:T(8,128)} %get-tuple-element.83), channel_id=1, source_target_pairs={{0,2},{1,3},{2,0},{3,1},{4,6},{5,7},{6,4},{7,5},{8,10},{9,11},{10,... | collective-permute-start | bytes 368648 | tf_op jit(solution)/shard_map/ppermute | solution.py:676
  131.1 7.7 %collective-permute-start.12 = (f32[240,128]{1,0:T(8,128)}, f32[240,128]{1,0:T(8,128)S(1)}, u32[]{:S(2)}, u32[]{:S(2)}) collective-permute-start(f32[240,128]{1,0:T(8,128)} %get-tuple-element.84), channel_id=1, source_target_pairs={{0,3},{1,2},{2,1},{3,0},{4,7},{5,6},{6,5},{7,4},{8,11},{9,10},{10,... | collective-permute-start | bytes 368648 | tf_op jit(solution)/shard_map/ppermute | solution.py:676
  132.1 9.2 %collective-permute-start.13 = (f32[240,128]{1,0:T(8,128)}, f32[240,128]{1,0:T(8,128)S(1)}, u32[]{:S(2)}, u32[]{:S(2)}) collective-permute-start(f32[240,128]{1,0:T(8,128)} %get-tuple-element.85), channel_id=1, source_target_pairs={{0,4},{1,5},{2,6},{3,7},{4,0},{5,1},{6,2},{7,3},{8,12},{9,13},{10,... | collective-permute-start | bytes 368648 | tf_op jit(solution)/shard_map/ppermute | solution.py:676
  133.7 10.9 %collective-permute-start.14 = (f32[240,128]{1,0:T(8,128)}, f32[240,128]{1,0:T(8,128)S(1)}, u32[]{:S(2)}, u32[]{:S(2)}) collective-permute-start(f32[240,128]{1,0:T(8,128)} %get-tuple-element.86), channel_id=1, source_target_pairs={{0,5},{1,4},{2,7},{3,6},{4,1},{5,0},{6,3},{7,2},{8,13},{9,12},{10,... | collective-permute-start | bytes 368648 | tf_op jit(solution)/shard_map/ppermute | solution.py:676
  135.1 11.3 %collective-permute-start.15 = (f32[240,128]{1,0:T(8,128)}, f32[240,128]{1,0:T(8,128)S(1)}, u32[]{:S(2)}, u32[]{:S(2)}) collective-permute-start(f32[240,128]{1,0:T(8,128)} %get-tuple-element.87), channel_id=1, source_target_pairs={{0,6},{1,7},{2,4},{3,5},{4,2},{5,3},{6,0},{7,1},{8,14},{9,15},{10,... | collective-permute-start | bytes 368648 | tf_op jit(solution)/shard_map/ppermute | solution.py:676
  136.7 12.5 %collective-permute-start.16 = (f32[240,128]{1,0:T(8,128)}, f32[240,128]{1,0:T(8,128)S(1)}, u32[]{:S(2)}, u32[]{:S(2)}) collective-permute-start(f32[240,128]{1,0:T(8,128)} %get-tuple-element.88), channel_id=1, source_target_pairs={{0,7},{1,6},{2,5},{3,4},{4,3},{5,2},{6,1},{7,0},{8,15},{9,14},{10,... | collective-permute-start | bytes 368648 | tf_op jit(solution)/shard_map/ppermute | solution.py:676
  (15 other events, 76.1 us)

commit v3 on v2

--- a/solution.py
+++ b/solution.py
@@ -31,7 +31,8 @@
 DEG_USED = (320, 256, 192, 128, 64)
 DEG_BASE = (0, 768, 1280, 1792, 2048)
 DEG_TOTAL = 2304
-VMEM = 60 * 1024 * 1024
+VMEM = 40 * 1024 * 1024
+VMEM_LARGE = 60 * 1024 * 1024
 
 f32 = jnp.float32
 bf16 = jnp.bfloat16
@@ -81,6 +82,16 @@
     )
 
 
+def first_lanes():
+    latitude = 0.5 * math.pi - math.pi * (np.arange(HALF) + 0.5) / NLAT
+    exponent = log_norms()[:, None] + np.arange(NM)[:, None] * np.log(np.cos(latitude))[None, :]
+    firsts = np.argmax(exponent >= -61.0, axis=1).reshape(GROUPS, NM // GROUPS).min(axis=1)
+    return [int(first) // TILE * TILE for first in firsts]
+
+
+LANES = first_lanes()
+
+
 def split(values):
     high = values.astype(bf16)
     low = (values - high.astype(f32)).astype(bf16)
@@ -100,27 +111,38 @@
     outs, (out_ref, sems) = rest[:N_LON], rest[N_LON:]
     block = grid_ref.shape[0]
     step = pl.program_id(0)
-    target = lax.broadcasted_iota(jnp.int32, (TILE, STEN * TILE), 0).astype(jnp.int16)
-    one = jnp.ones((TILE, STEN * TILE), bf16)
-    zero = jnp.zeros((TILE, STEN * TILE), bf16)
+    target = lax.broadcasted_iota(jnp.int32, (TILE, TILE), 0).astype(jnp.int16)
+
+    def tall(row, kind):
+        block16 = jnp.broadcast_to(row, (16, TILE)).astype(kind)
+        return jnp.concatenate([block16] * (TILE // 16), axis=0)
+
     for r in range(block):
         for k in range(TPR):
             field = grid_ref[r, :, k * TILE : (k + 1) * TILE]
-            scaled = jnp.concatenate(
-                [field * weight_ref[r, k, s : s + 1, :] for s in range(STEN)], axis=1
-            )
-            high = scaled.astype(bf16).astype(f32)
-            sides = jnp.concatenate([high, scaled - high], axis=0).astype(bf16)
-            points = jnp.concatenate(
+            points = [stencil_ref[r, k, s : s + 1, :] for s in range(STEN)]
+            weights = [weight_ref[r, k, s : s + 1, :] for s in range(STEN)]
+            for s in range(STEN):
+                for later in range(s + 1, STEN):
+                    weights[s] = weights[s] + jnp.where(
+                        points[later] == points[s], weight_ref[r, k, later : later + 1, :], 0.0
+                    )
+            high = jnp.zeros((TILE, TILE), bf16)
+            low = high
+            for s in reversed(range(STEN)):
+                top = weights[s].astype(bf16).astype(f32)
+                here = tall(points[s], jnp.int16) == target
+                high = jnp.where(here, tall(top, bf16), high)
+                low = jnp.where(here, tall(weights[s] - top, bf16), low)
+            top = field.astype(bf16).astype(f32)
+            sides = jnp.concatenate(
                 [
-                    jnp.broadcast_to(stencil_ref[r, k, s : s + 1, :], (16, TILE))
-                    for s in range(STEN)
+                    jnp.concatenate([top, field - top], axis=0),
+                    jnp.concatenate([top, jnp.zeros_like(top)], axis=0),
                 ],
                 axis=1,
-            ).astype(jnp.int16)
-            points = jnp.concatenate([points] * (TILE // 16), axis=0)
-            hot = jnp.where(points == target, one, zero)
-            both = dot(sides, hot, NT)
+            ).astype(bf16)
+            both = dot(sides, jnp.concatenate([high, low], axis=1), NT)
             tile = step * (block * TPR) + r * TPR + k
             out_ref[pl.ds(tile, FL, stride=CHUNK), :] = both[:FL] + both[FL:]
 
@@ -153,7 +175,7 @@
 
 
 def spread_call(lon, grid, stencil, weight, owner, slot):
-    block = 8
+    block = 40
     return pl.pallas_call(
         spread_kernel,
         grid=(ROWS // block,),
@@ -171,7 +193,7 @@
             pltpu.VMEM((FL * CHUNK, TILE), f32),
             pltpu.SemaphoreType.DMA((N_LON,)),
         ],
-        compiler_params=pltpu.CompilerParams(vmem_limit_bytes=VMEM),
+        compiler_params=pltpu.CompilerParams(vmem_limit_bytes=VMEM_LARGE),
         name="spread",
     )(lon, grid, stencil, weight, owner, slot)
 
@@ -256,27 +278,41 @@
     )(order, norm, sine, logcos)
 
 
-def fourier_kernel(south_ref, *refs):
+def fourier_kernel(south_ref, extra_ref, *refs):
     chunks = refs[:N_LON]
-    real_high, real_low, mixed_high, mixed_low, extra_ref = refs[N_LON : N_LON + 5]
-    bands = refs[N_LON + 5 : N_LON + 8]
-    out_ref = refs[N_LON + 8]
-    scratch = refs[N_LON + 9 :]
+    stored = refs[N_LON : N_LON + 4]
+    bands = refs[N_LON + 4 : N_LON + 7]
+    out_hbm = refs[N_LON + 7]
+    scratch = refs[N_LON + 8 :]
     sums = scratch[:CHAINS]
-    c_high, c_low, tiles, keys, dense_ref, sems = scratch[CHAINS:]
-    loads = []
-    for k in range(N_LON):
-        loads.append(pltpu.make_async_copy(chunks[k], tiles.at[k], sems.at[k]))
-        loads.append(
-            pltpu.make_async_copy(
-                chunks[k].at[pl.ds(TILES, 8), :], keys.at[k], sems.at[N_LON + k]
-            )
+    c_high, c_low, tiles, lines, whole, keys, dense_ref, out_ref = scratch[CHAINS : CHAINS + 8]
+    tables = scratch[CHAINS + 8 : CHAINS + 12]
+    key_sems, tile_sems, table_sems, band_sems, out_sems = scratch[CHAINS + 12 :]
+    real_high, real_low, mixed_high, mixed_low = tables
+    key_loads = [
+        pltpu.make_async_copy(
+            chunks[k].at[pl.ds(TILES, 8), :], lines.at[pl.ds(8 * k, 8), :], key_sems.at[k]
         )
-    for copy in loads:
+        for k in range(N_LON)
+    ]
+    tile_loads = [
+        pltpu.make_async_copy(chunks[k].at[pl.ds(0, TILES), :], tiles.at[k], tile_sems.at[k])
+        for k in range(N_LON)
+    ]
+    table_loads = [
+        pltpu.make_async_copy(stored[i], tables[i], table_sems.at[i]) for i in range(4)
+    ]
+    for copy in key_loads + tile_loads + table_loads:
         copy.start()
+    for copy in key_loads:
+        copy.wait()
+    whole[...] = lines[...].astype(jnp.int32)
+    to_scalars = pltpu.make_async_copy(whole, keys, key_sems.at[N_LON])
+    to_scalars.start()
     for chain in sums:
         chain[...] = jnp.zeros(chain.shape, f32)
-    for copy in loads:
+    to_scalars.wait()
+    for copy in tile_loads:
         copy.wait()
     share = N_LON // CHAINS
     for part in range(share):
@@ -285,12 +321,12 @@
             def scatter(t, _):
                 for c, chain in enumerate(sums):
                     k = c * share + part
-                    slot = keys[k, line, t].astype(jnp.int32)
+                    slot = keys[8 * k + line, t]
                     tile = tiles[k, pl.ds(line * TILE + t, 1), :]
                     chain[pl.ds(slot, 1), :] = chain[pl.ds(slot, 1), :] + tile
                 return 0
 
-            lax.fori_loop(0, count, scatter, 0, unroll=4)
+            lax.fori_loop(0, count, scatter, 0, unroll=8)
     south = south_ref[0]
     root = math.sqrt(0.5)
     blank = jnp.zeros((16, NLON), bf16)
@@ -338,20 +374,25 @@
     lax.fori_loop(0, 15, butterfly, 0)
     stores = [
         pltpu.make_async_copy(
-            dense_ref.at[pl.ds(i * DENSE, DENSE), :], bands[i], sems.at[2 * N_LON + i]
+            dense_ref.at[pl.ds(i * DENSE, DENSE), :], bands[i], band_sems.at[i]
         )
         for i in range(3)
     ]
     for copy in stores:
         copy.start()
     extra = extra_ref[...]
+    for copy in table_loads:
+        copy.wait()
 
     def emit(m1, block):
         block = jnp.concatenate([block[:, :TILE], block[:, TILE:] + extra], axis=1)
         for h in range(N_LAT):
             for g in range(GROUPS):
                 start = h * WAVE_DEV + 2 * g
-                out_ref[h * 8 + m1, g, :, :] = block[start : start + 2, :]
+                out_ref[m1, h, g, :, :] = block[start : start + 2, :]
+        sent = pltpu.make_async_copy(out_ref.at[m1], out_hbm.at[:, m1], out_sems.at[m1])
+        sent.start()
+        stores.append(sent)
 
     def transform(ch, cl, wh, wl):
         rows = wh.shape[0]
@@ -373,23 +414,35 @@
 def fourier_call(south, chunks, tables, extra):
     vmem = pl.BlockSpec(memory_space=pltpu.VMEM)
     smem = pl.BlockSpec(memory_space=pltpu.SMEM)
-    return pl.pallas_call(
+    anywhere = pl.BlockSpec(memory_space=pl.ANY)
+    result = pl.pallas_call(
         fourier_kernel,
-        in_specs=[smem] + [pl.BlockSpec(memory_space=pl.ANY)] * N_LON + [vmem] * 5,
-        out_specs=[pl.BlockSpec(memory_space=pl.ANY)] * 3 + [vmem],
+        in_specs=[smem, vmem] + [anywhere] * (N_LON + 4),
+        out_specs=[anywhere] * 4,
         out_shape=[jax.ShapeDtypeStruct((DENSE, TILE), f32)] * 3
-        + [jax.ShapeDtypeStruct((N_LAT * N_LON, GROUPS, 2, 256), f32)],
+        + [jax.ShapeDtypeStruct((N_LAT, N_LON, GROUPS, 2, 256), f32)],
         scratch_shapes=[pltpu.VMEM((3 * DENSE, TILE), f32)] * CHAINS
         + [pltpu.VMEM((256, NLON), bf16)] * 2
         + [
-            pltpu.VMEM((N_LON, CHUNK, TILE), f32),
-            pltpu.SMEM((N_LON, 8, TILE), f32),
+            pltpu.VMEM((N_LON, TILES, TILE), f32),
+            pltpu.VMEM((8 * N_LON, TILE), f32),
+            pltpu.VMEM((8 * N_LON, TILE), jnp.int32),
+            pltpu.SMEM((8 * N_LON, TILE), jnp.int32),
             pltpu.VMEM((3 * DENSE, TILE), f32),
-            pltpu.SemaphoreType.DMA((2 * N_LON + 3,)),
+            pltpu.VMEM((N_LON, N_LAT, GROUPS, 2, 256), f32),
+        ]
+        + [pltpu.VMEM(table.shape, table.dtype) for table in tables]
+        + [
+            pltpu.SemaphoreType.DMA((N_LON + 1,)),
+            pltpu.SemaphoreType.DMA((N_LON,)),
+            pltpu.SemaphoreType.DMA((4,)),
+            pltpu.SemaphoreType.DMA((3,)),
+            pltpu.SemaphoreType.DMA((N_LON,)),
         ],
-        compiler_params=pltpu.CompilerParams(vmem_limit_bytes=VMEM),
+        compiler_params=pltpu.CompilerParams(vmem_limit_bytes=VMEM_LARGE),
         name="scatter_fourier",
-    )(south, *chunks, *tables, extra)
+    )(south, extra, *chunks, *tables)
+    return list(result[:3]) + [result[3].reshape(N_LAT * N_LON, GROUPS, 2, 256)]
 
 
 def legendre_kernel(
@@ -445,11 +498,11 @@
         rate = jnp.concatenate([rate_ref[...]] * (pad_len // TILE), axis=1)
         results = []
         for parity, folded in enumerate((full_n + full_s, full_n - full_s)):
-            folded = folded * weight
-            both = stacked_parts(folded)
+            skip = LANES[g]
+            both = stacked_parts((folded * weight)[:, skip:])
             start = DEG_BASE[g] + parity * pad_len
-            ph = high_ref[start : start + pad_len, :]
-            pw = low_ref[start : start + pad_len, :]
+            ph = high_ref[start : start + pad_len, skip:]
+            pw = low_ref[start : start + pad_len, skip:]
             main = dot(both, ph, NT)
             spectrum = main[:16] + (main[16:] + dot(both[:16], pw, NT))
             degree = wave + parity + 2 * lane
@@ -459,7 +512,10 @@
             damped = jnp.where(degree < NM, damped, 0.0)
             both = stacked_parts(damped)
             main = dot(both, ph, NN)
-            results.append(main[:16] + (main[16:] + dot(both[:16], pw, NN)))
+            grid = main[:16] + (main[16:] + dot(both[:16], pw, NN))
+            if skip:
+                grid = jnp.concatenate([jnp.zeros((16, skip), f32), grid], axis=1)
+            results.append(grid)
         for a in range(N_LAT):
             place = a if a < 8 else 15 - a
             offset = ROWS * place

time: 153 us -> 139 us (0.908)
  Pallas kernels: 52.2 us -> 33.4 us
  blocking collectives: 55.6 us -> 58.8 us
  waiting for transfers between devices: 10.9 us -> 12.5 us
    pallas_call x1, Pallas kernels: 8.92 us -> 3.79 us  [legendre_call(): pl.pallas_call(legendre_kernel, in_specs=[smem] + [vmem] * 5, out_specs=v...]
    pallas_call x1, Pallas kernels: 11.4 us -> 7.43 us  [spread_call(): pl.pallas_call(spread_kernel, grid=(ROWS // block,), in_specs=[pl.BlockSp...]
    all_to_all x1, blocking collectives: 24.6 us -> 28.2 us  [local(): back = lax.all_to_all(back, ('lat', 'lon'), 0, 0, tiled=True)]
    pallas_call x1, Pallas kernels: 8.82 us -> 5.54 us  [table_call(): pl.pallas_call(table_kernel, out_shape=(shape, shape), scratch_shapes=[pl...]
    pallas_call x1, Pallas kernels: 4.19 us -> 1.03 us  [synthesis_call(): pl.pallas_call(synthesis_kernel, in_specs=[vmem] * 5, out_specs=vmem, out...]
    unnamed x44 -> x38, local copies, waits for them, and re-layouts: 2.45 us -> 4.64 us
    pallas_call x1, Pallas kernels: 13.1 us -> 11.3 us  [fourier_call(): pl.pallas_call(fourier_kernel, in_specs=[smem, vmem] + [anywhere] * (N_LO...]
    ppermute x14, waiting for transfers between devices: 10.9 us -> 12.5 us  [exchanged(): lax.ppermute(chunks[k], 'lon', [(i, i ^ k) for i in range(N_LON)])]
  transfers between devices with their start and end apart: 17 -> 17, of which waited for: 5 -> 6; matrix products, arithmetic and copies ran while one was open for 4% -> 2% of each run, Pallas kernels for 14% -> 7%
where the time goes in v3:
time: 139 us; the launch traced here: 138 us
  blocking collectives  58.8 us (42%)
  Pallas kernels  33.4 us (24%)
  starting transfers between devices  24.7 us (18%)
  waiting for transfers between devices  12.5 us (9%)
  local copies, waits for them, and re-layouts  7.57 us (5%)
    all_to_all x1, blocking collectives, local(): coeff = lax.all_to_all(coeff, ('lat', 'lon'), 0, 0, tiled=True)  30.6 us
    all_to_all x1, blocking collectives, local(): back = lax.all_to_all(back, ('lat', 'lon'), 0, 0, tiled=True)  28.2 us
    ppermute x14, starting transfers between devices, exchanged(): lax.ppermute(chunks[k], 'lon', [(i, i ^ k) for i in range(N_LON)])  18.9 us
    ppermute x14, waiting for transfers between devices, exchanged(): lax.ppermute(chunks[k], 'lon', [(i, i ^ k) for i in range(N_LON)])  12.5 us
    pallas_call x1, Pallas kernels, fourier_call(): pl.pallas_call(fourier_kernel, in_specs=[smem, vmem] + [anywhere] * (N_LO...  11.3 us
    pallas_call x1, Pallas kernels, spread_call(): pl.pallas_call(spread_kernel, grid=(ROWS // block,), in_specs=[pl.BlockSp...  7.43 us
    pallas_call x1, Pallas kernels, table_call(): pl.pallas_call(table_kernel, out_shape=(shape, shape), scratch_shapes=[pl...  5.54 us
    unnamed x38, local copies, waits for them, and re-layouts  4.64 us
  transfers between devices with their start and end apart: 17, of which 6 were waited for; matrix products, arithmetic and copies ran while one was open for 2% of the time, Pallas kernels for 7%

profile of v3, /device:TPU:1, one launch (start us, length us, event | category | flops | bytes accessed | tf_op | source)
XLA Modules:
  0.0 138.2 jit_solution(9803950311097856555)
XLA Ops:
  0.6 7.4 %spread.1 = (f32[248,128]{1,0:T(8,128)}, f32[248,128]{1,0:T(8,128)}, f32[248,128]{1,0:T(8,128)}, f32[248,128]{1,0:T(8,128)}, f32[248,128]{1,0:T(8,128)}, /*index...) custom-call(s32[2]{0:T(128)} %pad_add_fusion.lon_ref, f32[80,8,384]{2,1,0:T(8,128)} %grid_ref.1, ...), custom_call_target="tpu_custom_call" | custom-call | tf_op jit(solution)/shard_map/spread/pallas_call | solution.py:179
  8.1 1.5 %collective-permute-start = (f32[248,128]{1,0:T(8,128)}, f32[248,128]{1,0:T(8,128)S(1)}, u32[]{:S(2)}, u32[]{:S(2)}) collective-permute-start(f32[248,128]{1,0:T(8,128)} %get-tuple-element.57), channel_id=1, source_target_pairs={{0,1},{1,0},{2,3},{3,2},{4,5},{5,4},{6,7},{7,6},{8,9},{9,8},{10,11... | collective-permute-start | bytes 380936 | tf_op jit(solution)/shard_map/ppermute | solution.py:732
  9.5 1.4 %collective-permute-start.1 = (f32[248,128]{1,0:T(8,128)}, f32[248,128]{1,0:T(8,128)S(1)}, u32[]{:S(2)}, u32[]{:S(2)}) collective-permute-start(f32[248,128]{1,0:T(8,128)} %get-tuple-element.58), channel_id=1, source_target_pairs={{0,2},{1,3},{2,0},{3,1},{4,6},{5,7},{6,4},{7,5},{8,10},{9,11},{10,... | collective-permute-start | bytes 380936 | tf_op jit(solution)/shard_map/ppermute | solution.py:732
  11.3 3.0 %collective-permute-start.3 = (f32[248,128]{1,0:T(8,128)}, f32[248,128]{1,0:T(8,128)S(1)}, u32[]{:S(2)}, u32[]{:S(2)}) collective-permute-start(f32[248,128]{1,0:T(8,128)} %get-tuple-element.60), channel_id=1, source_target_pairs={{0,4},{1,5},{2,6},{3,7},{4,0},{5,1},{6,2},{7,3},{8,12},{9,13},{10,... | collective-permute-start | bytes 380936 | tf_op jit(solution)/shard_map/ppermute | solution.py:732
  14.9 2.9 %collective-permute-start.5 = (f32[248,128]{1,0:T(8,128)}, f32[248,128]{1,0:T(8,128)}, u32[]{:S(2)}, u32[]{:S(2)}) collective-permute-start(f32[248,128]{1,0:T(8,128)} %get-tuple-element.62), channel_id=1, source_target_pairs={{0,6},{1,7},{2,4},{3,5},{4,2},{5,3},{6,0},{7,1},{8,14},{9,15},{10,... | collective-permute-start | bytes 380936 | tf_op jit(solution)/shard_map/ppermute | solution.py:732
  21.3 5.5 %legendre_table.1 = (bf16[2304,640]{1,0:T(8,128)(2,1)S(1)}, bf16[2304,640]{1,0:T(8,128)(2,1)S(1)}) custom-call(f32[8,128]{1,0:T(8,128)S(1)} %broadcast_in_dim.11.order_ref, f32[8,128]{1,0:T(8,128)S(1)} %broadcast_in_dim.13.norm_ref, f32[1,640]{1,0:T(1,128)S(1)} %copy-done.9, f32[1,640]{1,0:T(1,128)S(1)} %copy-done.8), custom_call_target="tpu_custom_call" | custom-call | flops 65536000 | bytes 6000000 | tf_op jit(solution)/shard_map/legendre_table/pallas_call | solution.py:269
  26.9 1.6 %copy-done.3 = bf16[2304,640]{1,0:T(8,128)(2,1)} copy-done((bf16[2304,640]{1,0:T(8,128)(2,1)}, bf16[2304,640]{1,0:T(8,128)(2,1)S(1)}, u32[]{:S(2)}) %copy-start.3) | copy-done | bytes 2949144
  30.0 11.3 %scatter_fourier.1 = (f32[1920,128]{1,0:T(8,128)}, f32[1920,128]{1,0:T(8,128)}, f32[1920,128]{1,0:T(8,128)}, f32[16,8,5,2,256]{4,3,2,1,0:T(2,128)}) custom-call(s32[1]{0:T(128)} %bitcast.south_ref, f32[160,128]{1,0:T(8,128)} %pad.7.extra_ref, f32[248,128]{1,0:T(8,128)} %get-tuple-element.56.refs_0_, f32[248,128]{1,0:T(8,128)} %copy-done.11, ...), custom_call_target="tpu_custom_call" | custom-call | tf_op jit(solution)/shard_map/scatter_fourier/pallas_call | solution.py:418
  41.3 30.6 %all_to_all.10.coeff_ref = f32[128,5,2,256]{3,2,1,0:T(2,128)S(1)} all-to-all(f32[128,5,2,256]{3,2,1,0:T(2,128)} %bitcast.18), channel_id=1, replica_groups=mesh['lat'=16,'lon'=8] {'lat','lon'}, dimensions={0} | all-to-all | bytes 2621440 | tf_op jit(solution)/shard_map/all_to_all | solution.py:749
  71.9 1.3 collective-permute-start.7
  73.2 4.0 %collective-permute-start.8 = (f32[1920,128]{1,0:T(8,128)S(1)}, f32[1920,128]{1,0:T(8,128)S(1)}, u32[]{:S(2)}, u32[]{:S(2)}) collective-permute-start(f32[1920,128]{1,0:T(8,128)S(1)} %copy-done.17), channel_id=1, source_target_pairs={{0,8},{8,16},{16,24},{24,32},{32,40},{40,48},{48,56},{56,64},{64,7... | collective-permute-start | bytes 2949128 | tf_op jit(solution)/shard_map/ppermute | solution.py:752
  77.2 1.8 %copy-done.4 = bf16[2304,640]{1,0:T(8,128)(2,1)S(1)} copy-done((bf16[2304,640]{1,0:T(8,128)(2,1)S(1)}, bf16[2304,640]{1,0:T(8,128)(2,1)}, u32[]{:S(2)}) %copy-start.4) | copy-done | bytes 2949144
  79.1 3.8 %legendre.1 = f32[128,5,2,128]{3,2,1,0:T(2,128)S(1)} custom-call(s32[1]{0:T(128)} %bitcast.10.wave_ref, f32[128,5,2,256]{3,2,1,0:T(2,128)S(1)} %all_to_all.10.coeff_ref, bf16[2304,640]{1,0:T(8,128)(2,1)S(1)} %get-tuple-element.73.high_ref, bf16[2304,640]{1,0:T(8,128)(2,1)S(1)} %copy-done.4, f32[1,640]{1,0:T(1,128)S(1)} %copy-done.7, ...), custom_call_target="tpu_custom_call" | custom-call | tf_op jit(solution)/shard_map/legendre/pallas_call | solution.py:537
  82.9 28.2 %all_to_all.11.back_ref = f32[128,5,2,128]{3,2,1,0:T(2,128)S(1)} all-to-all(f32[128,5,2,128]{3,2,1,0:T(2,128)S(1)} %legendre.1), channel_id=1, replica_groups=mesh['lat'=16,'lon'=8] {'lat','lon'}, dimensions={0} | all-to-all | bytes 1310720 | tf_op jit(solution)/shard_map/all_to_all | solution.py:754
  114.0 1.6 %combine.1 = (f32[240,128]{1,0:T(8,128)S(1)}, f32[240,128]{1,0:T(8,128)S(1)}, f32[240,128]{1,0:T(8,128)S(1)}, f32[240,128]{1,0:T(8,128)S(1)}, f32[240,128]{1,0:T...) custom-call(s32[1]{0:T(128)} %bitcast.1.lon_ref, ...), custom_call_target="tpu_custom_call" | custom-call | tf_op jit(solution)/shard_map/combine/pallas_call | solution.py:634
  116.2 1.3 collective-permute-start.11
  118.0 1.8 %collective-permute-start.13 = (f32[240,128]{1,0:T(8,128)S(1)}, f32[240,128]{1,0:T(8,128)S(1)}, u32[]{:S(2)}, u32[]{:S(2)}) collective-permute-start(f32[240,128]{1,0:T(8,128)S(1)} %get-tuple-element.85), channel_id=1, source_target_pairs={{0,4},{1,5},{2,6},{3,7},{4,0},{5,1},{6,2},{7,3},{8,12},{9,13},{10,... | collective-permute-start | bytes 368648 | tf_op jit(solution)/shard_map/ppermute | solution.py:732
  119.7 1.5 %collective-permute-start.14 = (f32[240,128]{1,0:T(8,128)S(1)}, f32[240,128]{1,0:T(8,128)S(1)}, u32[]{:S(2)}, u32[]{:S(2)}) collective-permute-start(f32[240,128]{1,0:T(8,128)S(1)} %get-tuple-element.86), channel_id=1, source_target_pairs={{0,5},{1,4},{2,7},{3,6},{4,1},{5,0},{6,3},{7,2},{8,13},{9,12},{10,... | collective-permute-start | bytes 368648 | tf_op jit(solution)/shard_map/ppermute | solution.py:732
  121.3 1.7 %collective-permute-start.15 = (f32[240,128]{1,0:T(8,128)S(1)}, f32[240,128]{1,0:T(8,128)S(1)}, u32[]{:S(2)}, u32[]{:S(2)}) collective-permute-start(f32[240,128]{1,0:T(8,128)S(1)} %get-tuple-element.87), channel_id=1, source_target_pairs={{0,6},{1,7},{2,4},{3,5},{4,2},{5,3},{6,0},{7,1},{8,14},{9,15},{10,... | collective-permute-start | bytes 368648 | tf_op jit(solution)/shard_map/ppermute | solution.py:732
  124.4 3.5 %collective-permute-done.13.rest_4_ = f32[240,128]{1,0:T(8,128)S(1)} collective-permute-done((f32[240,128]{1,0:T(8,128)S(1)}, f32[240,128]{1,0:T(8,128)S(1)}, u32[]{:S(2)}, u32[]{:S(2)}) %collective-permute-start.13) | collective-permute-done | bytes 122912 | tf_op jit(solution)/shard_map/ppermute | solution.py:732
  127.9 2.9 %collective-permute-done.14.rest_5_ = f32[240,128]{1,0:T(8,128)S(1)} collective-permute-done((f32[240,128]{1,0:T(8,128)S(1)}, f32[240,128]{1,0:T(8,128)S(1)}, u32[]{:S(2)}, u32[]{:S(2)}) %collective-permute-start.14) | collective-permute-done | bytes 122912 | tf_op jit(solution)/shard_map/ppermute | solution.py:732
  130.8 2.0 %collective-permute-done.15.rest_6_ = f32[240,128]{1,0:T(8,128)S(1)} collective-permute-done((f32[240,128]{1,0:T(8,128)S(1)}, f32[240,128]{1,0:T(8,128)S(1)}, u32[]{:S(2)}, u32[]{:S(2)}) %collective-permute-start.15) | collective-permute-done | bytes 122912 | tf_op jit(solution)/shard_map/ppermute | solution.py:732
  132.8 2.6 %collective-permute-done.16.rest_7_ = f32[240,128]{1,0:T(8,128)S(1)} collective-permute-done((f32[240,128]{1,0:T(8,128)S(1)}, f32[240,128]{1,0:T(8,128)S(1)}, u32[]{:S(2)}, u32[]{:S(2)}) %collective-permute-start.16) | collective-permute-done | bytes 122912 | tf_op jit(solution)/shard_map/ppermute | solution.py:732
  135.4 2.6 %place_rows.1 = f32[80,8,384]{2,1,0:T(8,128)} custom-call(s32[1]{0:T(128)} %bitcast.south_ref, s32[1]{0:T(128)} %bitcast.1.lon_ref, f32[240,128]{1,0:T(8,128)S(1)} %get-tuple-element.81.rest_0_, f32[240,128]{1,0:T(8,128)S(1)} %collective-permute-done.10.rest_1_, f32[240,128]{1,0:T(8,128)S(1)} %collective-permute-done.11.rest_2_, ...), custom_call_target="tpu_custom_call" | custom-call | tf_op jit(solution)/shard_map/place_rows/pallas_call | solution.py:678
  (81 shorter events, 11.7 us)
Async XLA Ops:
  0.0 19.8 %copy-start = (f32[8]{0:T(128)S(1)}, f32[8]{0:T(128)}, u32[]{:S(2)}) copy-start(f32[8]{0:T(128)} %param.23) | copy-start | bytes 100
  0.6 20.7 %copy-start.8 = (f32[1,640]{1,0:T(1,128)S(1)}, f32[1,640]{1,0:T(1,128)}, u32[]{:S(2)}) copy-start(f32[1,640]{1,0:T(1,128)} %constant.150.clone.logcos_ref) | copy-start | bytes 7684
  0.6 20.7 %copy-start.9 = (f32[1,640]{1,0:T(1,128)S(1)}, f32[1,640]{1,0:T(1,128)}, u32[]{:S(2)}) copy-start(f32[1,640]{1,0:T(1,128)} %constant.149.clone.sine_ref) | copy-start | bytes 7684
  8.1 6.8 %collective-permute-start = (f32[248,128]{1,0:T(8,128)}, f32[248,128]{1,0:T(8,128)S(1)}, u32[]{:S(2)}, u32[]{:S(2)}) collective-permute-start(f32[248,128]{1,0:T(8,128)} %get-tuple-element.57), channel_id=1, source_target_pairs={{0,1},{1,0},{2,3},{3,2},{4,5},{5,4},{6,7},{7,6},{8,9},{9,8},{10,11... | collective-permute-start | bytes 380936 | tf_op jit(solution)/shard_map/ppermute | solution.py:732
  9.5 8.3 %collective-permute-start.1 = (f32[248,128]{1,0:T(8,128)}, f32[248,128]{1,0:T(8,128)S(1)}, u32[]{:S(2)}, u32[]{:S(2)}) collective-permute-start(f32[248,128]{1,0:T(8,128)} %get-tuple-element.58), channel_id=1, source_target_pairs={{0,2},{1,3},{2,0},{3,1},{4,6},{5,7},{6,4},{7,5},{8,10},{9,11},{10,... | collective-permute-start | bytes 380936 | tf_op jit(solution)/shard_map/ppermute | solution.py:732
  11.0 17.7 %collective-permute-start.2 = (f32[248,128]{1,0:T(8,128)}, f32[248,128]{1,0:T(8,128)S(1)}, u32[]{:S(2)}, u32[]{:S(2)}) collective-permute-start(f32[248,128]{1,0:T(8,128)} %get-tuple-element.59), channel_id=1, source_target_pairs={{0,3},{1,2},{2,1},{3,0},{4,7},{5,6},{6,5},{7,4},{8,11},{9,10},{10,... | collective-permute-start | bytes 380936 | tf_op jit(solution)/shard_map/ppermute | solution.py:732
  11.3 17.4 %collective-permute-start.3 = (f32[248,128]{1,0:T(8,128)}, f32[248,128]{1,0:T(8,128)S(1)}, u32[]{:S(2)}, u32[]{:S(2)}) collective-permute-start(f32[248,128]{1,0:T(8,128)} %get-tuple-element.60), channel_id=1, source_target_pairs={{0,4},{1,5},{2,6},{3,7},{4,0},{5,1},{6,2},{7,3},{8,12},{9,13},{10,... | collective-permute-start | bytes 380936 | tf_op jit(solution)/shard_map/ppermute | solution.py:732
  14.3 14.4 %collective-permute-start.4 = (f32[248,128]{1,0:T(8,128)}, f32[248,128]{1,0:T(8,128)}, u32[]{:S(2)}, u32[]{:S(2)}) collective-permute-start(f32[248,128]{1,0:T(8,128)} %get-tuple-element.61), channel_id=1, source_target_pairs={{0,5},{1,4},{2,7},{3,6},{4,1},{5,0},{6,3},{7,2},{8,13},{9,12},{10,... | collective-permute-start | bytes 380936 | tf_op jit(solution)/shard_map/ppermute | solution.py:732
  14.9 13.8 %collective-permute-start.5 = (f32[248,128]{1,0:T(8,128)}, f32[248,128]{1,0:T(8,128)}, u32[]{:S(2)}, u32[]{:S(2)}) collective-permute-start(f32[248,128]{1,0:T(8,128)} %get-tuple-element.62), channel_id=1, source_target_pairs={{0,6},{1,7},{2,4},{3,5},{4,2},{5,3},{6,0},{7,1},{8,14},{9,15},{10,... | collective-permute-start | bytes 380936 | tf_op jit(solution)/shard_map/ppermute | solution.py:732
  17.8 12.1 %collective-permute-start.6 = (f32[248,128]{1,0:T(8,128)}, f32[248,128]{1,0:T(8,128)}, u32[]{:S(2)}, u32[]{:S(2)}) collective-permute-start(f32[248,128]{1,0:T(8,128)} %get-tuple-element.63), channel_id=1, source_target_pairs={{0,7},{1,6},{2,5},{3,4},{4,3},{5,2},{6,1},{7,0},{8,15},{9,14},{10,... | collective-permute-start | bytes 380936 | tf_op jit(solution)/shard_map/ppermute | solution.py:732
  41.3 30.6 %copy-start.18 = (f32[1920,128]{1,0:T(8,128)S(1)}, f32[1920,128]{1,0:T(8,128)}, u32[]{:S(2)}) copy-start(f32[1920,128]{1,0:T(8,128)} %get-tuple-element.78) | copy-start | bytes 2949124
  41.3 31.9 %copy-start.17 = (f32[1920,128]{1,0:T(8,128)S(1)}, f32[1920,128]{1,0:T(8,128)}, u32[]{:S(2)}) copy-start(f32[1920,128]{1,0:T(8,128)} %get-tuple-element.79) | copy-start | bytes 2949124
  41.3 35.9 %copy-start.7 = (f32[1,640]{1,0:T(1,128)S(1)}, f32[1,640]{1,0:T(1,128)}, u32[]{:S(2)}) copy-start(f32[1,640]{1,0:T(1,128)} %constant.151.clone.weight_ref) | copy-start | bytes 7684
  71.9 39.2 %collective-permute-start.7 = (f32[1920,128]{1,0:T(8,128)S(1)}, f32[1920,128]{1,0:T(8,128)S(1)}, u32[]{:S(2)}, u32[]{:S(2)}) collective-permute-start(f32[1920,128]{1,0:T(8,128)S(1)} %copy-done.18), channel_id=1, source_target_pairs={{8,0},{16,8},{24,16},{32,24},{40,32},{48,40},{56,48},{64,56},{72,6... | collective-permute-start | bytes 2949128 | tf_op jit(solution)/shard_map/ppermute | solution.py:751
  73.2 38.0 %collective-permute-start.8 = (f32[1920,128]{1,0:T(8,128)S(1)}, f32[1920,128]{1,0:T(8,128)S(1)}, u32[]{:S(2)}, u32[]{:S(2)}) collective-permute-start(f32[1920,128]{1,0:T(8,128)S(1)} %copy-done.17), channel_id=1, source_target_pairs={{0,8},{8,16},{16,24},{24,32},{32,40},{40,48},{48,56},{56,64},{64,7... | collective-permute-start | bytes 2949128 | tf_op jit(solution)/shard_map/ppermute | solution.py:752
  82.9 28.3 %copy-start.10 = (f32[1920,128]{1,0:T(8,128)S(1)}, f32[1920,128]{1,0:T(8,128)}, u32[]{:S(2)}) copy-start(f32[1920,128]{1,0:T(8,128)} %get-tuple-element.77) | copy-start | bytes 2949124
  111.3 2.7 %collective-permute-start.9 = (f32[1920,128]{1,0:T(8,128)S(1)}, f32[1920,128]{1,0:T(8,128)S(1)}, u32[]{:S(2)}, u32[]{:S(2)}) collective-permute-start(f32[1920,128]{1,0:T(8,128)S(1)} %add_add_fusion.own_ref), channel_id=1, source_target_pairs={{0,1},{1,0},{2,3},{3,2},{4,5},{5,4},{6,7},{7,6},{8,9},{9,8},{10,11... | collective-permute-start | bytes 2949128 | tf_op jit(solution)/shard_map/ppermute | solution.py:757
  115.7 5.6 %collective-permute-start.10 = (f32[240,128]{1,0:T(8,128)S(1)}, f32[240,128]{1,0:T(8,128)S(1)}, u32[]{:S(2)}, u32[]{:S(2)}) collective-permute-start(f32[240,128]{1,0:T(8,128)S(1)} %get-tuple-element.82), channel_id=1, source_target_pairs={{0,1},{1,0},{2,3},{3,2},{4,5},{5,4},{6,7},{7,6},{8,9},{9,8},{10,11... | collective-permute-start | bytes 368648 | tf_op jit(solution)/shard_map/ppermute | solution.py:732
  116.2 6.8 %collective-permute-start.11 = (f32[240,128]{1,0:T(8,128)S(1)}, f32[240,128]{1,0:T(8,128)S(1)}, u32[]{:S(2)}, u32[]{:S(2)}) collective-permute-start(f32[240,128]{1,0:T(8,128)S(1)} %get-tuple-element.83), channel_id=1, source_target_pairs={{0,2},{1,3},{2,0},{3,1},{4,6},{5,7},{6,4},{7,5},{8,10},{9,11},{10,... | collective-permute-start | bytes 368648 | tf_op jit(solution)/shard_map/ppermute | solution.py:732
  117.5 6.9 %collective-permute-start.12 = (f32[240,128]{1,0:T(8,128)S(1)}, f32[240,128]{1,0:T(8,128)S(1)}, u32[]{:S(2)}, u32[]{:S(2)}) collective-permute-start(f32[240,128]{1,0:T(8,128)S(1)} %get-tuple-element.84), channel_id=1, source_target_pairs={{0,3},{1,2},{2,1},{3,0},{4,7},{5,6},{6,5},{7,4},{8,11},{9,10},{10,... | collective-permute-start | bytes 368648 | tf_op jit(solution)/shard_map/ppermute | solution.py:732
  118.0 9.9 %collective-permute-start.13 = (f32[240,128]{1,0:T(8,128)S(1)}, f32[240,128]{1,0:T(8,128)S(1)}, u32[]{:S(2)}, u32[]{:S(2)}) collective-permute-start(f32[240,128]{1,0:T(8,128)S(1)} %get-tuple-element.85), channel_id=1, source_target_pairs={{0,4},{1,5},{2,6},{3,7},{4,0},{5,1},{6,2},{7,3},{8,12},{9,13},{10,... | collective-permute-start | bytes 368648 | tf_op jit(solution)/shard_map/ppermute | solution.py:732
  119.7 11.0 %collective-permute-start.14 = (f32[240,128]{1,0:T(8,128)S(1)}, f32[240,128]{1,0:T(8,128)S(1)}, u32[]{:S(2)}, u32[]{:S(2)}) collective-permute-start(f32[240,128]{1,0:T(8,128)S(1)} %get-tuple-element.86), channel_id=1, source_target_pairs={{0,5},{1,4},{2,7},{3,6},{4,1},{5,0},{6,3},{7,2},{8,13},{9,12},{10,... | collective-permute-start | bytes 368648 | tf_op jit(solution)/shard_map/ppermute | solution.py:732
  121.3 11.5 %collective-permute-start.15 = (f32[240,128]{1,0:T(8,128)S(1)}, f32[240,128]{1,0:T(8,128)S(1)}, u32[]{:S(2)}, u32[]{:S(2)}) collective-permute-start(f32[240,128]{1,0:T(8,128)S(1)} %get-tuple-element.87), channel_id=1, source_target_pairs={{0,6},{1,7},{2,4},{3,5},{4,2},{5,3},{6,0},{7,1},{8,14},{9,15},{10,... | collective-permute-start | bytes 368648 | tf_op jit(solution)/shard_map/ppermute | solution.py:732
  123.0 12.4 %collective-permute-start.16 = (f32[240,128]{1,0:T(8,128)S(1)}, f32[240,128]{1,0:T(8,128)S(1)}, u32[]{:S(2)}, u32[]{:S(2)}) collective-permute-start(f32[240,128]{1,0:T(8,128)S(1)} %get-tuple-element.88), channel_id=1, source_target_pairs={{0,7},{1,6},{2,5},{3,4},{4,3},{5,2},{6,1},{7,0},{8,15},{9,14},{10,... | collective-permute-start | bytes 368648 | tf_op jit(solution)/shard_map/ppermute | solution.py:732
  (12 other events, 63.2 us)

commit v4 on v3

--- a/solution.py
+++ b/solution.py
@@ -326,17 +326,15 @@
                     chain[pl.ds(slot, 1), :] = chain[pl.ds(slot, 1), :] + tile
                 return 0
 
-            lax.fori_loop(0, count, scatter, 0, unroll=8)
+            lax.fori_loop(0, count, scatter, 0, unroll=16)
     south = south_ref[0]
     root = math.sqrt(0.5)
     blank = jnp.zeros((16, NLON), bf16)
     c_high[240:256, :] = blank
     c_low[240:256, :] = blank
 
-    def butterfly(item, _):
-        place = item // 5
-        chunk = item % 5
-        band = jnp.where(south == 1, 2 - place, place)
+    def butterfly(band, chunk):
+        place = jnp.where(south == 1, 2 - band, band)
         row = pl.multiple_of(place * ROWS + chunk * 16, 16)
 
         def put(column, values):
@@ -369,17 +367,20 @@
             put(5 * BAND + at, s[3] - s[1])
             put(6 * BAND + at, t[0] - minus)
             put(7 * BAND + at, t[2] - plus)
-        return 0
-
-    lax.fori_loop(0, 15, butterfly, 0)
-    stores = [
-        pltpu.make_async_copy(
-            dense_ref.at[pl.ds(i * DENSE, DENSE), :], bands[i], band_sems.at[i]
-        )
-        for i in range(3)
-    ]
-    for copy in stores:
-        copy.start()
+
+    stores = []
+    for band in range(3):
+
+        def step(chunk, _, band=band):
+            butterfly(band, chunk)
+            return 0
+
+        lax.fori_loop(0, ROWS // 16, step, 0)
+        sent = pltpu.make_async_copy(
+            dense_ref.at[pl.ds(band * DENSE, DENSE), :], bands[band], band_sems.at[band]
+        )
+        sent.start()
+        stores.append(sent)
     extra = extra_ref[...]
     for copy in table_loads:
         copy.wait()
@@ -414,7 +415,7 @@
 def fourier_call(south, chunks, tables, extra):
     vmem = pl.BlockSpec(memory_space=pltpu.VMEM)
     smem = pl.BlockSpec(memory_space=pltpu.SMEM)
-    anywhere = pl.BlockSpec(memory_space=pl.ANY)
+    anywhere = pl.BlockSpec(memory_space=pltpu.HBM)
     result = pl.pallas_call(
         fourier_kernel,
         in_specs=[smem, vmem] + [anywhere] * (N_LON + 4),
@@ -439,7 +440,7 @@
             pltpu.SemaphoreType.DMA((3,)),
             pltpu.SemaphoreType.DMA((N_LON,)),
         ],
-        compiler_params=pltpu.CompilerParams(vmem_limit_bytes=VMEM_LARGE),
+        compiler_params=pltpu.CompilerParams(vmem_limit_bytes=50 * 1024 * 1024),
         name="scatter_fourier",
     )(south, extra, *chunks, *tables)
     return list(result[:3]) + [result[3].reshape(N_LAT * N_LON, GROUPS, 2, 256)]
@@ -646,7 +647,7 @@
 
 
 def place_kernel(south_ref, lon_ref, *rest):
-    chunks, (out_ref, rows_ref, sems) = rest[:N_LON], rest[N_LON:]
+    chunks, (out_hbm, rows_ref, out_ref, sems, out_sems) = rest[:N_LON], rest[N_LON:]
     south = south_ref[0]
     loads = [
         pltpu.make_async_copy(
@@ -669,20 +670,32 @@
             ]
         return 0
 
-    lax.fori_loop(0, ROWS, place, 0, unroll=8)
+    block = 16
+    stores = []
+    for piece in range(ROWS // block):
+        lax.fori_loop(piece * block, (piece + 1) * block, place, 0, unroll=8)
+        first = jnp.where(south == 1, ROWS - (piece + 1) * block, piece * block)
+        sent = pltpu.make_async_copy(
+            out_ref.at[pl.ds(first, block)], out_hbm.at[pl.ds(first, block)], out_sems.at[piece]
+        )
+        sent.start()
+        stores.append(sent)
+    for copy in stores:
+        copy.wait()
 
 
 def place_call(south, lon, chunks):
-    vmem = pl.BlockSpec(memory_space=pltpu.VMEM)
     smem = pl.BlockSpec(memory_space=pltpu.SMEM)
     return pl.pallas_call(
         place_kernel,
         in_specs=[smem, smem] + [pl.BlockSpec(memory_space=pl.ANY)] * N_LON,
-        out_specs=vmem,
+        out_specs=pl.BlockSpec(memory_space=pl.ANY),
         out_shape=jax.ShapeDtypeStruct((ROWS, FL, BAND), f32),
         scratch_shapes=[
             pltpu.VMEM((FL * TILES, TILE), f32),
+            pltpu.VMEM((ROWS, FL, BAND), f32),
             pltpu.SemaphoreType.DMA((N_LON,)),
+            pltpu.SemaphoreType.DMA((ROWS // 16,)),
         ],
         compiler_params=pltpu.CompilerParams(vmem_limit_bytes=VMEM),
         name="place_rows",
@@ -747,7 +760,6 @@
     )
     dense_below, dense_here, dense_above, coeff = fourier_call(south, chunks, tables, extra)
     coeff = lax.all_to_all(coeff, ("lat", "lon"), 0, 0, tiled=True)
-    dense_below, dense_above, coeff = lax.optimization_barrier((dense_below, dense_above, coeff))
     below = lax.ppermute(dense_below, "lat", [(i + 1, i) for i in range(N_LAT - 1)])
     above = lax.ppermute(dense_above, "lat", [(i, i + 1) for i in range(N_LAT - 1)])
     back = legendre_call(wave.reshape(1), coeff, high, low, weight, rate)

time: 139 us -> 130 us (0.935)
  blocking collectives: 58.8 us -> 20.3 us
  waiting for transfers between devices: 12.5 us -> 27.5 us
  starting transfers between devices: 24.7 us -> 35.6 us
  local copies, waits for them, and re-layouts: 7.57 us -> 10.2 us
  other arithmetic: 0.78 us -> 2.49 us
    all_to_all x1 -> x0, blocking collectives: 30.6 us -> none  [local(): coeff = lax.all_to_all(coeff, ('lat', 'lon'), 0, 0, tiled=True)]
    all_to_all x0 -> x1, waiting for transfers between devices: none -> 15.8 us  [local(): coeff = lax.all_to_all(coeff, ('lat', 'lon'), 0, 0, tiled=True)]
    all_to_all x0 -> x1, starting transfers between devices: none -> 9.05 us  [local(): coeff = lax.all_to_all(coeff, ('lat', 'lon'), 0, 0, tiled=True)]
    all_to_all x1, blocking collectives: 28.2 us -> 20.3 us  [local(): back = lax.all_to_all(back, ('lat', 'lon'), 0, 0, tiled=True)]
    unnamed x38 -> x32, local copies, waits for them, and re-layouts: 4.64 us -> 7.92 us
    ppermute x14, waiting for transfers between devices: 12.5 us -> 10.5 us  [exchanged(): lax.ppermute(chunks[k], 'lon', [(i, i ^ k) for i in range(N_LON)])]
    add x1, other arithmetic: 0.14 us -> 1.79 us  [local(): departed = dense_here + below + above]
  transfers between devices with their start and end apart: 17 -> 18, of which waited for: 6 -> 8; matrix products, arithmetic and copies ran while one was open for 2% -> 2% of each run, Pallas kernels for 7% -> 8%
where the time goes in v4:
time: 130 us; the launch traced here: 129 us
  starting transfers between devices  35.6 us (27%)
  Pallas kernels  32.8 us (25%)
  waiting for transfers between devices  27.5 us (21%)
  blocking collectives  20.3 us (16%)
  local copies, waits for them, and re-layouts  10.2 us (8%)
  other arithmetic  2.49 us (2%)
    all_to_all x1, blocking collectives, local(): back = lax.all_to_all(back, ('lat', 'lon'), 0, 0, tiled=True)  20.3 us
    ppermute x14, starting transfers between devices, exchanged(): lax.ppermute(chunks[k], 'lon', [(i, i ^ k) for i in range(N_LON)])  18.9 us
    all_to_all x1, waiting for transfers between devices, local(): coeff = lax.all_to_all(coeff, ('lat', 'lon'), 0, 0, tiled=True)  15.8 us
    pallas_call x1, Pallas kernels, fourier_call(): pl.pallas_call(fourier_kernel, in_specs=[smem, vmem] + [anywhere] * (N_LO...  11 us
    ppermute x14, waiting for transfers between devices, exchanged(): lax.ppermute(chunks[k], 'lon', [(i, i ^ k) for i in range(N_LON)])  10.5 us
    all_to_all x1, starting transfers between devices, local(): coeff = lax.all_to_all(coeff, ('lat', 'lon'), 0, 0, tiled=True)  9.05 us
    unnamed x32, local copies, waits for them, and re-layouts  7.92 us
    pallas_call x1, Pallas kernels, spread_call(): pl.pallas_call(spread_kernel, grid=(ROWS // block,), in_specs=[pl.BlockSp...  7.43 us
  transfers between devices with their start and end apart: 18, of which 8 were waited for; matrix products, arithmetic and copies ran while one was open for 2% of the time, Pallas kernels for 8%

profile of v4, /device:TPU:1, one launch (start us, length us, event | category | flops | bytes accessed | tf_op | source)
XLA Modules:
  0.0 129.3 jit_solution(9645374259644048098)
XLA Ops:
  0.7 7.4 %spread.1 = (f32[248,128]{1,0:T(8,128)}, f32[248,128]{1,0:T(8,128)}, f32[248,128]{1,0:T(8,128)}, f32[248,128]{1,0:T(8,128)}, f32[248,128]{1,0:T(8,128)}, /*index...) custom-call(s32[2]{0:T(128)} %pad_add_fusion.lon_ref, f32[80,8,384]{2,1,0:T(8,128)} %grid_ref.1, ...), custom_call_target="tpu_custom_call" | custom-call | tf_op jit(solution)/shard_map/spread/pallas_call | solution.py:179
  8.1 1.5 %collective-permute-start = (f32[248,128]{1,0:T(8,128)}, f32[248,128]{1,0:T(8,128)S(1)}, u32[]{:S(2)}, u32[]{:S(2)}) collective-permute-start(f32[248,128]{1,0:T(8,128)} %get-tuple-element.54), channel_id=1, source_target_pairs={{0,1},{1,0},{2,3},{3,2},{4,5},{5,4},{6,7},{7,6},{8,9},{9,8},{10,11... | collective-permute-start | bytes 380936 | tf_op jit(solution)/shard_map/ppermute | solution.py:745
  11.3 3.0 %collective-permute-start.3 = (f32[248,128]{1,0:T(8,128)}, f32[248,128]{1,0:T(8,128)S(1)}, u32[]{:S(2)}, u32[]{:S(2)}) collective-permute-start(f32[248,128]{1,0:T(8,128)} %get-tuple-element.57), channel_id=1, source_target_pairs={{0,4},{1,5},{2,6},{3,7},{4,0},{5,1},{6,2},{7,3},{8,12},{9,13},{10,... | collective-permute-start | bytes 380936 | tf_op jit(solution)/shard_map/ppermute | solution.py:745
  14.9 2.9 %collective-permute-start.5 = (f32[248,128]{1,0:T(8,128)}, f32[248,128]{1,0:T(8,128)S(1)}, u32[]{:S(2)}, u32[]{:S(2)}) collective-permute-start(f32[248,128]{1,0:T(8,128)} %get-tuple-element.59), channel_id=1, source_target_pairs={{0,6},{1,7},{2,4},{3,5},{4,2},{5,3},{6,0},{7,1},{8,14},{9,15},{10,... | collective-permute-start | bytes 380936 | tf_op jit(solution)/shard_map/ppermute | solution.py:745
  20.8 5.5 %legendre_table.1 = (bf16[2304,640]{1,0:T(8,128)(2,1)S(1)}, bf16[2304,640]{1,0:T(8,128)(2,1)S(1)}) custom-call(f32[8,128]{1,0:T(8,128)S(1)} %broadcast_in_dim.11.order_ref, f32[8,128]{1,0:T(8,128)S(1)} %broadcast_in_dim.13.norm_ref, f32[1,640]{1,0:T(1,128)S(1)} %copy-done.13, f32[1,640]{1,0:T(1,128)S(1)} %copy-done.12), custom_call_target="tpu_custom_call" | custom-call | flops 65536000 | bytes 6000000 | tf_op jit(solution)/shard_map/legendre_table/pallas_call | solution.py:269
  26.4 1.6 %copy-done.3 = bf16[2304,640]{1,0:T(8,128)(2,1)} copy-done((bf16[2304,640]{1,0:T(8,128)(2,1)}, bf16[2304,640]{1,0:T(8,128)(2,1)S(1)}, u32[]{:S(2)}) %copy-start.3) | copy-done | bytes 2949144
  27.9 1.6 %copy-done.5 = bf16[2304,640]{1,0:T(8,128)(2,1)} copy-done((bf16[2304,640]{1,0:T(8,128)(2,1)}, bf16[2304,640]{1,0:T(8,128)(2,1)S(1)}, u32[]{:S(2)}) %copy-start.5) | copy-done | bytes 2949144
  29.9 11.0 %scatter_fourier.1 = (f32[1920,128]{1,0:T(8,128)S(1)}, f32[1920,128]{1,0:T(8,128)S(1)}, f32[1920,128]{1,0:T(8,128)}, f32[16,8,5,2,256]{4,3,2,1,0:T(2,128)}) custom-call(s32[1]{0:T(128)} %bitcast.south_ref, f32[160,128]{1,0:T(8,128)S(1)} %pad.7.extra_ref, f32[248,128]{1,0:T(8,128)S(1)} %copy-done.9, f32[248,128]{1,0:T(8,128)S(1)} %collective-permute-done.refs_1_, ...), custom_call_target="tpu_custom_call" | custom-call | tf_op jit(solution)/shard_map/scatter_fourier/pallas_call | solution.py:419
  41.9 9.1 %all-to-all-start = ((f32[128,5,2,256]{3,2,1,0:T(2,128)}), f32[128,5,2,256]{3,2,1,0:T(2,128)S(1)}, u32[]{:S(2)}, u32[]{:S(2)}) async-start(f32[128,5,2,256]{3,2,1,0:T(2,128)} %bitcast.18), calls=%async_computation | async-start | bytes 2621440 | tf_op jit(solution)/shard_map/all_to_all | solution.py:762
  52.3 5.0 %collective-permute-start.8 = (f32[1920,128]{1,0:T(8,128)}, f32[1920,128]{1,0:T(8,128)}, u32[]{:S(2)}, u32[]{:S(2)}) collective-permute-start(f32[1920,128]{1,0:T(8,128)} %get-tuple-element.73), channel_id=1, source_target_pairs={{0,8},{8,16},{16,24},{24,32},{32,40},{40,48},{48,56},{56,64},{64,7... | collective-permute-start | bytes 2949128 | tf_op jit(solution)/shard_map/ppermute | solution.py:764
  57.3 15.8 %all-to-all-done.coeff_ref = f32[128,5,2,256]{3,2,1,0:T(2,128)S(1)} async-done(((f32[128,5,2,256]{3,2,1,0:T(2,128)}), f32[128,5,2,256]{3,2,1,0:T(2,128)S(1)}, u32[]{:S(2)}, u32[]{:S(2)}) %all-to-all-start) | async-done | bytes 1310752 | tf_op jit(solution)/shard_map/all_to_all | solution.py:762
  73.2 1.8 %copy-done.4 = bf16[2304,640]{1,0:T(8,128)(2,1)S(1)} copy-done((bf16[2304,640]{1,0:T(8,128)(2,1)S(1)}, bf16[2304,640]{1,0:T(8,128)(2,1)}, u32[]{:S(2)}) %copy-start.4) | copy-done | bytes 2949144
  75.0 1.8 %copy-done.6 = bf16[2304,640]{1,0:T(8,128)(2,1)S(1)} copy-done((bf16[2304,640]{1,0:T(8,128)(2,1)S(1)}, bf16[2304,640]{1,0:T(8,128)(2,1)}, u32[]{:S(2)}) %copy-start.6) | copy-done | bytes 2949144
  76.8 3.7 %legendre.1 = f32[128,5,2,128]{3,2,1,0:T(2,128)S(1)} custom-call(s32[1]{0:T(128)} %bitcast.10.wave_ref, f32[128,5,2,256]{3,2,1,0:T(2,128)S(1)} %all-to-all-done.coeff_ref, bf16[2304,640]{1,0:T(8,128)(2,1)S(1)} %copy-done.4, bf16[2304,640]{1,0:T(8,128)(2,1)S(1)} %copy-done.6, f32[1,640]{1,0:T(1,128)S(1)} %copy-done.10, f32[16,128]{1,0:T(8,128)S(1)} %broadcast_in_dim.15.rate_ref), custom_call_target="tpu_custom_call" | custom-call | tf_op jit(solution)/shard_map/legendre/pallas_call | solution.py:538
  80.6 20.3 %all_to_all.10.back_ref = f32[128,5,2,128]{3,2,1,0:T(2,128)S(1)} all-to-all(f32[128,5,2,128]{3,2,1,0:T(2,128)S(1)} %legendre.1), channel_id=1, replica_groups=mesh['lat'=16,'lon'=8] {'lat','lon'}, dimensions={0} | all-to-all | bytes 1310720 | tf_op jit(solution)/shard_map/all_to_all | solution.py:766
  100.9 1.8 %add_add_fusion.own_ref = f32[1920,128]{1,0:T(8,128)S(1)} fusion(f32[1920,128]{1,0:T(8,128)} %collective-permute-done.8, f32[1920,128]{1,0:T(8,128)S(1)} %get-tuple-element.71, f32[1920,128]{1,0:T(8,128)} %collective-permute-done.7), kind=kLoop, calls=%fused_computation.1 | loop fusion | flops 491520 | bytes 3932160 | tf_op jit(solution)/shard_map/add | solution.py:768
  106.2 1.6 %combine.1 = (f32[240,128]{1,0:T(8,128)S(1)}, f32[240,128]{1,0:T(8,128)S(1)}, f32[240,128]{1,0:T(8,128)S(1)}, f32[240,128]{1,0:T(8,128)S(1)}, f32[240,128]{1,0:T...) custom-call(s32[1]{0:T(128)} %bitcast.1.lon_ref, ...), custom_call_target="tpu_custom_call" | custom-call | tf_op jit(solution)/shard_map/combine/pallas_call | solution.py:635
  108.3 1.8 %collective-permute-start.12 = (f32[240,128]{1,0:T(8,128)S(1)}, f32[240,128]{1,0:T(8,128)S(1)}, u32[]{:S(2)}, u32[]{:S(2)}) collective-permute-start(f32[240,128]{1,0:T(8,128)S(1)} %get-tuple-element.78), channel_id=1, source_target_pairs={{0,3},{1,2},{2,1},{3,0},{4,7},{5,6},{6,5},{7,4},{8,11},{9,10},{10,... | collective-permute-start | bytes 368648 | tf_op jit(solution)/shard_map/ppermute | solution.py:745
  110.6 2.7 %collective-permute-start.14 = (f32[240,128]{1,0:T(8,128)S(1)}, f32[240,128]{1,0:T(8,128)S(1)}, u32[]{:S(2)}, u32[]{:S(2)}) collective-permute-start(f32[240,128]{1,0:T(8,128)S(1)} %get-tuple-element.80), channel_id=1, source_target_pairs={{0,5},{1,4},{2,7},{3,6},{4,1},{5,0},{6,3},{7,2},{8,13},{9,12},{10,... | collective-permute-start | bytes 368648 | tf_op jit(solution)/shard_map/ppermute | solution.py:745
  113.5 2.8 %collective-permute-start.16 = (f32[240,128]{1,0:T(8,128)S(1)}, f32[240,128]{1,0:T(8,128)S(1)}, u32[]{:S(2)}, u32[]{:S(2)}) collective-permute-start(f32[240,128]{1,0:T(8,128)S(1)} %get-tuple-element.82), channel_id=1, source_target_pairs={{0,7},{1,6},{2,5},{3,4},{4,3},{5,2},{6,1},{7,0},{8,15},{9,14},{10,... | collective-permute-start | bytes 368648 | tf_op jit(solution)/shard_map/ppermute | solution.py:745
  118.3 3.0 %collective-permute-done.14.rest_5_ = f32[240,128]{1,0:T(8,128)S(1)} collective-permute-done((f32[240,128]{1,0:T(8,128)S(1)}, f32[240,128]{1,0:T(8,128)S(1)}, u32[]{:S(2)}, u32[]{:S(2)}) %collective-permute-start.14) | collective-permute-done | bytes 122912 | tf_op jit(solution)/shard_map/ppermute | solution.py:745
  121.3 2.8 %collective-permute-done.15.rest_6_ = f32[240,128]{1,0:T(8,128)S(1)} collective-permute-done((f32[240,128]{1,0:T(8,128)S(1)}, f32[240,128]{1,0:T(8,128)S(1)}, u32[]{:S(2)}, u32[]{:S(2)}) %collective-permute-start.15) | collective-permute-done | bytes 122912 | tf_op jit(solution)/shard_map/ppermute | solution.py:745
  124.1 2.6 %collective-permute-done.16.rest_7_ = f32[240,128]{1,0:T(8,128)S(1)} collective-permute-done((f32[240,128]{1,0:T(8,128)S(1)}, f32[240,128]{1,0:T(8,128)S(1)}, u32[]{:S(2)}, u32[]{:S(2)}) %collective-permute-start.16) | collective-permute-done | bytes 122912 | tf_op jit(solution)/shard_map/ppermute | solution.py:745
  126.7 2.4 %place_rows.1 = f32[80,8,384]{2,1,0:T(8,128)} custom-call(s32[1]{0:T(128)} %bitcast.south_ref, s32[1]{0:T(128)} %bitcast.1.lon_ref, f32[240,128]{1,0:T(8,128)S(1)} %get-tuple-element.75.rest_0_, f32[240,128]{1,0:T(8,128)S(1)} %collective-permute-done.10.rest_1_, f32[240,128]{1,0:T(8,128)S(1)} %collective-permute-done.11.rest_2_, ...), custom_call_target="tpu_custom_call" | custom-call | tf_op jit(solution)/shard_map/place_rows/pallas_call | solution.py:689
  (76 shorter events, 15.1 us)
Async XLA Ops:
  0.0 19.9 %copy-start = (f32[8]{0:T(128)S(1)}, f32[8]{0:T(128)}, u32[]{:S(2)}) copy-start(f32[8]{0:T(128)} %param.23) | copy-start | bytes 100
  0.0 14.6 %copy-start.15 = (s32[16]{0:T(128)S(1)}, s32[16]{0:T(128)}, u32[]{:S(2)}) copy-start(s32[16]{0:T(128)} %constant.163) | copy-start | bytes 196
  0.0 14.6 %copy-start.14 = (f32[80,4,2,2]{0,3,2,1:T(2,128)S(1)}, f32[80,4,2,2]{0,3,2,1:T(2,128)}, u32[]{:S(2)}) copy-start(f32[80,4,2,2]{0,3,2,1:T(2,128)} %param.22) | copy-start | bytes 15364
  0.7 20.1 %copy-start.12 = (f32[1,640]{1,0:T(1,128)S(1)}, f32[1,640]{1,0:T(1,128)}, u32[]{:S(2)}) copy-start(f32[1,640]{1,0:T(1,128)} %constant.150.clone.logcos_ref) | copy-start | bytes 7684
  0.7 20.1 %copy-start.13 = (f32[1,640]{1,0:T(1,128)S(1)}, f32[1,640]{1,0:T(1,128)}, u32[]{:S(2)}) copy-start(f32[1,640]{1,0:T(1,128)} %constant.149.clone.sine_ref) | copy-start | bytes 7684
  8.1 6.8 %collective-permute-start = (f32[248,128]{1,0:T(8,128)}, f32[248,128]{1,0:T(8,128)S(1)}, u32[]{:S(2)}, u32[]{:S(2)}) collective-permute-start(f32[248,128]{1,0:T(8,128)} %get-tuple-element.54), channel_id=1, source_target_pairs={{0,1},{1,0},{2,3},{3,2},{4,5},{5,4},{6,7},{7,6},{8,9},{9,8},{10,11... | collective-permute-start | bytes 380936 | tf_op jit(solution)/shard_map/ppermute | solution.py:745
  9.6 8.2 %collective-permute-start.1 = (f32[248,128]{1,0:T(8,128)}, f32[248,128]{1,0:T(8,128)S(1)}, u32[]{:S(2)}, u32[]{:S(2)}) collective-permute-start(f32[248,128]{1,0:T(8,128)} %get-tuple-element.55), channel_id=1, source_target_pairs={{0,2},{1,3},{2,0},{3,1},{4,6},{5,7},{6,4},{7,5},{8,10},{9,11},{10,... | collective-permute-start | bytes 380936 | tf_op jit(solution)/shard_map/ppermute | solution.py:745
  11.0 18.7 %collective-permute-start.2 = (f32[248,128]{1,0:T(8,128)}, f32[248,128]{1,0:T(8,128)S(1)}, u32[]{:S(2)}, u32[]{:S(2)}) collective-permute-start(f32[248,128]{1,0:T(8,128)} %get-tuple-element.56), channel_id=1, source_target_pairs={{0,3},{1,2},{2,1},{3,0},{4,7},{5,6},{6,5},{7,4},{8,11},{9,10},{10,... | collective-permute-start | bytes 380936 | tf_op jit(solution)/shard_map/ppermute | solution.py:745
  11.3 18.4 %collective-permute-start.3 = (f32[248,128]{1,0:T(8,128)}, f32[248,128]{1,0:T(8,128)S(1)}, u32[]{:S(2)}, u32[]{:S(2)}) collective-permute-start(f32[248,128]{1,0:T(8,128)} %get-tuple-element.57), channel_id=1, source_target_pairs={{0,4},{1,5},{2,6},{3,7},{4,0},{5,1},{6,2},{7,3},{8,12},{9,13},{10,... | collective-permute-start | bytes 380936 | tf_op jit(solution)/shard_map/ppermute | solution.py:745
  14.3 15.4 %collective-permute-start.4 = (f32[248,128]{1,0:T(8,128)}, f32[248,128]{1,0:T(8,128)S(1)}, u32[]{:S(2)}, u32[]{:S(2)}) collective-permute-start(f32[248,128]{1,0:T(8,128)} %get-tuple-element.58), channel_id=1, source_target_pairs={{0,5},{1,4},{2,7},{3,6},{4,1},{5,0},{6,3},{7,2},{8,13},{9,12},{10,... | collective-permute-start | bytes 380936 | tf_op jit(solution)/shard_map/ppermute | solution.py:745
  14.9 14.8 %collective-permute-start.5 = (f32[248,128]{1,0:T(8,128)}, f32[248,128]{1,0:T(8,128)S(1)}, u32[]{:S(2)}, u32[]{:S(2)}) collective-permute-start(f32[248,128]{1,0:T(8,128)} %get-tuple-element.59), channel_id=1, source_target_pairs={{0,6},{1,7},{2,4},{3,5},{4,2},{5,3},{6,0},{7,1},{8,14},{9,15},{10,... | collective-permute-start | bytes 380936 | tf_op jit(solution)/shard_map/ppermute | solution.py:745
  17.9 12.0 %collective-permute-start.6 = (f32[248,128]{1,0:T(8,128)}, f32[248,128]{1,0:T(8,128)S(1)}, u32[]{:S(2)}, u32[]{:S(2)}) collective-permute-start(f32[248,128]{1,0:T(8,128)} %get-tuple-element.60), channel_id=1, source_target_pairs={{0,7},{1,6},{2,5},{3,4},{4,3},{5,2},{6,1},{7,0},{8,15},{9,14},{10,... | collective-permute-start | bytes 380936 | tf_op jit(solution)/shard_map/ppermute | solution.py:745
  41.9 31.2 %copy-start.10 = (f32[1,640]{1,0:T(1,128)S(1)}, f32[1,640]{1,0:T(1,128)}, u32[]{:S(2)}) copy-start(f32[1,640]{1,0:T(1,128)} %constant.151.clone.weight_ref) | copy-start | bytes 7684
  41.9 31.2 %all-to-all-start = ((f32[128,5,2,256]{3,2,1,0:T(2,128)}), f32[128,5,2,256]{3,2,1,0:T(2,128)S(1)}, u32[]{:S(2)}, u32[]{:S(2)}) async-start(f32[128,5,2,256]{3,2,1,0:T(2,128)} %bitcast.18), calls=%async_computation | async-start | bytes 2621440 | tf_op jit(solution)/shard_map/all_to_all | solution.py:762
  51.0 49.9 %collective-permute-start.7 = (f32[1920,128]{1,0:T(8,128)}, f32[1920,128]{1,0:T(8,128)}, u32[]{:S(2)}, u32[]{:S(2)}) collective-permute-start(f32[1920,128]{1,0:T(8,128)} %copy-done.11), channel_id=1, source_target_pairs={{8,0},{16,8},{24,16},{32,24},{40,32},{48,40},{56,48},{64,56},{72,6... | collective-permute-start | bytes 2949128 | tf_op jit(solution)/shard_map/ppermute | solution.py:763
  52.3 48.6 %collective-permute-start.8 = (f32[1920,128]{1,0:T(8,128)}, f32[1920,128]{1,0:T(8,128)}, u32[]{:S(2)}, u32[]{:S(2)}) collective-permute-start(f32[1920,128]{1,0:T(8,128)} %get-tuple-element.73), channel_id=1, source_target_pairs={{0,8},{8,16},{16,24},{24,32},{32,40},{40,48},{48,56},{56,64},{64,7... | collective-permute-start | bytes 2949128 | tf_op jit(solution)/shard_map/ppermute | solution.py:764
  102.7 3.5 %collective-permute-start.9 = (f32[1920,128]{1,0:T(8,128)S(1)}, f32[1920,128]{1,0:T(8,128)S(1)}, u32[]{:S(2)}, u32[]{:S(2)}) collective-permute-start(f32[1920,128]{1,0:T(8,128)S(1)} %add_add_fusion.own_ref), channel_id=1, source_target_pairs={{0,1},{1,0},{2,3},{3,2},{4,5},{5,4},{6,7},{7,6},{8,9},{9,8},{10,11... | collective-permute-start | bytes 2949128 | tf_op jit(solution)/shard_map/ppermute | solution.py:769
  107.9 5.5 %collective-permute-start.10 = (f32[240,128]{1,0:T(8,128)S(1)}, f32[240,128]{1,0:T(8,128)S(1)}, u32[]{:S(2)}, u32[]{:S(2)}) collective-permute-start(f32[240,128]{1,0:T(8,128)S(1)} %get-tuple-element.76), channel_id=1, source_target_pairs={{0,1},{1,0},{2,3},{3,2},{4,5},{5,4},{6,7},{7,6},{8,9},{9,8},{10,11... | collective-permute-start | bytes 368648 | tf_op jit(solution)/shard_map/ppermute | solution.py:745
  108.3 5.2 %collective-permute-start.11 = (f32[240,128]{1,0:T(8,128)S(1)}, f32[240,128]{1,0:T(8,128)S(1)}, u32[]{:S(2)}, u32[]{:S(2)}) collective-permute-start(f32[240,128]{1,0:T(8,128)S(1)} %get-tuple-element.77), channel_id=1, source_target_pairs={{0,2},{1,3},{2,0},{3,1},{4,6},{5,7},{6,4},{7,5},{8,10},{9,11},{10,... | collective-permute-start | bytes 368648 | tf_op jit(solution)/shard_map/ppermute | solution.py:745
  108.3 8.5 %collective-permute-start.12 = (f32[240,128]{1,0:T(8,128)S(1)}, f32[240,128]{1,0:T(8,128)S(1)}, u32[]{:S(2)}, u32[]{:S(2)}) collective-permute-start(f32[240,128]{1,0:T(8,128)S(1)} %get-tuple-element.78), channel_id=1, source_target_pairs={{0,3},{1,2},{2,1},{3,0},{4,7},{5,6},{6,5},{7,4},{8,11},{9,10},{10,... | collective-permute-start | bytes 368648 | tf_op jit(solution)/shard_map/ppermute | solution.py:745
  110.1 8.2 %collective-permute-start.13 = (f32[240,128]{1,0:T(8,128)S(1)}, f32[240,128]{1,0:T(8,128)S(1)}, u32[]{:S(2)}, u32[]{:S(2)}) collective-permute-start(f32[240,128]{1,0:T(8,128)S(1)} %get-tuple-element.79), channel_id=1, source_target_pairs={{0,4},{1,5},{2,6},{3,7},{4,0},{5,1},{6,2},{7,3},{8,12},{9,13},{10,... | collective-permute-start | bytes 368648 | tf_op jit(solution)/shard_map/ppermute | solution.py:745
  110.6 10.7 %collective-permute-start.14 = (f32[240,128]{1,0:T(8,128)S(1)}, f32[240,128]{1,0:T(8,128)S(1)}, u32[]{:S(2)}, u32[]{:S(2)}) collective-permute-start(f32[240,128]{1,0:T(8,128)S(1)} %get-tuple-element.80), channel_id=1, source_target_pairs={{0,5},{1,4},{2,7},{3,6},{4,1},{5,0},{6,3},{7,2},{8,13},{9,12},{10,... | collective-permute-start | bytes 368648 | tf_op jit(solution)/shard_map/ppermute | solution.py:745
  113.3 10.7 %collective-permute-start.15 = (f32[240,128]{1,0:T(8,128)S(1)}, f32[240,128]{1,0:T(8,128)S(1)}, u32[]{:S(2)}, u32[]{:S(2)}) collective-permute-start(f32[240,128]{1,0:T(8,128)S(1)} %get-tuple-element.81), channel_id=1, source_target_pairs={{0,6},{1,7},{2,4},{3,5},{4,2},{5,3},{6,0},{7,1},{8,14},{9,15},{10,... | collective-permute-start | bytes 368648 | tf_op jit(solution)/shard_map/ppermute | solution.py:745
  113.5 13.2 %collective-permute-start.16 = (f32[240,128]{1,0:T(8,128)S(1)}, f32[240,128]{1,0:T(8,128)S(1)}, u32[]{:S(2)}, u32[]{:S(2)}) collective-permute-start(f32[240,128]{1,0:T(8,128)S(1)} %get-tuple-element.82), channel_id=1, source_target_pairs={{0,7},{1,6},{2,5},{3,4},{4,3},{5,2},{6,1},{7,0},{8,15},{9,14},{10,... | collective-permute-start | bytes 368648 | tf_op jit(solution)/shard_map/ppermute | solution.py:745
  (10 other events, 42.3 us)

commit v5 on v4

--- a/solution.py
+++ b/solution.py
@@ -27,10 +27,10 @@
 DENSE = N_LON * TPR * ROWS
 CHUNK = TILES + 8
 CHAINS = 4
-DEG_PAD = (384, 256, 256, 128, 128)
+DEG_PAD = (320, 256, 192, 128, 64)
 DEG_USED = (320, 256, 192, 128, 64)
-DEG_BASE = (0, 768, 1280, 1792, 2048)
-DEG_TOTAL = 2304
+DEG_BASE = (0, 640, 1152, 1536, 1792)
+DEG_TOTAL = 1920
 VMEM = 40 * 1024 * 1024
 VMEM_LARGE = 60 * 1024 * 1024
 
@@ -496,7 +496,7 @@
         wave = wave_ref[0] + 128 * g
         factor = jnp.where(wave == 0, 1.0, 2.0).astype(f32)
         lane = lax.broadcasted_iota(jnp.int32, (16, pad_len), 1)
-        rate = jnp.concatenate([rate_ref[...]] * (pad_len // TILE), axis=1)
+        rate = jnp.concatenate([rate_ref[...]] * (-(-pad_len // TILE)), axis=1)[:, :pad_len]
         results = []
         for parity, folded in enumerate((full_n + full_s, full_n - full_s)):
             skip = LANES[g]

time: 130 us -> 129 us (level)
  no operation moved by 1% of the time
where the time goes in v5:
time: 129 us
  starting transfers between devices  35.3 us (27%)
  Pallas kernels  33.2 us (26%)
  waiting for transfers between devices  27.8 us (22%)
  blocking collectives  20.1 us (16%)
  local copies, waits for them, and re-layouts  9.66 us (7%)
  other arithmetic  2.41 us (2%)
    all_to_all x1, blocking collectives, local(): back = lax.all_to_all(back, ('lat', 'lon'), 0, 0, tiled=True)  20.1 us
    ppermute x14, starting transfers between devices, exchanged(): lax.ppermute(chunks[k], 'lon', [(i, i ^ k) for i in range(N_LON)])  18.9 us
    all_to_all x1, waiting for transfers between devices, local(): coeff = lax.all_to_all(coeff, ('lat', 'lon'), 0, 0, tiled=True)  15.9 us
    pallas_call x1, Pallas kernels, fourier_call(): pl.pallas_call(fourier_kernel, in_specs=[smem, vmem] + [anywhere] * (N_LO...  11.1 us
    ppermute x14, waiting for transfers between devices, exchanged(): lax.ppermute(chunks[k], 'lon', [(i, i ^ k) for i in range(N_LON)])  10.8 us
    all_to_all x1, starting transfers between devices, local(): coeff = lax.all_to_all(coeff, ('lat', 'lon'), 0, 0, tiled=True)  8.88 us
    pallas_call x1, Pallas kernels, spread_call(): pl.pallas_call(spread_kernel, grid=(ROWS // block,), in_specs=[pl.BlockSp...  7.44 us
    unnamed x32, local copies, waits for them, and re-layouts  7.38 us
  transfers between devices with their start and end apart: 18, of which 8 were waited for; matrix products, arithmetic and copies ran while one was open for 2% of the time, Pallas kernels for 8%

profile of v5, /device:TPU:1, one launch (start us, length us, event | category | flops | bytes accessed | tf_op | source)
XLA Modules:
  0.0 128.9 jit_solution(11276590685988721303)
XLA Ops:
  0.6 7.4 %spread.1 = (f32[248,128]{1,0:T(8,128)}, f32[248,128]{1,0:T(8,128)}, f32[248,128]{1,0:T(8,128)}, f32[248,128]{1,0:T(8,128)}, f32[248,128]{1,0:T(8,128)}, /*index...) custom-call(s32[2]{0:T(128)} %pad_add_fusion.lon_ref, f32[80,8,384]{2,1,0:T(8,128)} %grid_ref.1, ...), custom_call_target="tpu_custom_call" | custom-call | tf_op jit(solution)/shard_map/spread/pallas_call | solution.py:179
  8.1 1.5 %collective-permute-start = (f32[248,128]{1,0:T(8,128)}, f32[248,128]{1,0:T(8,128)S(1)}, u32[]{:S(2)}, u32[]{:S(2)}) collective-permute-start(f32[248,128]{1,0:T(8,128)} %get-tuple-element.54), channel_id=1, source_target_pairs={{0,1},{1,0},{2,3},{3,2},{4,5},{5,4},{6,7},{7,6},{8,9},{9,8},{10,11... | collective-permute-start | bytes 380936 | tf_op jit(solution)/shard_map/ppermute | solution.py:745
  11.3 3.0 %collective-permute-start.3 = (f32[248,128]{1,0:T(8,128)}, f32[248,128]{1,0:T(8,128)S(1)}, u32[]{:S(2)}, u32[]{:S(2)}) collective-permute-start(f32[248,128]{1,0:T(8,128)} %get-tuple-element.57), channel_id=1, source_target_pairs={{0,4},{1,5},{2,6},{3,7},{4,0},{5,1},{6,2},{7,3},{8,12},{9,13},{10,... | collective-permute-start | bytes 380936 | tf_op jit(solution)/shard_map/ppermute | solution.py:745
  14.9 2.9 %collective-permute-start.5 = (f32[248,128]{1,0:T(8,128)}, f32[248,128]{1,0:T(8,128)S(1)}, u32[]{:S(2)}, u32[]{:S(2)}) collective-permute-start(f32[248,128]{1,0:T(8,128)} %get-tuple-element.59), channel_id=1, source_target_pairs={{0,6},{1,7},{2,4},{3,5},{4,2},{5,3},{6,0},{7,1},{8,14},{9,15},{10,... | collective-permute-start | bytes 380936 | tf_op jit(solution)/shard_map/ppermute | solution.py:745
  20.7 5.5 %legendre_table.1 = (bf16[1920,640]{1,0:T(8,128)(2,1)S(1)}, bf16[1920,640]{1,0:T(8,128)(2,1)S(1)}) custom-call(f32[8,128]{1,0:T(8,128)S(1)} %broadcast_in_dim.11.order_ref, f32[8,128]{1,0:T(8,128)S(1)} %broadcast_in_dim.13.norm_ref, f32[1,640]{1,0:T(1,128)S(1)} %copy-done.13, f32[1,640]{1,0:T(1,128)S(1)} %copy-done.12), custom_call_target="tpu_custom_call" | custom-call | flops 65536000 | bytes 6000000 | tf_op jit(solution)/shard_map/legendre_table/pallas_call | solution.py:269
  26.2 1.4 %copy-done.3 = bf16[1920,640]{1,0:T(8,128)(2,1)} copy-done((bf16[1920,640]{1,0:T(8,128)(2,1)}, bf16[1920,640]{1,0:T(8,128)(2,1)S(1)}, u32[]{:S(2)}) %copy-start.3) | copy-done | bytes 2457624
  27.7 1.5 %copy-done.5 = bf16[1920,640]{1,0:T(8,128)(2,1)} copy-done((bf16[1920,640]{1,0:T(8,128)(2,1)}, bf16[1920,640]{1,0:T(8,128)(2,1)S(1)}, u32[]{:S(2)}) %copy-start.5) | copy-done | bytes 2457624
  29.8 11.1 %scatter_fourier.1 = (f32[1920,128]{1,0:T(8,128)S(1)}, f32[1920,128]{1,0:T(8,128)S(1)}, f32[1920,128]{1,0:T(8,128)}, f32[16,8,5,2,256]{4,3,2,1,0:T(2,128)}) custom-call(s32[1]{0:T(128)} %bitcast.south_ref, f32[160,128]{1,0:T(8,128)S(1)} %pad.7.extra_ref, f32[248,128]{1,0:T(8,128)S(1)} %copy-done.9, f32[248,128]{1,0:T(8,128)S(1)} %collective-permute-done.refs_1_, ...), custom_call_target="tpu_custom_call" | custom-call | tf_op jit(solution)/shard_map/scatter_fourier/pallas_call | solution.py:419
  41.9 8.9 %all-to-all-start = ((f32[128,5,2,256]{3,2,1,0:T(2,128)}), f32[128,5,2,256]{3,2,1,0:T(2,128)S(1)}, u32[]{:S(2)}, u32[]{:S(2)}) async-start(f32[128,5,2,256]{3,2,1,0:T(2,128)} %bitcast.18), calls=%async_computation | async-start | bytes 2621440 | tf_op jit(solution)/shard_map/all_to_all | solution.py:762
  52.1 4.9 %collective-permute-start.8 = (f32[1920,128]{1,0:T(8,128)}, f32[1920,128]{1,0:T(8,128)}, u32[]{:S(2)}, u32[]{:S(2)}) collective-permute-start(f32[1920,128]{1,0:T(8,128)} %get-tuple-element.73), channel_id=1, source_target_pairs={{0,8},{8,16},{16,24},{24,32},{32,40},{40,48},{48,56},{56,64},{64,7... | collective-permute-start | bytes 2949128 | tf_op jit(solution)/shard_map/ppermute | solution.py:764
  57.1 15.9 %all-to-all-done.coeff_ref = f32[128,5,2,256]{3,2,1,0:T(2,128)S(1)} async-done(((f32[128,5,2,256]{3,2,1,0:T(2,128)}), f32[128,5,2,256]{3,2,1,0:T(2,128)S(1)}, u32[]{:S(2)}, u32[]{:S(2)}) %all-to-all-start) | async-done | bytes 1310752 | tf_op jit(solution)/shard_map/all_to_all | solution.py:762
  73.0 1.7 %copy-done.4 = bf16[1920,640]{1,0:T(8,128)(2,1)S(1)} copy-done((bf16[1920,640]{1,0:T(8,128)(2,1)S(1)}, bf16[1920,640]{1,0:T(8,128)(2,1)}, u32[]{:S(2)}) %copy-start.4) | copy-done | bytes 2457624
  74.7 1.7 %copy-done.6 = bf16[1920,640]{1,0:T(8,128)(2,1)S(1)} copy-done((bf16[1920,640]{1,0:T(8,128)(2,1)S(1)}, bf16[1920,640]{1,0:T(8,128)(2,1)}, u32[]{:S(2)}) %copy-start.6) | copy-done | bytes 2457624
  76.4 4.1 %legendre.1 = f32[128,5,2,128]{3,2,1,0:T(2,128)S(1)} custom-call(s32[1]{0:T(128)} %bitcast.10.wave_ref, f32[128,5,2,256]{3,2,1,0:T(2,128)S(1)} %all-to-all-done.coeff_ref, bf16[1920,640]{1,0:T(8,128)(2,1)S(1)} %copy-done.4, bf16[1920,640]{1,0:T(8,128)(2,1)S(1)} %copy-done.6, f32[1,640]{1,0:T(1,128)S(1)} %copy-done.10, f32[16,128]{1,0:T(8,128)S(1)} %broadcast_in_dim.15.rate_ref), custom_call_target="tpu_custom_call" | custom-call | tf_op jit(solution)/shard_map/legendre/pallas_call | solution.py:538
  80.5 20.1 %all_to_all.10.back_ref = f32[128,5,2,128]{3,2,1,0:T(2,128)S(1)} all-to-all(f32[128,5,2,128]{3,2,1,0:T(2,128)S(1)} %legendre.1), channel_id=1, replica_groups=mesh['lat'=16,'lon'=8] {'lat','lon'}, dimensions={0} | all-to-all | bytes 1310720 | tf_op jit(solution)/shard_map/all_to_all | solution.py:766
  100.7 1.8 %add_add_fusion.own_ref = f32[1920,128]{1,0:T(8,128)S(1)} fusion(f32[1920,128]{1,0:T(8,128)} %collective-permute-done.8, f32[1920,128]{1,0:T(8,128)S(1)} %get-tuple-element.71, f32[1920,128]{1,0:T(8,128)} %collective-permute-done.7), kind=kLoop, calls=%fused_computation.1 | loop fusion | flops 491520 | bytes 3932160 | tf_op jit(solution)/shard_map/add | solution.py:768
  106.0 1.6 %combine.1 = (f32[240,128]{1,0:T(8,128)S(1)}, f32[240,128]{1,0:T(8,128)S(1)}, f32[240,128]{1,0:T(8,128)S(1)}, f32[240,128]{1,0:T(8,128)S(1)}, f32[240,128]{1,0:T...) custom-call(s32[1]{0:T(128)} %bitcast.1.lon_ref, ...), custom_call_target="tpu_custom_call" | custom-call | tf_op jit(solution)/shard_map/combine/pallas_call | solution.py:635
  108.1 1.8 %collective-permute-start.12 = (f32[240,128]{1,0:T(8,128)S(1)}, f32[240,128]{1,0:T(8,128)S(1)}, u32[]{:S(2)}, u32[]{:S(2)}) collective-permute-start(f32[240,128]{1,0:T(8,128)S(1)} %get-tuple-element.78), channel_id=1, source_target_pairs={{0,3},{1,2},{2,1},{3,0},{4,7},{5,6},{6,5},{7,4},{8,11},{9,10},{10,... | collective-permute-start | bytes 368648 | tf_op jit(solution)/shard_map/ppermute | solution.py:745
  110.4 2.7 %collective-permute-start.14 = (f32[240,128]{1,0:T(8,128)S(1)}, f32[240,128]{1,0:T(8,128)S(1)}, u32[]{:S(2)}, u32[]{:S(2)}) collective-permute-start(f32[240,128]{1,0:T(8,128)S(1)} %get-tuple-element.80), channel_id=1, source_target_pairs={{0,5},{1,4},{2,7},{3,6},{4,1},{5,0},{6,3},{7,2},{8,13},{9,12},{10,... | collective-permute-start | bytes 368648 | tf_op jit(solution)/shard_map/ppermute | solution.py:745
  113.2 2.9 %collective-permute-start.16 = (f32[240,128]{1,0:T(8,128)S(1)}, f32[240,128]{1,0:T(8,128)S(1)}, u32[]{:S(2)}, u32[]{:S(2)}) collective-permute-start(f32[240,128]{1,0:T(8,128)S(1)} %get-tuple-element.82), channel_id=1, source_target_pairs={{0,7},{1,6},{2,5},{3,4},{4,3},{5,2},{6,1},{7,0},{8,15},{9,14},{10,... | collective-permute-start | bytes 368648 | tf_op jit(solution)/shard_map/ppermute | solution.py:745
  117.8 3.2 %collective-permute-done.14.rest_5_ = f32[240,128]{1,0:T(8,128)S(1)} collective-permute-done((f32[240,128]{1,0:T(8,128)S(1)}, f32[240,128]{1,0:T(8,128)S(1)}, u32[]{:S(2)}, u32[]{:S(2)}) %collective-permute-start.14) | collective-permute-done | bytes 122912 | tf_op jit(solution)/shard_map/ppermute | solution.py:745
  121.0 2.8 %collective-permute-done.15.rest_6_ = f32[240,128]{1,0:T(8,128)S(1)} collective-permute-done((f32[240,128]{1,0:T(8,128)S(1)}, f32[240,128]{1,0:T(8,128)S(1)}, u32[]{:S(2)}, u32[]{:S(2)}) %collective-permute-start.15) | collective-permute-done | bytes 122912 | tf_op jit(solution)/shard_map/ppermute | solution.py:745
  123.7 2.6 %collective-permute-done.16.rest_7_ = f32[240,128]{1,0:T(8,128)S(1)} collective-permute-done((f32[240,128]{1,0:T(8,128)S(1)}, f32[240,128]{1,0:T(8,128)S(1)}, u32[]{:S(2)}, u32[]{:S(2)}) %collective-permute-start.16) | collective-permute-done | bytes 122912 | tf_op jit(solution)/shard_map/ppermute | solution.py:745
  126.4 2.4 %place_rows.1 = f32[80,8,384]{2,1,0:T(8,128)} custom-call(s32[1]{0:T(128)} %bitcast.south_ref, s32[1]{0:T(128)} %bitcast.1.lon_ref, f32[240,128]{1,0:T(8,128)S(1)} %get-tuple-element.75.rest_0_, f32[240,128]{1,0:T(8,128)S(1)} %collective-permute-done.10.rest_1_, f32[240,128]{1,0:T(8,128)S(1)} %collective-permute-done.11.rest_2_, ...), custom_call_target="tpu_custom_call" | custom-call | tf_op jit(solution)/shard_map/place_rows/pallas_call | solution.py:689
  (76 shorter events, 15.0 us)
Async XLA Ops:
  0.0 19.8 %copy-start = (f32[8]{0:T(128)S(1)}, f32[8]{0:T(128)}, u32[]{:S(2)}) copy-start(f32[8]{0:T(128)} %param.23) | copy-start | bytes 100
  0.0 14.6 %copy-start.15 = (s32[16]{0:T(128)S(1)}, s32[16]{0:T(128)}, u32[]{:S(2)}) copy-start(s32[16]{0:T(128)} %constant.163) | copy-start | bytes 196
  0.0 14.6 %copy-start.14 = (f32[80,4,2,2]{0,3,2,1:T(2,128)S(1)}, f32[80,4,2,2]{0,3,2,1:T(2,128)}, u32[]{:S(2)}) copy-start(f32[80,4,2,2]{0,3,2,1:T(2,128)} %param.22) | copy-start | bytes 15364
  0.6 20.1 %copy-start.12 = (f32[1,640]{1,0:T(1,128)S(1)}, f32[1,640]{1,0:T(1,128)}, u32[]{:S(2)}) copy-start(f32[1,640]{1,0:T(1,128)} %constant.150.clone.logcos_ref) | copy-start | bytes 7684
  0.6 20.1 %copy-start.13 = (f32[1,640]{1,0:T(1,128)S(1)}, f32[1,640]{1,0:T(1,128)}, u32[]{:S(2)}) copy-start(f32[1,640]{1,0:T(1,128)} %constant.149.clone.sine_ref) | copy-start | bytes 7684
  8.1 6.8 %collective-permute-start = (f32[248,128]{1,0:T(8,128)}, f32[248,128]{1,0:T(8,128)S(1)}, u32[]{:S(2)}, u32[]{:S(2)}) collective-permute-start(f32[248,128]{1,0:T(8,128)} %get-tuple-element.54), channel_id=1, source_target_pairs={{0,1},{1,0},{2,3},{3,2},{4,5},{5,4},{6,7},{7,6},{8,9},{9,8},{10,11... | collective-permute-start | bytes 380936 | tf_op jit(solution)/shard_map/ppermute | solution.py:745
  9.5 8.2 %collective-permute-start.1 = (f32[248,128]{1,0:T(8,128)}, f32[248,128]{1,0:T(8,128)S(1)}, u32[]{:S(2)}, u32[]{:S(2)}) collective-permute-start(f32[248,128]{1,0:T(8,128)} %get-tuple-element.55), channel_id=1, source_target_pairs={{0,2},{1,3},{2,0},{3,1},{4,6},{5,7},{6,4},{7,5},{8,10},{9,11},{10,... | collective-permute-start | bytes 380936 | tf_op jit(solution)/shard_map/ppermute | solution.py:745
  10.9 18.4 %collective-permute-start.2 = (f32[248,128]{1,0:T(8,128)}, f32[248,128]{1,0:T(8,128)S(1)}, u32[]{:S(2)}, u32[]{:S(2)}) collective-permute-start(f32[248,128]{1,0:T(8,128)} %get-tuple-element.56), channel_id=1, source_target_pairs={{0,3},{1,2},{2,1},{3,0},{4,7},{5,6},{6,5},{7,4},{8,11},{9,10},{10,... | collective-permute-start | bytes 380936 | tf_op jit(solution)/shard_map/ppermute | solution.py:745
  11.3 18.1 %collective-permute-start.3 = (f32[248,128]{1,0:T(8,128)}, f32[248,128]{1,0:T(8,128)S(1)}, u32[]{:S(2)}, u32[]{:S(2)}) collective-permute-start(f32[248,128]{1,0:T(8,128)} %get-tuple-element.57), channel_id=1, source_target_pairs={{0,4},{1,5},{2,6},{3,7},{4,0},{5,1},{6,2},{7,3},{8,12},{9,13},{10,... | collective-permute-start | bytes 380936 | tf_op jit(solution)/shard_map/ppermute | solution.py:745
  14.3 15.1 %collective-permute-start.4 = (f32[248,128]{1,0:T(8,128)}, f32[248,128]{1,0:T(8,128)S(1)}, u32[]{:S(2)}, u32[]{:S(2)}) collective-permute-start(f32[248,128]{1,0:T(8,128)} %get-tuple-element.58), channel_id=1, source_target_pairs={{0,5},{1,4},{2,7},{3,6},{4,1},{5,0},{6,3},{7,2},{8,13},{9,12},{10,... | collective-permute-start | bytes 380936 | tf_op jit(solution)/shard_map/ppermute | solution.py:745
  14.9 14.5 %collective-permute-start.5 = (f32[248,128]{1,0:T(8,128)}, f32[248,128]{1,0:T(8,128)S(1)}, u32[]{:S(2)}, u32[]{:S(2)}) collective-permute-start(f32[248,128]{1,0:T(8,128)} %get-tuple-element.59), channel_id=1, source_target_pairs={{0,6},{1,7},{2,4},{3,5},{4,2},{5,3},{6,0},{7,1},{8,14},{9,15},{10,... | collective-permute-start | bytes 380936 | tf_op jit(solution)/shard_map/ppermute | solution.py:745
  17.8 12.0 %collective-permute-start.6 = (f32[248,128]{1,0:T(8,128)}, f32[248,128]{1,0:T(8,128)S(1)}, u32[]{:S(2)}, u32[]{:S(2)}) collective-permute-start(f32[248,128]{1,0:T(8,128)} %get-tuple-element.60), channel_id=1, source_target_pairs={{0,7},{1,6},{2,5},{3,4},{4,3},{5,2},{6,1},{7,0},{8,15},{9,14},{10,... | collective-permute-start | bytes 380936 | tf_op jit(solution)/shard_map/ppermute | solution.py:745
  41.9 31.1 %copy-start.10 = (f32[1,640]{1,0:T(1,128)S(1)}, f32[1,640]{1,0:T(1,128)}, u32[]{:S(2)}) copy-start(f32[1,640]{1,0:T(1,128)} %constant.151.clone.weight_ref) | copy-start | bytes 7684
  41.9 31.1 %all-to-all-start = ((f32[128,5,2,256]{3,2,1,0:T(2,128)}), f32[128,5,2,256]{3,2,1,0:T(2,128)S(1)}, u32[]{:S(2)}, u32[]{:S(2)}) async-start(f32[128,5,2,256]{3,2,1,0:T(2,128)} %bitcast.18), calls=%async_computation | async-start | bytes 2621440 | tf_op jit(solution)/shard_map/all_to_all | solution.py:762
  50.8 49.9 %collective-permute-start.7 = (f32[1920,128]{1,0:T(8,128)}, f32[1920,128]{1,0:T(8,128)}, u32[]{:S(2)}, u32[]{:S(2)}) collective-permute-start(f32[1920,128]{1,0:T(8,128)} %copy-done.11), channel_id=1, source_target_pairs={{8,0},{16,8},{24,16},{32,24},{40,32},{48,40},{56,48},{64,56},{72,6... | collective-permute-start | bytes 2949128 | tf_op jit(solution)/shard_map/ppermute | solution.py:763
  52.1 48.6 %collective-permute-start.8 = (f32[1920,128]{1,0:T(8,128)}, f32[1920,128]{1,0:T(8,128)}, u32[]{:S(2)}, u32[]{:S(2)}) collective-permute-start(f32[1920,128]{1,0:T(8,128)} %get-tuple-element.73), channel_id=1, source_target_pairs={{0,8},{8,16},{16,24},{24,32},{32,40},{40,48},{48,56},{56,64},{64,7... | collective-permute-start | bytes 2949128 | tf_op jit(solution)/shard_map/ppermute | solution.py:764
  102.5 3.5 %collective-permute-start.9 = (f32[1920,128]{1,0:T(8,128)S(1)}, f32[1920,128]{1,0:T(8,128)S(1)}, u32[]{:S(2)}, u32[]{:S(2)}) collective-permute-start(f32[1920,128]{1,0:T(8,128)S(1)} %add_add_fusion.own_ref), channel_id=1, source_target_pairs={{0,1},{1,0},{2,3},{3,2},{4,5},{5,4},{6,7},{7,6},{8,9},{9,8},{10,11... | collective-permute-start | bytes 2949128 | tf_op jit(solution)/shard_map/ppermute | solution.py:769
  107.6 5.5 %collective-permute-start.10 = (f32[240,128]{1,0:T(8,128)S(1)}, f32[240,128]{1,0:T(8,128)S(1)}, u32[]{:S(2)}, u32[]{:S(2)}) collective-permute-start(f32[240,128]{1,0:T(8,128)S(1)} %get-tuple-element.76), channel_id=1, source_target_pairs={{0,1},{1,0},{2,3},{3,2},{4,5},{5,4},{6,7},{7,6},{8,9},{9,8},{10,11... | collective-permute-start | bytes 368648 | tf_op jit(solution)/shard_map/ppermute | solution.py:745
  108.1 5.1 %collective-permute-start.11 = (f32[240,128]{1,0:T(8,128)S(1)}, f32[240,128]{1,0:T(8,128)S(1)}, u32[]{:S(2)}, u32[]{:S(2)}) collective-permute-start(f32[240,128]{1,0:T(8,128)S(1)} %get-tuple-element.77), channel_id=1, source_target_pairs={{0,2},{1,3},{2,0},{3,1},{4,6},{5,7},{6,4},{7,5},{8,10},{9,11},{10,... | collective-permute-start | bytes 368648 | tf_op jit(solution)/shard_map/ppermute | solution.py:745
  108.1 8.5 %collective-permute-start.12 = (f32[240,128]{1,0:T(8,128)S(1)}, f32[240,128]{1,0:T(8,128)S(1)}, u32[]{:S(2)}, u32[]{:S(2)}) collective-permute-start(f32[240,128]{1,0:T(8,128)S(1)} %get-tuple-element.78), channel_id=1, source_target_pairs={{0,3},{1,2},{2,1},{3,0},{4,7},{5,6},{6,5},{7,4},{8,11},{9,10},{10,... | collective-permute-start | bytes 368648 | tf_op jit(solution)/shard_map/ppermute | solution.py:745
  109.9 7.9 %collective-permute-start.13 = (f32[240,128]{1,0:T(8,128)S(1)}, f32[240,128]{1,0:T(8,128)S(1)}, u32[]{:S(2)}, u32[]{:S(2)}) collective-permute-start(f32[240,128]{1,0:T(8,128)S(1)} %get-tuple-element.79), channel_id=1, source_target_pairs={{0,4},{1,5},{2,6},{3,7},{4,0},{5,1},{6,2},{7,3},{8,12},{9,13},{10,... | collective-permute-start | bytes 368648 | tf_op jit(solution)/shard_map/ppermute | solution.py:745
  110.4 10.6 %collective-permute-start.14 = (f32[240,128]{1,0:T(8,128)S(1)}, f32[240,128]{1,0:T(8,128)S(1)}, u32[]{:S(2)}, u32[]{:S(2)}) collective-permute-start(f32[240,128]{1,0:T(8,128)S(1)} %get-tuple-element.80), channel_id=1, source_target_pairs={{0,5},{1,4},{2,7},{3,6},{4,1},{5,0},{6,3},{7,2},{8,13},{9,12},{10,... | collective-permute-start | bytes 368648 | tf_op jit(solution)/shard_map/ppermute | solution.py:745
  113.1 10.7 %collective-permute-start.15 = (f32[240,128]{1,0:T(8,128)S(1)}, f32[240,128]{1,0:T(8,128)S(1)}, u32[]{:S(2)}, u32[]{:S(2)}) collective-permute-start(f32[240,128]{1,0:T(8,128)S(1)} %get-tuple-element.81), channel_id=1, source_target_pairs={{0,6},{1,7},{2,4},{3,5},{4,2},{5,3},{6,0},{7,1},{8,14},{9,15},{10,... | collective-permute-start | bytes 368648 | tf_op jit(solution)/shard_map/ppermute | solution.py:745
  113.2 13.2 %collective-permute-start.16 = (f32[240,128]{1,0:T(8,128)S(1)}, f32[240,128]{1,0:T(8,128)S(1)}, u32[]{:S(2)}, u32[]{:S(2)}) collective-permute-start(f32[240,128]{1,0:T(8,128)S(1)} %get-tuple-element.82), channel_id=1, source_target_pairs={{0,7},{1,6},{2,5},{3,4},{4,3},{5,2},{6,1},{7,0},{8,15},{9,14},{10,... | collective-permute-start | bytes 368648 | tf_op jit(solution)/shard_map/ppermute | solution.py:745
  (10 other events, 41.7 us)
